TPU v7x, 256 devices: a whole 4x4x8 slice. The times are simulated.
256 devices in a mesh: lon: 16 (over x_hi, y, core), lat: 8 (over z), rep: 2 (over x_lo).
Axes of the slice: x: 4 (x_hi: 2, x_lo: 2; x = x_hi * 2 + x_lo), y: 4, z: 8, core: 2. Of those that a mesh axis runs over, the one named last changes fastest.
Arguments:
- fine_field: bfloat16 [4, 96, 384, 192], P('rep', 'lat', 'lon'), may hold values from -6 to 6
- fine_gain: float32 [192], replicated, may hold values from 0.1 to 1.9
- fine_qkv: bfloat16 [192, 576], replicated, may hold values from -0.4375 to 0.4375
- fine_proj: bfloat16 [192, 192], replicated, may hold values from -0.4375 to 0.4375
- fine_table: float32 [2, 16, 6, 3312], P('rep', 'lat'), may hold values from -6 to 6
- merge_gain: float32 [768], replicated, may hold values from 0.1 to 1.9
- merge_weight: bfloat16 [768, 384], replicated, may hold values from -0.21875 to 0.21875
- coarse_gain: float32 [384], replicated, may hold values from 0.1 to 1.9
- coarse_qkv: bfloat16 [384, 1152], replicated, may hold values from -0.3125 to 0.3125
- coarse_proj: bfloat16 [384, 384], replicated, may hold values from -0.3125 to 0.3125
- coarse_table: float32 [2, 8, 12, 3312], P('rep', 'lat'), may hold values from -6 to 6
- cotangent: bfloat16 [4, 48, 192, 384], P('rep', 'lat', 'lon'), may hold values from -6 to 6
Outputs:
- coarse_out: bfloat16 [4, 48, 192, 384], P('rep', 'lat', 'lon')
- field_grad: bfloat16 [4, 96, 384, 192], P('rep', 'lat', 'lon')
- fine_gain_grad: float32 [192], replicated
- fine_qkv_grad: float32 [192, 576], replicated
- fine_proj_grad: float32 [192, 192], replicated
- fine_table_grad: float32 [2, 16, 6, 3312], P('rep', 'lat')
- merge_gain_grad: float32 [768], replicated
- merge_weight_grad: float32 [768, 384], replicated
- coarse_gain_grad: float32 [384], replicated
- coarse_qkv_grad: float32 [384, 1152], replicated
- coarse_proj_grad: float32 [384, 384], replicated
- coarse_table_grad: float32 [2, 8, 12, 3312], P('rep', 'lat')
All inputs are finite; a program needn't handle non-finite values.
Results may differ from a plain program's by a relative error of at most 0.033.
Values may be sent and summed in bfloat16 or wider, within the bound.
No kernel may reach another device: no remote copies, remote signals or barrier semaphores. Data moves between devices by JAX's collectives and lax.ppermute only.
A program may use at most 192 MiB of HBM per device.

v0:
```python
import jax
import jax.numpy as jnp
from jax import lax
from jax.sharding import PartitionSpec as P

WIN_LEV = 2
WIN_LAT = 6
WIN_LON = 12
WIN_TOK = 144
POS = 3312


EPS = 1e-05


def from_behind(array, axis, by):
    peers = lax.axis_size(axis)
    return lax.ppermute(array, axis, [(i, (i + by) % peers) for i in range(peers)])


def layer_norm(values, gain_vec):
    full = values.astype(jnp.float32)
    centre = jnp.mean(full, axis=-1, keepdims=True)
    shifted = full - centre
    spread = jnp.mean(shifted * shifted, axis=-1, keepdims=True)
    inv_std = lax.rsqrt(spread + EPS)
    normed = shifted * inv_std
    return ((normed * gain_vec).astype(jnp.bfloat16), normed, inv_std)


def layer_norm_back(grad_in, gain_vec, normed, inv_std):
    grad_full = grad_in.astype(jnp.float32)
    scaled = grad_full * gain_vec
    gain_grad = jnp.sum((grad_full * normed).reshape(-1, normed.shape[-1]), axis=0)
    first = jnp.mean(scaled, axis=-1, keepdims=True)
    second = jnp.mean(scaled * normed, axis=-1, keepdims=True)
    return (inv_std * (scaled - first - normed * second), gain_grad)


def to_windows(tensor):
    levels, lat_rows, lon_cols = tensor.shape[:3]
    trailing = tensor.shape[3:]
    shaped = tensor.reshape(
        (levels // WIN_LEV, WIN_LEV, lat_rows // WIN_LAT, WIN_LAT, lon_cols // WIN_LON, WIN_LON)
        + trailing
    )
    axes_order = (0, 2, 4, 1, 3, 5) + tuple(range(6, 6 + len(trailing)))
    return jnp.transpose(shaped, axes_order).reshape(
        (levels // WIN_LEV, lat_rows // WIN_LAT, lon_cols // WIN_LON, WIN_TOK) + trailing
    )


def from_windows(tensor, levels, lat_rows, lon_cols):
    trailing = tensor.shape[4:]
    shaped = tensor.reshape(
        (levels // WIN_LEV, lat_rows // WIN_LAT, lon_cols // WIN_LON, WIN_LEV, WIN_LAT, WIN_LON)
        + trailing
    )
    axes_order = (0, 3, 1, 4, 2, 5) + tuple(range(6, 6 + len(trailing)))
    return jnp.transpose(shaped, axes_order).reshape((levels, lat_rows, lon_cols) + trailing)


def expand_bias(table):
    blocks_lev, blocks_lat, head_count = table.shape[:3]
    parted = table.reshape(
        blocks_lev, blocks_lat, head_count, WIN_LEV, WIN_LEV, WIN_LAT, WIN_LAT, 2 * WIN_LON - 1
    )
    flipped = parted[..., ::-1]
    rows_list = [
        flipped[..., WIN_LON - 1 - query_col : 2 * WIN_LON - 1 - query_col]
        for query_col in range(WIN_LON)
    ]
    spread = jnp.stack(rows_list, axis=-2)
    spread = jnp.transpose(spread, (0, 1, 2, 3, 5, 7, 4, 6, 8))
    return spread.reshape(blocks_lev, blocks_lat, head_count, WIN_TOK, WIN_TOK)


def bias_grad(grad_bias):
    blocks_lev, blocks_lat, head_count = grad_bias.shape[:3]
    parted = grad_bias.reshape(
        blocks_lev, blocks_lat, head_count, WIN_LEV, WIN_LAT, WIN_LON, WIN_LEV, WIN_LAT, WIN_LON
    )
    parted = jnp.transpose(parted, (0, 1, 2, 3, 6, 4, 7, 5, 8))
    pad_none = [(0, 0)] * 7
    folded = None
    for query_col in range(WIN_LON):
        placed = jnp.pad(
            parted[..., query_col, :], pad_none + [(WIN_LON - 1 - query_col, query_col)]
        )
        folded = placed if folded is None else folded + placed
    folded = folded[..., ::-1]
    return folded.reshape(blocks_lev, blocks_lat, head_count, POS)


def window_mask(levels, lat_rows, lev_start, lat_start, lev_total, lat_total):
    lev_pos = lev_start + jnp.arange(levels, dtype=jnp.int32)
    lat_pos = lat_start + jnp.arange(lat_rows, dtype=jnp.int32)
    lev_tag = (lev_pos >= lev_total - WIN_LEV // 2).astype(jnp.int32)
    lat_tag = (lat_pos >= lat_total - WIN_LAT // 2).astype(jnp.int32)
    tags = 2 * lev_tag[:, None] + lat_tag[None, :]
    tags = tags.reshape(levels // WIN_LEV, WIN_LEV, lat_rows // WIN_LAT, WIN_LAT).transpose(
        0, 2, 1, 3
    )
    tags = jnp.broadcast_to(tags[..., None], tags.shape + (WIN_LON,))
    tags = tags.reshape(levels // WIN_LEV, lat_rows // WIN_LAT, WIN_TOK)
    return (tags[:, :, :, None] == tags[:, :, None, :])[:, :, None, None]


def batched(form, left, right):
    return jnp.einsum(form, left, right, preferred_element_type=jnp.float32)


def attention_pieces(rolled, qkv_weight, bias, same, head_count):
    levels, lat_rows, lon_cols, width = rolled.shape
    head_size = width // head_count
    projected = jnp.dot(rolled.reshape(-1, width), qkv_weight, preferred_element_type=jnp.float32)
    windows = to_windows(projected.reshape(levels, lat_rows, lon_cols, 3, head_count, head_size))
    queries = (windows[..., 0, :, :] * head_size ** (-0.5)).astype(jnp.bfloat16)
    keys_win = windows[..., 1, :, :].astype(jnp.bfloat16)
    values_win = windows[..., 2, :, :].astype(jnp.bfloat16)
    scores = batched("abcind,abcjnd->abcnij", queries, keys_win) + bias[:, :, None]
    raised = jnp.where(same, jnp.exp(scores), 0.0)
    probs = raised / jnp.sum(raised, axis=-1, keepdims=True)
    probs_low = probs.astype(jnp.bfloat16)
    mixed = batched("abcnij,abcjnd->abcind", probs_low, values_win).astype(jnp.bfloat16)
    mixed_flat = from_windows(
        mixed.reshape(mixed.shape[:4] + (width,)), levels, lat_rows, lon_cols
    ).reshape(-1, width)
    return (queries, keys_win, values_win, probs, probs_low, mixed_flat)


def block_forward(rolled, qkv_weight, proj_weight, bias, same, head_count):
    pieces = attention_pieces(rolled, qkv_weight, bias, same, head_count)
    output = jnp.dot(pieces[5], proj_weight, preferred_element_type=jnp.float32).astype(
        jnp.bfloat16
    )
    return output.reshape(rolled.shape)


def backward_from(pieces, rolled, grad_out, qkv_weight, proj_weight, head_count):
    queries, keys_win, values_win, probs, probs_low, mixed_flat = pieces
    levels, lat_rows, lon_cols, width = rolled.shape
    head_size = width // head_count
    grad_flat = grad_out.reshape(-1, width)
    proj_grad = lax.dot_general(
        mixed_flat, grad_flat, (((0,), (0,)), ((), ())), preferred_element_type=jnp.float32
    )
    grad_mixed = lax.dot_general(
        grad_flat, proj_weight, (((1,), (1,)), ((), ())), preferred_element_type=jnp.float32
    ).astype(jnp.bfloat16)
    grad_mixed = to_windows(grad_mixed.reshape(levels, lat_rows, lon_cols, head_count, head_size))
    grad_probs = batched("abcind,abcjnd->abcnij", grad_mixed, values_win)
    grad_values = batched("abcnij,abcind->abcjnd", probs_low, grad_mixed)
    grad_scores = probs * (grad_probs - jnp.sum(probs * grad_probs, axis=-1, keepdims=True))
    bias_part = jnp.sum(grad_scores, axis=2)
    scores_low = grad_scores.astype(jnp.bfloat16)
    grad_queries = batched("abcnij,abcjnd->abcind", scores_low, keys_win) * head_size ** (-0.5)
    grad_keys = batched("abcnij,abcind->abcjnd", scores_low, queries)
    stacked = jnp.stack([grad_queries, grad_keys, grad_values], axis=4).astype(jnp.bfloat16)
    stacked_flat = from_windows(stacked, levels, lat_rows, lon_cols).reshape(-1, 3 * width)
    qkv_grad = lax.dot_general(
        rolled.reshape(-1, width),
        stacked_flat,
        (((0,), (0,)), ((), ())),
        preferred_element_type=jnp.float32,
    )
    grad_rolled = lax.dot_general(
        stacked_flat, qkv_weight, (((1,), (1,)), ((), ())), preferred_element_type=jnp.float32
    )
    return (grad_rolled.astype(jnp.bfloat16).reshape(rolled.shape), qkv_grad, proj_grad, bias_part)


def block_backward(rolled, grad_out, qkv_weight, proj_weight, bias, same, head_count):
    pieces = attention_pieces(rolled, qkv_weight, bias, same, head_count)
    return backward_from(pieces, rolled, grad_out, qkv_weight, proj_weight, head_count)


def block_both(rolled, grad_out, qkv_weight, proj_weight, bias, same, head_count):
    pieces = attention_pieces(rolled, qkv_weight, bias, same, head_count)
    output = jnp.dot(pieces[5], proj_weight, preferred_element_type=jnp.float32).astype(
        jnp.bfloat16
    )
    return (output.reshape(rolled.shape),) + backward_from(
        pieces, rolled, grad_out, qkv_weight, proj_weight, head_count
    )


def fine_roll_in(tensor):
    lon_piece = from_behind(tensor[:, :, : WIN_LON // 2], "lon", -1)
    tensor = jnp.concatenate([tensor[:, :, WIN_LON // 2 :], lon_piece], axis=2)
    lat_piece = from_behind(tensor[:, : WIN_LAT // 2], "lat", -1)
    tensor = jnp.concatenate([tensor[:, WIN_LAT // 2 :], lat_piece], axis=1)
    lev_piece = from_behind(tensor[: WIN_LEV // 2], "rep", -1)
    return jnp.concatenate([tensor[WIN_LEV // 2 :], lev_piece], axis=0)


def fine_roll_out(tensor):
    lev_piece = from_behind(tensor[-(WIN_LEV // 2) :], "rep", 1)
    tensor = jnp.concatenate([lev_piece, tensor[: -(WIN_LEV // 2)]], axis=0)
    lat_piece = from_behind(tensor[:, -(WIN_LAT // 2) :], "lat", 1)
    tensor = jnp.concatenate([lat_piece, tensor[:, : -(WIN_LAT // 2)]], axis=1)
    lon_piece = from_behind(tensor[:, :, -(WIN_LON // 2) :], "lon", 1)
    return jnp.concatenate([lon_piece, tensor[:, :, : -(WIN_LON // 2)]], axis=2)


def coarse_roll_in(tensor):
    lon_piece = from_behind(tensor[:, :, : WIN_LON // 2], "lon", -1)
    tensor = jnp.concatenate([tensor[:, :, WIN_LON // 2 :], lon_piece], axis=2)
    lat_piece = from_behind(tensor[:, : WIN_LAT // 2], "lat", -1)
    tensor = jnp.concatenate([tensor[:, WIN_LAT // 2 :], lat_piece], axis=1)
    lev_piece = from_behind(tensor[: WIN_LEV // 2], "rep", -1)
    return jnp.concatenate([tensor[WIN_LEV // 2 :], lev_piece], axis=0)


def coarse_roll_out(tensor):
    lev_piece = from_behind(tensor[-(WIN_LEV // 2) :], "rep", 1)
    tensor = jnp.concatenate([lev_piece, tensor[: -(WIN_LEV // 2)]], axis=0)
    lat_piece = from_behind(tensor[:, -(WIN_LAT // 2) :], "lat", 1)
    tensor = jnp.concatenate([lat_piece, tensor[:, : -(WIN_LAT // 2)]], axis=1)
    lon_piece = from_behind(tensor[:, :, -(WIN_LON // 2) :], "lon", 1)
    return jnp.concatenate([lon_piece, tensor[:, :, : -(WIN_LON // 2)]], axis=2)


def merge_rows(tensor):
    levels, lat_rows, lon_cols, width = tensor.shape
    shaped = tensor.reshape(levels, lat_rows // 2, 2, lon_cols // 2, 2, width).transpose(
        0, 1, 3, 2, 4, 5
    )
    return shaped.reshape(levels, lat_rows // 2, lon_cols // 2, 4 * width)


def split_rows(tensor):
    levels, half_lat, half_lon, wide = tensor.shape
    shaped = tensor.reshape(levels, half_lat, half_lon, 2, 2, wide // 4).transpose(0, 1, 3, 2, 4, 5)
    return shaped.reshape(levels, 2 * half_lat, 2 * half_lon, wide // 4)


def body(
    fine_field,
    fine_gain,
    fine_qkv,
    fine_proj,
    fine_table,
    merge_gain,
    merge_weight,
    coarse_gain,
    coarse_qkv,
    coarse_proj,
    coarse_table,
    cotangent,
):
    levels, lat_rows, lon_cols, width = fine_field.shape
    lev_total = levels * lax.axis_size("rep")
    lat_total = lat_rows * lax.axis_size("lat")
    lon_total = lon_cols * lax.axis_size("lon")
    lev_start = lax.axis_index("rep") * levels
    lat_index = lax.axis_index("lat")
    fine_heads = fine_table.shape[2]
    coarse_heads = coarse_table.shape[2]
    fine_bias = expand_bias(fine_table)
    coarse_bias = expand_bias(coarse_table)
    fine_same = window_mask(levels, lat_rows, lev_start, lat_index * lat_rows, lev_total, lat_total)
    coarse_same = window_mask(
        levels, lat_rows // 2, lev_start, lat_index * (lat_rows // 2), lev_total, lat_total // 2
    )
    normed_fine, hat_fine, inv_fine = layer_norm(fine_field, fine_gain)
    rolled_fine = fine_roll_in(normed_fine)
    fine_branch = fine_roll_out(
        block_forward(rolled_fine, fine_qkv, fine_proj, fine_bias, fine_same, fine_heads)
    )
    fine_out = (fine_field.astype(jnp.float32) + fine_branch.astype(jnp.float32)).astype(
        jnp.bfloat16
    )
    merged = merge_rows(fine_out)
    normed_merge, hat_merge, inv_merge = layer_norm(merged, merge_gain)
    merge_flat = normed_merge.reshape(-1, 4 * width)
    coarse_in = jnp.dot(merge_flat, merge_weight, preferred_element_type=jnp.float32).astype(
        jnp.bfloat16
    )
    coarse_in = coarse_in.reshape(merged.shape[:3] + (merge_weight.shape[1],))
    normed_coarse, hat_coarse, inv_coarse = layer_norm(coarse_in, coarse_gain)
    rolled_coarse = coarse_roll_in(normed_coarse)
    coarse_attended, grad_coarse_rolled, coarse_qkv_part, coarse_proj_part, coarse_bias_part = (
        block_both(
            rolled_coarse,
            coarse_roll_in(cotangent),
            coarse_qkv,
            coarse_proj,
            coarse_bias,
            coarse_same,
            coarse_heads,
        )
    )
    coarse_branch = coarse_roll_out(coarse_attended)
    coarse_out = (coarse_in.astype(jnp.float32) + coarse_branch.astype(jnp.float32)).astype(
        jnp.bfloat16
    )
    grad_coarse_ln, coarse_gain_part = layer_norm_back(
        coarse_roll_out(grad_coarse_rolled), coarse_gain, hat_coarse, inv_coarse
    )
    grad_coarse_in = (cotangent.astype(jnp.float32) + grad_coarse_ln).astype(jnp.bfloat16)
    grad_flat = grad_coarse_in.reshape(-1, grad_coarse_in.shape[-1])
    merge_weight_part = lax.dot_general(
        merge_flat, grad_flat, (((0,), (0,)), ((), ())), preferred_element_type=jnp.float32
    )
    grad_merge_ln = lax.dot_general(
        grad_flat, merge_weight, (((1,), (1,)), ((), ())), preferred_element_type=jnp.float32
    )
    grad_merge_ln = grad_merge_ln.astype(jnp.bfloat16).reshape(merged.shape)
    grad_merged, merge_gain_part = layer_norm_back(grad_merge_ln, merge_gain, hat_merge, inv_merge)
    grad_fine_out = split_rows(grad_merged).astype(jnp.bfloat16)
    coarse_parts = (
        merge_gain_part,
        merge_weight_part,
        coarse_gain_part,
        coarse_qkv_part,
        coarse_proj_part,
    )
    coarse_table_part = bias_grad(coarse_bias_part)
    grad_fine_rolled, fine_qkv_part, fine_proj_part, fine_bias_part = block_backward(
        rolled_fine,
        fine_roll_in(grad_fine_out),
        fine_qkv,
        fine_proj,
        fine_bias,
        fine_same,
        fine_heads,
    )
    grad_fine_ln, fine_gain_part = layer_norm_back(
        fine_roll_out(grad_fine_rolled), fine_gain, hat_fine, inv_fine
    )
    field_grad = (grad_fine_out.astype(jnp.float32) + grad_fine_ln).astype(jnp.bfloat16)
    fine_parts = (fine_gain_part, fine_qkv_part, fine_proj_part)
    fine_table_part = bias_grad(fine_bias_part)
    joined = lax.psum(fine_parts + coarse_parts, ("lon", "lat", "rep"))
    fine_sums = joined[:3]
    coarse_sums = joined[3:]
    fine_table_sum, coarse_table_sum = (
        lax.psum(fine_table_part.astype(jnp.bfloat16), "lon").astype(jnp.float32),
        lax.psum(coarse_table_part.astype(jnp.bfloat16), "lon").astype(jnp.float32),
    )
    fine_scale = (lev_total * lat_total * lon_total) ** (-0.5)
    coarse_scale = (lev_total * (lat_total // 2) * (lon_total // 2)) ** (-0.5)
    fine_table_scale = (lon_total // WIN_LON) ** (-0.5)
    coarse_table_scale = (lon_total // (2 * WIN_LON)) ** (-0.5)
    return (
        coarse_out,
        field_grad,
        fine_sums[0] * fine_scale,
        fine_sums[1] * fine_scale,
        fine_sums[2] * fine_scale,
        fine_table_sum * fine_table_scale,
        coarse_sums[0] * coarse_scale,
        coarse_sums[1] * coarse_scale,
        coarse_sums[2] * coarse_scale,
        coarse_sums[3] * coarse_scale,
        coarse_sums[4] * coarse_scale,
        coarse_table_sum * coarse_table_scale,
    )


def solution(mesh):
    return jax.shard_map(
        body,
        mesh=mesh,
        in_specs=(
            P("rep", "lat", "lon", None),
            P(),
            P(),
            P(),
            P("rep", "lat", None, None),
            P(),
            P(),
            P(),
            P(),
            P(),
            P("rep", "lat", None, None),
            P("rep", "lat", "lon", None),
        ),
        out_specs=(
            P("rep", "lat", "lon", None),
            P("rep", "lat", "lon", None),
            P(),
            P(),
            P(),
            P("rep", "lat", None, None),
            P(),
            P(),
            P(),
            P(),
            P(),
            P("rep", "lat", None, None),
        ),
        check_vma=False,
    )
```

profile of v0, /device:TPU:1, one launch (start us, length us, event | category | flops | bytes accessed | tf_op | source)
XLA Modules:
  0.0 967.1 jit_solution(4476927996232909961)
XLA Ops:
  19.9 8.1 fusion.80
  62.4 8.2 fusion.79
  140.6 5.7 collective-permute-start.1
  148.2 21.2 %copy.329 = f32[1,2,6,2,6,12,2,6,12]{5,4,3,8,7,6,2,1,0:T(8,128)} copy(f32[1,2,6,2,6,12,2,6,12]{8,7,4,6,3,1,2,5,0:T(8,128)} %bitcast.290) | data formatting | bytes 1990656 | tf_op jit(solution)/shard_map/add | solution.py:121
  169.4 9.3 reshape.705
  180.6 6.4 copy.253
  187.0 8.4 copy.254
  218.0 22.5 %copy.331 = f32[1,1,12,2,6,12,2,6,12]{5,4,3,8,7,6,2,1,0:T(8,128)} copy(f32[1,1,12,2,6,12,2,6,12]{8,6,7,4,3,2,5,1,0:T(2,128)} %bitcast.53) | data formatting | bytes 1990656 | tf_op jit(solution)/shard_map/broadcast_in_dim;reshape | solution.py:121
  240.5 10.3 %reshape.707 = f32[12,144,144]{1,2,0:T(8,128)} reshape(f32[1,1,12,2,6,12,2,6,12]{5,4,3,8,7,6,2,1,0:T(8,128)} %copy.331) | data formatting | bytes 1990656 | tf_op jit(solution)/shard_map/broadcast_in_dim;reshape | solution.py:121
  274.7 6.9 collective-permute-start.6
  318.2 10.0 %reshape.709 = f32[1,1,12,2,6,12,2,6,12]{5,4,3,8,7,6,2,1,0:T(8,128)} reshape(f32[12,144,144]{1,2,0:T(8,128)} %subtract_multiply_fusion.1) | data formatting | bytes 1990656 | tf_op jit(solution)/shard_map/reshape | solution.py:80
  335.6 21.0 %copy.311 = f32[1,1,12,2,6,12,2,6,12]{8,6,7,4,3,2,5,1,0:T(2,128)} copy(f32[1,1,12,2,6,12,2,6,12]{5,4,3,8,7,6,2,1,0:T(8,128)} %reshape.709) | data formatting | bytes 1990656 | tf_op jit(solution)/shard_map/reshape | solution.py:80
  356.6 8.0 slice_bitcast_fusion.11
  374.5 13.4 %pad_add_fusion = bf16[1,1,12,2,2,6,6,23]{7,4,6,5,3,2,1,0:T(2,128)(2,1)} fusion(f32[1,1,12,2,2,6,6,12]{7,4,6,5,3,2,1,0:T(2,128)} %get-tuple-element.68, f32[1,1,12,2,2,6,6,12]{7,4,6,5,3,2,1,0:T(2,128)} %get-tuple-element.69, f32[1,1,12,2,2,6,6,12]{7,4,6,5,3,2,1,0:T(2,128)} %get-tuple-element.70, f32[1,1,12,2,2,6,6,12]{7,4,6,5,3,2,1,0:T(2,128)} %get-tuple-element.71, ...), kind=kLoop, calls=%fused_computation.87 | loop fusion | flops 476928 | bytes 1074816 | tf_op jit(solution)/shard_map/add | solution.py:90
  419.2 6.8 collective-permute-start.18
  428.1 5.8 rev.9
  467.6 8.5 reshape.708
  476.1 21.1 %copy.307 = f32[1,2,6,2,6,12,2,6,12]{8,6,7,4,3,2,1,5,0:T(2,128)} copy(f32[1,2,6,2,6,12,2,6,12]{5,4,3,8,7,6,2,1,0:T(8,128)} %reshape.708) | data formatting | bytes 1990656 | tf_op jit(solution)/shard_map/reshape | solution.py:80
  497.1 7.6 slice_bitcast_fusion.23
  504.7 10.3 %pad_add_fusion.1 = bf16[1,2,6,2,2,6,6,23]{7,4,6,5,3,2,1,0:T(2,128)(2,1)S(1)} fusion(f32[1,2,6,2,2,6,6,12]{7,4,6,5,3,2,1,0:T(2,128)S(1)} %get-tuple-element.80, f32[1,2,6,2,2,6,6,12]{7,4,6,5,3,2,1,0:T(2,128)S(1)} %get-tuple-element.81, f32[1,2,6,2,2,6,6,12]{7,4,6,5,3,2,1,0:T(2,128)S(1)} %get-tuple-element.82, ...), kind=kLoop, calls=%fused_computation.89 | loop fusion | flops 476928 | bytes 1074816 | tf_op jit(solution)/shard_map/add | solution.py:90
  525.8 6.3 maximum_bitcast_fusion
  545.0 126.8 %all-reduce.32.cloned.1.call-done = (bf16[1,2,6,3312]{3,1,2,0:T(2,128)(2,1)}, bf16[1,1,12,3312]{3,2,1,0:T(8,128)(2,1)}) async-done(((bf16[1,2,6,3312]{3,1,2,0:T(2,128)(2,1)}, bf16[1,1,12,3312]{3,2,1,0:T(8,128)(2,1)}), (bf16[1,2,6,3312]{3,1,2,0:T(2,128)(2,1)}, bf16[1,1,12,3312]{3,2,1,0:T(8,128)(2,1)})) %all-reduce.32.cloned.1.call-update) | async-done | bytes 158992 | tf_op jit(solution)/shard_map/psum | solution.py:339
  677.8 81.2 %all-reduce.24 = (f32[192]{0:T(256)S(1)}, f32[768]{0:T(1024)S(1)}, f32[384]{0:T(512)S(1)}) all-reduce(f32[192]{0:T(256)S(1)} %get-tuple-element.50, f32[768]{0:T(1024)S(1)} %get-tuple-element.48, f32[384]{0:T(512)S(1)} %copy-done.101), channel_id=1, replica_groups=mesh['lon'=16,'lat'=8,'rep'=2] {'lon','lat','rep'}, use_global_device_ids=true, to_apply=%region_17.18 | all-reduce | flops 1344 | bytes 10752 | tf_op jit(solution)/shard_map/psum | solution.py:335
  761.9 191.7 %all-reduce.30.cloned.1.call-done = (f32[192,576]{1,0:T(8,128)}, f32[192,192]{1,0:T(8,128)}, f32[768,384]{1,0:T(8,128)}, f32[384,1152]{1,0:T(8,128)}, f32[384,384]{1,0:T(8,128)}) async-done(((f32[192,576]{1,0:T(8,128)}, f32[192,192]{1,0:T(8,128)}, f32[768,384]{1,0:T(8,128)}, f32[384,1152]{1,0:T(8,128)}, f32[384,384]{1,0:T(8,128)}), (f32[192,576]{1,0:T(8,128)}, f32[192,192]{1,0:T(8,128)}, ...) | async-done | bytes 4128784 | tf_op jit(solution)/shard_map/psum | solution.py:335
  (479 shorter events, 326.1 us)
Async XLA Ops:
  7.2 664.6 %all-reduce.32.cloned.1.call-start = ((), (), s32[]{:S(2)}) async-start(), calls=%async_computation.1 | async-start | bytes 372736 | tf_op jit(solution)/shard_map/psum | solution.py:339
  11.0 129.6 %collective-permute-start = (bf16[2,12,6,192]{3,2,1,0:T(8,128)(2,1)S(1)}, bf16[2,12,6,192]{3,2,1,0:T(8,128)(2,1)S(1)}, u32[]{:S(2)}, u32[]{:S(2)}) collective-permute-start(bf16[2,12,6,192]{3,2,1,0:T(8,128)(2,1)S(1)} %slice.544), channel_id=1, source_target_pairs={{0,240},{16,0},{32,16},{48,32},{64,48},{80,64},{96,80},{112,96},{1... | collective-permute-start | bytes 165896 | tf_op jit(solution)/shard_map/ppermute | solution.py:18
  15.8 236.6 %collective-permute-start.12 = (bf16[2,6,6,384]{3,0,2,1:T(2,128)(2,1)}, bf16[2,6,6,384]{3,0,2,1:T(2,128)(2,1)}, u32[]{:S(2)}, u32[]{:S(2)}) collective-permute-start(bf16[2,6,6,384]{3,0,2,1:T(2,128)(2,1)} %get-tuple-element.144), channel_id=1, source_target_pairs={{0,240},{16,0},{32,16},{48,32},{64,48},{80,64},{96,80},{112,96},{1... | collective-permute-start | bytes 165896 | tf_op jit(solution)/shard_map/ppermute | solution.py:18
  140.6 7.1 collective-permute-start.1
  147.7 31.3 %collective-permute-start.2 = (bf16[1,12,24,192]{3,2,1,0:T(8,128)(2,1)S(1)}, bf16[1,12,24,192]{3,2,1,0:T(8,128)(2,1)S(1)}, u32[]{:S(2)}, u32[]{:S(2)}) collective-permute-start(bf16[1,12,24,192]{3,2,1,0:T(8,128)(2,1)S(1)} %get-tuple-element.122), channel_id=1, source_target_pairs={{0,1},{1,0},{2,3},{3,2},{4,5},{5,4},{6,7},{7,6},{8,9},{9,8},{10,11... | collective-permute-start | bytes 331784 | tf_op jit(solution)/shard_map/ppermute | solution.py:18
  214.8 36.8 %collective-permute-start.3 = (bf16[1,12,24,192]{3,2,1,0:T(8,128)(2,1)}, bf16[1,12,24,192]{3,2,1,0:T(8,128)(2,1)}, u32[]{:S(2)}, u32[]{:S(2)}) collective-permute-start(bf16[1,12,24,192]{3,2,1,0:T(8,128)(2,1)} %bitcast.317), channel_id=1, source_target_pairs={{0,1},{1,0},{2,3},{3,2},{4,5},{5,4},{6,7},{7,6},{8,9},{9,8},{10,11... | collective-permute-start | bytes 331784 | tf_op jit(solution)/shard_map/ppermute | solution.py:18
  252.4 4.8 collective-permute-start.4
  253.4 4.7 collective-permute-start.13
  258.0 4.1 collective-permute-start.5
  259.0 22.6 %collective-permute-start.14 = (bf16[1,6,12,384]{3,0,2,1:T(2,128)(2,1)}, bf16[1,6,12,384]{3,0,2,1:T(2,128)(2,1)}, u32[]{:S(2)}, u32[]{:S(2)}) collective-permute-start(bf16[1,6,12,384]{3,0,2,1:T(2,128)(2,1)} %get-tuple-element.140), channel_id=1, source_target_pairs={{0,1},{1,0},{2,3},{3,2},{4,5},{5,4},{6,7},{7,6},{8,9},{9,8},{10,11... | collective-permute-start | bytes 165896 | tf_op jit(solution)/shard_map/ppermute | solution.py:18
  274.7 10.3 %collective-permute-start.6 = (bf16[2,6,6,384]{3,2,1,0:T(8,128)(2,1)}, bf16[2,6,6,384]{3,2,1,0:T(8,128)(2,1)}, u32[]{:S(2)}, u32[]{:S(2)}) collective-permute-start(bf16[2,6,6,384]{3,2,1,0:T(8,128)(2,1)} %get-tuple-element.136), channel_id=1, source_target_pairs={{0,240},{16,0},{32,16},{48,32},{64,48},{80,64},{96,80},{112,96},{1... | collective-permute-start | bytes 165896 | tf_op jit(solution)/shard_map/ppermute | solution.py:18
  286.6 9.6 collective-permute-start.7
  367.0 25.1 %collective-permute-start.9 = (bf16[1,6,12,384]{3,2,1,0:T(8,128)(2,1)}, bf16[1,6,12,384]{3,2,1,0:T(8,128)(2,1)}, u32[]{:S(2)}, u32[]{:S(2)}) collective-permute-start(bf16[1,6,12,384]{3,2,1,0:T(8,128)(2,1)} %slice.484), channel_id=1, source_target_pairs={{0,1},{1,0},{2,3},{3,2},{4,5},{5,4},{6,7},{7,6},{8,9},{9,8},{10,11... | collective-permute-start | bytes 165896 | tf_op jit(solution)/shard_map/ppermute | solution.py:18
  372.9 18.2 %collective-permute-start.15 = (bf16[1,6,12,384]{3,2,1,0:T(8,128)(2,1)}, bf16[1,6,12,384]{3,2,1,0:T(8,128)(2,1)}, u32[]{:S(2)}, u32[]{:S(2)}) collective-permute-start(bf16[1,6,12,384]{3,2,1,0:T(8,128)(2,1)} %slice.498), channel_id=1, source_target_pairs={{0,1},{1,0},{2,3},{3,2},{4,5},{5,4},{6,7},{7,6},{8,9},{9,8},{10,11... | collective-permute-start | bytes 165896 | tf_op jit(solution)/shard_map/ppermute | solution.py:18
  392.0 4.5 collective-permute-start.16
  394.0 5.4 collective-permute-start.10
  396.6 4.2 collective-permute-start.17
  400.0 6.5 collective-permute-start.11
  419.2 17.1 %collective-permute-start.18 = (bf16[2,12,6,192]{3,2,1,0:T(8,128)(2,1)}, bf16[2,12,6,192]{3,2,1,0:T(8,128)(2,1)}, u32[]{:S(2)}, u32[]{:S(2)}) collective-permute-start(bf16[2,12,6,192]{3,2,1,0:T(8,128)(2,1)} %slice.604), channel_id=1, source_target_pairs={{0,240},{16,0},{32,16},{48,32},{64,48},{80,64},{96,80},{112,96},{1... | collective-permute-start | bytes 165896 | tf_op jit(solution)/shard_map/ppermute | solution.py:18
  441.2 4.7 collective-permute-start.20
  540.8 4.1 collective-permute-start.21
  541.0 412.6 %all-reduce.30.cloned.1.call-start = ((), (), s32[]{:S(2)}) async-start(), calls=%async_computation | async-start | bytes 8454144 | tf_op jit(solution)/shard_map/psum | solution.py:335
  544.9 127.8 %collective-permute-start.22 = (bf16[2,3,24,192]{3,2,1,0:T(8,128)(2,1)S(1)}, bf16[2,3,24,192]{3,2,1,0:T(8,128)(2,1)S(1)}, u32[]{:S(2)}, u32[]{:S(2)}) collective-permute-start(bf16[2,3,24,192]{3,2,1,0:T(8,128)(2,1)S(1)} %pad_maximum_fusion.15), channel_id=1, source_target_pairs={{0,2},{2,4},{4,6},{6,8},{8,10},{10,12},{12,14},{14,0},{1,3},{3,5},... | collective-permute-start | bytes 165896 | tf_op jit(solution)/shard_map/ppermute | solution.py:18
  672.8 4.5 collective-permute-start.23
  (104 other events, 1452.3 us)
Sparse Core Ops, SparseCore 0:
  541.1 130.6 all-reduce.31
  680.4 273.1 all-reduce.29
where the time goes:
time: 982 us; the launch traced here: 967 us
  local copies, waits for them, and re-layouts  364 us (37%)
  waiting for transfers between devices  339 us (35%)
  other arithmetic  81.3 us (8%)
  blocking collectives  81.2 us (8%)
  matrix products  48.7 us (5%)
  starting transfers between devices  37.6 us (4%)
  between operations  15.6 us (2%)
    psum x1, waiting for transfers between devices, body(): joined = lax.psum(fine_parts + coarse_parts, ('lon', 'lat', 'rep'))  192 us
    psum x1, waiting for transfers between devices, body(): lax.psum(fine_table_part.astype(jnp.bfloat16), 'lon').astype(jnp.float32)  127 us
    psum x1, blocking collectives, body(): joined = lax.psum(fine_parts + coarse_parts, ('lon', 'lat', 'rep'))  81.2 us
    slice x26, local copies, waits for them, and re-layouts, expand_bias(): flipped[..., WIN_LON - 1 - query_col:2 * WIN_LON - 1 - query_col]  81.2 us
    reshape x4, local copies, waits for them, and re-layouts, bias_grad(): grad_bias.reshape(blocks_lev, blocks_lat, head_count, WIN_LEV, WIN_LAT, W...  60.6 us
    unnamed x232, local copies, waits for them, and re-layouts  45.3 us
    ppermute x24, starting transfers between devices, from_behind(): lax.ppermute(array, axis, [(i, (i + by) % peers) for i in range(peers)])  37.5 us
    another operation x2, local copies, waits for them, and re-layouts, attention_pieces(): bias[:, :, None]  32.8 us
  transfers between devices with their start and end apart: 26, of which 13 were waited for; matrix products, arithmetic and copies ran while one was open for 31% of the time, Pallas kernels for 0%

commit v1 on v0

v1 whole, which is shorter than its diff:
```python
import numpy as np
import jax
import jax.numpy as jnp
from jax import lax
from jax.experimental import pallas as pl
from jax.experimental.pallas import tpu as pltpu
from jax.sharding import PartitionSpec as P

F32, BF = jnp.float32, jnp.bfloat16
EPS = 1e-05
TOK, HALF, LANES = 144, 72, 256
POS, DIAG = 3312, 23
RUN = 6 * DIAG
HEAD = 32
NEG = -1e30
COARSE_ROWS, FINE_ROWS = 2560, 512
VMEM_LIMIT = 56 * 1024 * 1024


def dot(a, b, ca, cb):
    return lax.dot_general(a, b, (((ca,), (cb,)), ((), ())), preferred_element_type=F32)


def mm(a, b):
    return dot(a, b, 1, 0)


def mm_t(a, b):
    return dot(a, b, 1, 1)


def t_mm(a, b):
    return dot(a, b, 0, 0)


def low(x):
    return x.astype(BF)


def split3(x):
    hi = low(x)
    rest = x - hi.astype(F32)
    mid = low(rest)
    return hi, mid, low(rest - mid.astype(F32))


def iota(shape, dim):
    return lax.broadcasted_iota(jnp.int32, shape, dim)


def div_const(x, n):
    return lax.shift_right_logical(x * (65536 // n + 1), 16)


def one_hot(target, count):
    return jnp.where(iota((target.shape[0], count), 1) == target, 1.0, 0.0).astype(BF)


def window_index(rows):
    r = iota((rows, 1), 0)
    z = div_const(r, 72)
    r = r - z * 72
    h = div_const(r, 12)
    return z, h, r - h * 12


def pad_keys(x):
    gap = jnp.zeros((128 - HALF, x.shape[1]), F32)
    return low(jnp.concatenate([x[:HALF], gap, x[HALF:], gap], axis=0))


def unpad_keys(x):
    return jnp.concatenate([x[:HALF], x[128 : 128 + HALF]], axis=0)


def norm(x):
    width = sum(p.shape[1] for p in x)
    mean = sum(jnp.sum(p, axis=1, keepdims=True) for p in x) * (1.0 / width)
    shifted = [p - mean for p in x]
    var = sum(jnp.sum(p * p, axis=1, keepdims=True) for p in shifted) * (1.0 / width)
    inv = lax.rsqrt(var + EPS)
    return [p * inv for p in shifted], inv


def norm_back(grad, gain, hat, inv):
    width = sum(p.shape[1] for p in grad)
    scaled = [g * a for g, a in zip(grad, gain)]
    first = sum(jnp.sum(s, axis=1, keepdims=True) for s in scaled) * (1.0 / width)
    second = sum(jnp.sum(s * n, axis=1, keepdims=True) for s, n in zip(scaled, hat)) * (1.0 / width)
    gains = [jnp.sum(g * n, axis=0, keepdims=True) for g, n in zip(grad, hat)]
    return [inv * (s - first - n * second) for s, n in zip(scaled, hat)], gains


def load_bias(ref, kind, rows):
    return jnp.concatenate([ref[kind, 0, rows], ref[kind, 1, rows]], axis=1)


def head_mask(width, slot):
    lane = iota((1, width), 1)
    return (lane >= slot * HEAD) & (lane < (slot + 1) * HEAD)


def probabilities(q_h, keys, bias):
    e = jnp.exp(mm_t(q_h, keys) + bias)
    return e * (1.0 / jnp.sum(e, axis=1, keepdims=True))


def tile_forward(q, keys, values, bias_of, slots):
    mixed = None
    for slot in range(slots):
        mask = head_mask(q.shape[1], slot)
        p = probabilities(low(jnp.where(mask, q, 0.0)), keys, bias_of(slot))
        o = mm(low(p), values)
        mixed = o if mixed is None else jnp.where(mask, o, mixed)
    return mixed


def tile_both(q, keys, values, gmix, bias_of, bias_grad_to, slots):
    q_low, gmix_low = low(q), low(gmix)
    mixed = gq = gk = gv = None
    for slot in range(slots):
        mask = head_mask(q.shape[1], slot)
        p = probabilities(low(jnp.where(mask, q, 0.0)), keys, bias_of(slot))
        p_low = low(p)
        o = mm(p_low, values)
        gp = mm_t(low(jnp.where(mask, gmix, 0.0)), values)
        gs = p * (gp - jnp.sum(p * gp, axis=1, keepdims=True))
        bias_grad_to(slot, gs)
        gs_low = low(gs)
        dq = mm(gs_low, keys)
        dk = t_mm(gs_low, q_low)
        dv = t_mm(p_low, gmix_low)
        if slot == 0:
            mixed, gq, gk, gv = o, dq, dk, dv
        else:
            mixed = jnp.where(mask, o, mixed)
            gq = jnp.where(mask, dq, gq)
            gk = jnp.where(mask, dk, gk)
            gv = jnp.where(mask, dv, gv)
    return mixed, gq, gk, gv


def diagonal_select(wq):
    lane = iota((1, 128), 1)
    hk = div_const(lane, 12)
    wk = lane - hk * 12
    target = jnp.where(lane < HALF, hk * DIAG + wq - wk + 11, -1)
    return jnp.where(iota((RUN, 128), 0) == target, 1.0, 0.0).astype(BF)


def table_groups():
    return [(g, g // 12, (g // 6) % 2, g % 6) for g in range(24)]


def expand_tables(flags_ref, types, heads, pad, table_of, out_ref, u_ref, lat_flag):
    lane = iota((1, 128), 1)
    lev = flags_ref[0]
    for t in range(types):
        u_ref[...] = jnp.zeros(u_ref.shape, F32)
        table = table_of(t)
        for g, zq, zk, hq in table_groups():
            u_ref[g * pad : g * pad + heads] = table[:, g * RUN : (g + 1) * RUN]
        parts = split3(u_ref[...])
        lat = lat_flag(t)
        lev_term = jnp.where(lev > 0, NEG, 0.0)
        upper = jnp.where((lane >= 36) & (lat > 0), NEG, 0.0)
        lower = jnp.where((lane < 36) & (lat > 0), NEG, 0.0)
        outside = jnp.where(lane >= HALF, NEG, 0.0)
        for wq in range(12):
            sel = diagonal_select(wq)
            x = sum(mm(part, sel) for part in parts)
            for g, zq, zk, hq in table_groups():
                extra = outside + (upper if hq < 3 else lower)
                if zq != zk:
                    extra = extra + lev_term
                rows = x[g * pad : g * pad + heads] + extra
                out_ref[t, zk, pl.ds(zq * 72 + hq * 12 + wq, heads, stride=TOK)] = rows


def fold_tables(types, heads, pad, grad_ref, out_to, y_ref):
    y_ref[...] = jnp.zeros(y_ref.shape, F32)
    for t in range(types):
        acc = None
        for wq in range(12):
            sel = diagonal_select(wq)
            for g, zq, zk, hq in table_groups():
                y_ref[g * pad : g * pad + heads] = grad_ref[
                    t, zk, pl.ds(zq * 72 + hq * 12 + wq, heads, stride=TOK)
                ]
            y = y_ref[...]
            hi = low(y)
            part = mm_t(hi, sel) + mm_t(low(y - hi.astype(F32)), sel)
            acc = part if acc is None else acc + part
        out_to(t, acc)


def bias_kernel(flags_ref, fine_ref, coarse_ref, fine_out, coarse_out, uf_ref, uc_ref):
    last = flags_ref[1]
    expand_tables(
        flags_ref, 2, 6, 8, lambda t: fine_ref[t], fine_out, uf_ref,
        lambda t: last if t == 1 else 0,
    )
    expand_tables(
        flags_ref, 1, 12, 16, lambda t: coarse_ref[t], coarse_out, uc_ref, lambda t: last
    )


def next_bias_kernel(flags_ref, fine_ref, fine_out, uf_ref):
    expand_tables(flags_ref, 1, 6, 8, lambda t: fine_ref[t], fine_out, uf_ref, lambda t: 0)


def pack_kernel(field_ref, cot_ref, *outs):
    for s in range(2):
        for t in range(2):
            out = outs[2 * s + t]
            lev = 1 - s
            row, crow = (3, 3) if t == 0 else (0, 0)
            for h in range(9):
                out[h * 24 : h * 24 + 24] = field_ref[lev, row + h]
            for h in range(3):
                part = cot_ref[lev, crow + h].astype(F32)
                both = jnp.concatenate([part[:, :192], part[:, 192:]], axis=0)
                out[216 + h * 24 : 240 + h * 24] = low(both)


def fine_weights(qkv_ref):
    w = qkv_ref[...]
    return w[:, :192], w[:, 192:384], w[:, 384:]


FINE_TILES = ((0, 128, 4), (128, 64, 2))


def main_kernel(
    b000, b001, b010, b011, b100, b101, b110, b111,
    bias_ref, next_bias_ref, cbias_ref,
    fgain_ref, fqkv_ref, fproj_ref, mgain_ref, mw_ref, cgain_ref, cqkv_ref, cproj_ref,
    x_out, cout_out, gfo_out, latp_out, lonp_out, pack_out, ctab_out,
    x_ref, fo_ref, q_ref, k_ref, v_ref, gm_ref, mix_ref, gq_ref, gk_ref, gv_ref, gb_ref, y_ref,
):
    bufs = ((b000, b001), (b010, b011)), ((b100, b101), (b110, b111))
    _, hh, ww = window_index(HALF)
    for wr in range(3):
        for wc in range(3):
            acc = [None, None]
            for t in ((0,), (0, 1), (1,))[wr]:
                for u in ((0,), (0, 1), (1,))[wc]:
                    lat = 6 * wr + hh - 9 * t
                    lon = 12 * wc + ww - 18 * u
                    good = (lat >= 0) & (lat < 9) & (lon >= 0) & (lon < 18)
                    hot = one_hot(jnp.where(good, lat * 24 + lon + (6 if u == 0 else 0), -1), 288)
                    for z in range(2):
                        part = mm(hot, bufs[z][t][u][...])
                        acc[z] = part if acc[z] is None else acc[z] + part
            for z in range(2):
                x_ref[3 * wr + wc, z * HALF : (z + 1) * HALF] = acc[z]
    for wr in range(2):
        for wc in range(2):
            x_out[2 * wr + wc] = low(x_ref[3 * wr + wc])
    wq, wk, wv = fine_weights(fqkv_ref)

    def fine_window(w, table_ref, wr):
        x = x_ref[w]
        (hat,), _ = norm([x])
        xn = low(hat * fgain_ref[...])
        q = low(mm(xn, wq) * HEAD**-0.5).astype(F32)
        keys = pad_keys(mm(xn, wk))
        values = pad_keys(mm(xn, wv))
        out = None
        for start, width, slots in FINE_TILES:
            lanes = slice(start, start + width)

            def bias_of(slot):
                h = (start // HEAD + slot) * TOK
                return load_bias(table_ref, wr, slice(h, h + TOK))

            mixed = tile_forward(q[:, lanes], keys[:, lanes], values[:, lanes], bias_of, slots)
            part = mm(low(mixed), fproj_ref[lanes])
            out = part if out is None else out + part
        fo_ref[pl.ds(pl.multiple_of(w * TOK, 16), TOK)] = low(x + low(out).astype(F32))

    @pl.loop(0, 6)
    def _(w):
        fine_window(w, bias_ref, div_const(w, 3))

    @pl.loop(6, 9)
    def _(w):
        fine_window(w, next_bias_ref, 0)

    z, i, j = window_index(TOK)
    merged = []
    for p in range(4):
        lat = 3 + 2 * i + p // 2
        lon = 6 + 2 * j + p % 2
        wr, wc = div_const(lat, 6), div_const(lon, 12)
        target = (3 * wr + wc) * TOK + z * HALF + (lat - 6 * wr) * 12 + lon - 12 * wc
        merged.append(mm(one_hot(target, 9 * TOK), fo_ref[...]))
    mhat, minv = norm(merged)
    mgain = [mgain_ref[p : p + 1] for p in range(4)]
    mnorm = [low(h * g) for h, g in zip(mhat, mgain)]
    mweight = [mw_ref[192 * p : 192 * p + 192] for p in range(4)]
    cin = low(sum(mm(n, w) for n, w in zip(mnorm, mweight))).astype(F32)
    (chat,), cinv = norm([cin])
    cgain = cgain_ref[...]
    xc = low(chat * cgain)
    _, ci, cj = window_index(HALF)
    cot_rows = []
    for s in range(2):
        acc = [None, None]
        for t in range(2):
            for u in range(2):
                lat, lon = ci - 3 * t, cj - 6 * u
                good = (lat >= 0) & (lat < 3) & (lon >= 0) & (lon < 6)
                col = 216 + lat * 24 + lon + (6 if u == 0 else 0)
                for half in range(2):
                    hot = one_hot(jnp.where(good, col + half * 12, -1), 288)
                    part = mm(hot, bufs[s][t][u][...])
                    acc[half] = part if acc[half] is None else acc[half] + part
        cot_rows.append(jnp.concatenate(acc, axis=1))
    cot = jnp.concatenate(cot_rows, axis=0)
    gy = low(cot)
    gmix = low(mm_t(gy, cproj_ref[...])).astype(F32)
    for tile in range(3):
        lanes = slice(128 * tile, 128 * tile + 128)
        q_ref[tile] = low(mm(xc, cqkv_ref[:, lanes]) * HEAD**-0.5).astype(F32)
        k_ref[tile] = pad_keys(mm(xc, cqkv_ref[:, 384 + 128 * tile : 512 + 128 * tile]))
        v_ref[tile] = pad_keys(mm(xc, cqkv_ref[:, 768 + 128 * tile : 896 + 128 * tile]))
        gm_ref[tile] = gmix[:, lanes]

    def coarse_tile(tile, carry):
        def bias_of(slot):
            return load_bias(cbias_ref, 0, pl.ds(pl.multiple_of((4 * tile + slot) * TOK, 8), TOK))

        def bias_grad_to(slot, gs):
            rows = pl.ds(pl.multiple_of((4 * tile + slot) * TOK, 8), TOK)
            gb_ref[0, 0, rows] = gs[:, :128]
            gb_ref[0, 1, rows] = gs[:, 128:]

        mixed, gq, gk, gv = tile_both(
            q_ref[tile], k_ref[tile], v_ref[tile], gm_ref[tile], bias_of, bias_grad_to, 4
        )
        mix_ref[tile] = low(mixed)
        gq_ref[tile] = low(gq * HEAD**-0.5)
        gk_ref[tile] = low(unpad_keys(gk))
        gv_ref[tile] = low(unpad_keys(gv))
        return carry

    lax.fori_loop(0, 3, coarse_tile, 0)
    out = None
    grolled = None
    for tile in range(3):
        lanes = slice(128 * tile, 128 * tile + 128)
        part = mm(mix_ref[tile], cproj_ref[lanes])
        out = part if out is None else out + part
        pack_out[1920 + 128 * tile : 2048 + 128 * tile] = low(t_mm(mix_ref[tile], gy))
        for m, ref in enumerate((gq_ref, gk_ref, gv_ref)):
            g = ref[tile]
            pack_out[768 + 384 * m : 1152 + 384 * m, lanes] = low(t_mm(xc, g))
            wcols = slice(384 * m + 128 * tile, 384 * m + 128 * tile + 128)
            part = mm_t(g, cqkv_ref[:, wcols])
            grolled = part if grolled is None else grolled + part
    cout_out[...] = low(cin + low(out).astype(F32))
    (gci,), (cgain_grad,) = norm_back([low(grolled).astype(F32)], [cgain], [chat], cinv)
    gci = low(cot + gci)
    gml = []
    for p in range(4):
        pack_out[192 * p : 192 * p + 192] = low(t_mm(mnorm[p], gci))
        gml.append(low(mm_t(gci, mweight[p])).astype(F32))
    gmerged, mgain_grad = norm_back(gml, mgain, mhat, minv)
    blank = jnp.zeros((1, 192), F32)
    rows = [jnp.concatenate([g, blank], axis=1) for g in mgain_grad] + [cgain_grad]
    rows.append(jnp.zeros((11, 384), F32))
    pack_out[2304:2320] = low(jnp.concatenate(rows, axis=0))
    pack_out[2320:] = jnp.zeros((COARSE_ROWS - 2320, 384), BF)
    r40 = iota((40, 1), 0)
    zi = div_const(r40, 3)
    lon_hot = one_hot(jnp.where(r40 < 36, zi * 12 + 9 + r40 - 3 * zi, -1), TOK)
    for p in range(4):
        g = low(gmerged[p])
        gfo_out[p] = g
        gf = g.astype(F32)
        latp_out[48 * p : 48 * p + 48] = low(jnp.concatenate([gf[48:72], gf[120:144]], axis=0))
        lonp_out[40 * p : 40 * p + 40] = low(mm(lon_hot, g))

    def ctab(t, acc):
        for g in range(24):
            ctab_out[:, g * RUN : (g + 1) * RUN] = low(acc[g * 16 : g * 16 + 12])

    fold_tables(1, 12, 16, gb_ref, ctab, y_ref)


def back_kernel(
    x_in, gfo_ref, latp_ref, lonp_ref, corner_ref, bias_ref, fgain_ref, fqkv_ref, fproj_ref,
    fg_out, pack_out, ftab_out,
    gy_ref, gqkv_ref, gproj_ref, gain_ref, gb_ref, y_ref,
):
    z, h, w = window_index(TOK)
    for wr in range(2):
        for wc in range(2):
            lat, lon = 6 * wr + h, 12 * wc + w
            own = (lat >= 3) & (lon >= 6)

            def parity(a, b):
                return 2 * (a & 1) + (b & 1), lax.shift_right_logical(a, 1), lax.shift_right_logical(b, 1)

            p, i, j = parity(jnp.maximum(lat - 3, 0), jnp.maximum(lon - 6, 0))
            hot = one_hot(jnp.where(own, p * TOK + z * HALF + i * 12 + j, -1), 4 * TOK)
            acc = mm(hot, gfo_ref[...])
            if wr == 0:
                p, i, j = parity(lat + 9, jnp.maximum(lon - 6, 0))
                good = (lat < 3) & (lon >= 6)
                target = p * 48 + z * 24 + (i - 4) * 12 + j
                acc += mm(one_hot(jnp.where(good, target, -1), 192), latp_ref[...])
            if wc == 0:
                p, i, j = parity(jnp.maximum(lat - 3, 0), lon + 18)
                good = (lat >= 3) & (lon < 6)
                target = p * 40 + z * 18 + i * 3 + j - 9
                acc += mm(one_hot(jnp.where(good, target, -1), 160), lonp_ref[...])
            if wr == 0 and wc == 0:
                p, i, j = parity(lat + 9, lon + 18)
                good = (lat < 3) & (lon < 6)
                target = p * 40 + z * 18 + i * 3 + j - 9
                acc += mm(one_hot(jnp.where(good, target, -1), 160), corner_ref[...])
            gy_ref[2 * wr + wc] = acc
    gqkv_ref[...] = jnp.zeros(gqkv_ref.shape, F32)
    gproj_ref[...] = jnp.zeros(gproj_ref.shape, F32)
    gain_ref[...] = jnp.zeros(gain_ref.shape, F32)
    gb_ref[...] = jnp.zeros(gb_ref.shape, F32)
    weights = fine_weights(fqkv_ref)
    gain = fgain_ref[...]

    def fine_window(n, carry):
        x = x_in[n].astype(F32)
        gy32 = gy_ref[n]
        gy = low(gy32)
        (hat,), inv = norm([x])
        xn = low(hat * gain)
        q = low(mm(xn, weights[0]) * HEAD**-0.5).astype(F32)
        keys = pad_keys(mm(xn, weights[1]))
        values = pad_keys(mm(xn, weights[2]))
        gmix = low(mm_t(gy, fproj_ref[...])).astype(F32)
        wr = lax.shift_right_logical(n, 1)
        grolled = None
        for start, width, slots in FINE_TILES:
            lanes = slice(start, start + width)

            def rows_of(slot):
                h = (start // HEAD + slot) * TOK
                return slice(h, h + TOK)

            def bias_grad_to(slot, gs):
                gb_ref[wr, 0, rows_of(slot)] += gs[:, :128]
                gb_ref[wr, 1, rows_of(slot)] += gs[:, 128:]

            mixed, gq, gk, gv = tile_both(
                q[:, lanes], keys[:, lanes], values[:, lanes], gmix[:, lanes],
                lambda slot: load_bias(bias_ref, wr, rows_of(slot)), bias_grad_to, slots,
            )
            gproj_ref[lanes] += t_mm(low(mixed), gy)
            grads = low(gq * HEAD**-0.5), low(unpad_keys(gk)), low(unpad_keys(gv))
            for m, g in enumerate(grads):
                gqkv_ref[m, :, lanes] += t_mm(xn, g)
                part = mm_t(g, weights[m][:, lanes])
                grolled = part if grolled is None else grolled + part
        (gx,), (ggain,) = norm_back([low(grolled).astype(F32)], [gain], [hat], inv)
        gain_ref[...] += ggain
        fg = low(gy32 + gx)
        fg_out[0, pl.ds(pl.multiple_of(n * HALF, 8), HALF)] = fg[:HALF]
        fg_out[1, pl.ds(pl.multiple_of(n * HALF, 8), HALF)] = fg[HALF:]
        return carry

    lax.fori_loop(0, 4, fine_window, 0)
    pack_out[:192] = low(jnp.concatenate([gqkv_ref[0], gqkv_ref[1]], axis=1))
    pack_out[192:384] = low(jnp.concatenate([gqkv_ref[2], gproj_ref[...]], axis=1))
    row = jnp.concatenate([gain_ref[...], jnp.zeros((1, 192), F32)], axis=1)
    pack_out[384:400] = low(jnp.concatenate([row, jnp.zeros((15, 384), F32)], axis=0))
    pack_out[400:] = jnp.zeros((FINE_ROWS - 400, 384), BF)

    def ftab(t, acc):
        for g in range(24):
            ftab_out[t, :, g * RUN : (g + 1) * RUN] = low(acc[g * 8 : g * 8 + 6])

    fold_tables(2, 6, 8, gb_ref, ftab, y_ref)


def place_kernel(*refs):
    fine, coarse, (field_out, coarse_out) = refs[:8], refs[8:16], refs[16:]
    for lev in range(2):
        s = 1 - lev
        for t in range(2):
            rows = 72 if t == 1 else 216
            r = iota((rows, 1), 0)
            row = div_const(r, 24)
            col = r - row * 24
            lat = row + (9 if t == 1 else 0)
            acc = None
            for u in range(2):
                lon = jnp.where(col >= 6, col - 6, col + 18)
                mine = (col < 6) if u == 1 else (col >= 6)
                wr, wc = div_const(lat, 6), div_const(lon, 12)
                inside = (lat - 6 * wr) * 12 + lon - 12 * wc
                wrow = wr - 1 if t == 1 else wr
                wcol = wc - 1 if u == 1 else wc
                cols = 1 if u == 1 else 2
                target = (wrow * cols + wcol) * HALF + inside
                ref = fine[4 * s + 2 * t + u]
                count = ref.shape[0]
                part = mm(one_hot(jnp.where(mine, target, -1), count), ref[...])
                acc = part if acc is None else acc + part
            for h in range(rows // 24):
                field_out[lev, h + (0 if t == 1 else 3)] = low(acc[24 * h : 24 * h + 24])
        acc = None
        r = iota((HALF, 1), 0)
        row = div_const(r, 12)
        col = r - row * 12
        for t in range(2):
            for u in range(2):
                i = row + 3 if t == 1 else row - 3
                j = col + 6 if u == 1 else col - 6
                good = ((row < 3) if t == 1 else (row >= 3)) & ((col < 6) if u == 1 else (col >= 6))
                ref = coarse[4 * s + 2 * t + u]
                part = mm(one_hot(jnp.where(good, i * 12 + j, -1), HALF), ref[...])
                acc = part if acc is None else acc + part
        for h in range(6):
            coarse_out[lev, h] = low(acc[12 * h : 12 * h + 12])


def coarse_unpack_kernel(scale, sums_ref, tab_ref, table_scale, *outs):
    mgain_out, mw_out, cgain_out, cqkv_out, cproj_out, ctab_out = outs
    mw_out[...] = sums_ref[:768].astype(F32) * scale
    for m in range(3):
        cqkv_out[:, 384 * m : 384 * m + 384] = sums_ref[768 + 384 * m : 1152 + 384 * m].astype(F32) * scale
    cproj_out[...] = sums_ref[1920:2304].astype(F32) * scale
    gains = sums_ref[2304:2320].astype(F32) * scale
    mgain_out[...] = jnp.concatenate([gains[p : p + 1, :192] for p in range(4)], axis=1)
    cgain_out[...] = gains[4:5]
    ctab_out[0] = tab_ref[...].astype(F32) * table_scale


def fine_unpack_kernel(scale, sums_ref, tab_ref, table_scale, *outs):
    gain_out, qkv_out, proj_out, ftab_out = outs
    first = sums_ref[:192].astype(F32) * scale
    second = sums_ref[192:384].astype(F32) * scale
    qkv_out[:, :384] = first
    qkv_out[:, 384:] = second[:, :192]
    proj_out[...] = second[:, 192:]
    gain_out[...] = (sums_ref[384:400].astype(F32) * scale)[:1, :192]
    ftab_out[0] = tab_ref[...].astype(F32) * table_scale


def call(kernel, out_shapes, scratch=(), smem=0, flops=0, moved=0):
    def run(*args):
        specs = [pl.BlockSpec(memory_space=pltpu.SMEM)] * smem
        specs += [pl.BlockSpec(memory_space=pltpu.VMEM)] * (len(args) - smem)
        return pl.pallas_call(
            kernel,
            out_shape=[jax.ShapeDtypeStruct(s, d) for s, d in out_shapes],
            in_specs=specs,
            out_specs=[pl.BlockSpec(memory_space=pltpu.VMEM)] * len(out_shapes),
            scratch_shapes=[pltpu.VMEM(s, d) for s, d in scratch],
            compiler_params=pltpu.CompilerParams(vmem_limit_bytes=VMEM_LIMIT),
            cost_estimate=pl.CostEstimate(flops=flops, bytes_accessed=moved, transcendentals=0),
        )(*args)

    return run


def shifted(x, offset, sign):
    names = [n for n, o in zip(("lon", "lat", "rep"), offset[::-1]) if o]
    sizes = [lax.axis_size(n) for n in names]
    pairs = []
    for place in np.ndindex(*sizes):
        target = [(p - sign) % s for p, s in zip(place, sizes)]
        pairs.append((int(np.ravel_multi_index(place, sizes)), int(np.ravel_multi_index(target, sizes))))
    return lax.ppermute(x, tuple(names), pairs)


CORNERS = [(s, t, u) for s in range(2) for t in range(2) for u in range(2)]


def total(x, axes):
    return lax.psum(x, axes)


def body(
    fine_field, fine_gain, fine_qkv, fine_proj, fine_table, merge_gain, merge_weight,
    coarse_gain, coarse_qkv, coarse_proj, coarse_table, cotangent,
):
    rep, lat, lon = (lax.axis_size(n) for n in ("rep", "lat", "lon"))
    everywhere = ("lon", "lat", "rep")
    flags = jnp.stack([lax.axis_index("rep") == rep - 1, lax.axis_index("lat") == lat - 1]).astype(jnp.int32)

    packs = call(pack_kernel, [((288, 192), BF)] * 4)(fine_field, cotangent)
    bufs = []
    for s, t, u in CORNERS:
        b = packs[2 * s + t]
        bufs.append(shifted(b, (s, t, u), 1) if s + t + u else b)
    next_table = shifted(fine_table[:, :1], (0, 1, 0), 1)[0]
    bias, cbias = call(
        bias_kernel,
        [((2, 2, 6 * TOK, 128), F32), ((1, 2, 12 * TOK, 128), F32)],
        [((192, RUN), F32), ((384, RUN), F32)],
        smem=1,
    )(flags, fine_table[0], coarse_table[0])
    (next_bias,) = call(next_bias_kernel, [((1, 2, 6 * TOK, 128), F32)], [((192, RUN), F32)], smem=1)(
        flags, next_table
    )
    fgain = fine_gain.reshape(1, 192)
    x, cout, gfo, latp, lonp, cpack, ctab = call(
        main_kernel,
        [
            ((4, TOK, 192), BF), ((TOK, 384), BF), ((4, TOK, 192), BF), ((192, 192), BF), ((160, 192), BF),
            ((COARSE_ROWS, 384), BF), ((12, POS), BF),
        ],
        [
            ((9, TOK, 192), F32), ((9 * TOK, 192), BF),
            ((3, TOK, 128), F32), ((3, LANES, 128), BF), ((3, LANES, 128), BF), ((3, TOK, 128), F32),
            ((3, TOK, 128), BF), ((3, TOK, 128), BF), ((3, TOK, 128), BF), ((3, TOK, 128), BF),
            ((1, 2, 12 * TOK, 128), F32), ((384, 128), F32),
        ],
    )(
        *bufs, bias, next_bias, cbias, fgain, fine_qkv, fine_proj, merge_gain.reshape(4, 192),
        merge_weight, coarse_gain.reshape(1, 384), coarse_qkv, coarse_proj,
    )
    lat_recv = shifted(latp, (0, 1, 0), -1)
    lon_recv = shifted(lonp, (0, 0, 1), -1)
    corner_recv = shifted(lonp, (0, 1, 1), -1)
    csums = total(cpack, everywhere)
    ctab_sum = total(ctab, "lon")
    coarse_pieces = []
    for s, t, u in CORNERS:
        b = cout[HALF * s : HALF * s + HALF]
        coarse_pieces.append(shifted(b, (s, t, u), -1) if s + t + u else b)
    fg, fpack, ftab = call(
        back_kernel,
        [((2, 4 * HALF, 192), BF), ((FINE_ROWS, 384), BF), ((2, 6, POS), BF)],
        [
            ((4, TOK, 192), F32), ((3, 192, 192), F32), ((192, 192), F32), ((1, 192), F32),
            ((2, 2, 6 * TOK, 128), F32), ((192, 128), F32),
        ],
    )(x, gfo.reshape(4 * TOK, 192), lat_recv, lon_recv, corner_recv, bias, fgain, fine_qkv, fine_proj)
    fsums = total(fpack, everywhere)
    ftab_sum = total(ftab, "lon")
    fine_pieces = []
    for s, t, u in CORNERS:
        b = fg[s].reshape(2, 2, HALF, 192)
        b = (b[1:] if t else b)
        b = (b[:, 1:] if u else b)
        b = b.reshape(-1, 192)
        fine_pieces.append(shifted(b, (s, t, u), -1) if s + t + u else b)
    field_grad, coarse_out = call(
        place_kernel, [((2, 12, 24, 192), BF), ((2, 6, 12, 384), BF)]
    )(*fine_pieces, *coarse_pieces)
    levels, rows, cols = 2 * rep, 12 * lat, 24 * lon
    fine_scale = (levels * rows * cols) ** -0.5
    coarse_scale = (levels * rows * cols // 4) ** -0.5
    fine_table_scale = (cols // 12) ** -0.5
    coarse_table_scale = (cols // 24) ** -0.5
    mgain_g, mw_g, cgain_g, cqkv_g, cproj_g, ctab_g = call(
        lambda a, b, *o: coarse_unpack_kernel(coarse_scale, a, b, coarse_table_scale, *o),
        [((1, 768), F32), ((768, 384), F32), ((1, 384), F32), ((384, 1152), F32), ((384, 384), F32), ((1, 12, POS), F32)],
    )(csums, ctab_sum)
    fgain_g, fqkv_g, fproj_g, ftab_g = call(
        lambda a, b, *o: fine_unpack_kernel(fine_scale, a, b, fine_table_scale, *o),
        [((1, 192), F32), ((192, 576), F32), ((192, 192), F32), ((1, 2, 6, POS), F32)],
    )(fsums, ftab_sum)
    return (
        coarse_out, field_grad, fgain_g.reshape(192), fqkv_g, fproj_g, ftab_g,
        mgain_g.reshape(768), mw_g, cgain_g.reshape(384), cqkv_g, cproj_g, ctab_g.reshape(1, 1, 12, POS),
    )


def solution(mesh):
    tokens, tables = P("rep", "lat", "lon", None), P("rep", "lat", None, None)
    return jax.shard_map(
        body,
        mesh=mesh,
        in_specs=(tokens, P(), P(), P(), tables, P(), P(), P(), P(), P(), tables, tokens),
        out_specs=(tokens, tokens, P(), P(), P(), tables, P(), P(), P(), P(), P(), tables),
        check_vma=False,
    )
```

time: 982 us -> 540 us (0.55)
  local copies, waits for them, and re-layouts: 364 us -> 16.4 us
  blocking collectives: 81.2 us -> 0 us
  other arithmetic: 81.3 us -> 3.13 us
  Pallas kernels: 0 us -> 75.1 us
  matrix products: 48.7 us -> 0 us
  waiting for transfers between devices: 339 us -> 387 us
    slice x46 -> x6, local copies, waits for them, and re-layouts: 92.8 us -> 1.71 us  [the longest x1 0.97 us: body(): next_table = shifted(fine_table[:, :1], (0, 1, 0), 1)[0]]
    psum x1 -> x0, blocking collectives: 81.2 us -> none  [body(): joined = lax.psum(fine_parts + coarse_parts, ('lon', 'lat', 'rep'))]
    pallas_call x0 -> x8, Pallas kernels: none -> 75.1 us  [run(): pl.pallas_call(kernel, out_shape=[jax.ShapeDtypeStruct(s, d) for s, d in...]
    reshape x9 -> x4, local copies, waits for them, and re-layouts: 73.1 us -> 2.61 us  [the longest x1 1.35 us: body(): merge_gain.reshape(4, 192)]
    psum x2, waiting for transfers between devices: 319 us -> 372 us  [total(): return lax.psum(x, axes)]
    another operation x11 -> x0, local copies, waits for them, and re-layouts: 49.4 us -> none  [the longest x2 32.8 us: attention_pieces(): bias[:, :, None]]
    dot_general x26 -> x0, matrix products: 44.3 us -> none  [the longest x11 23.1 us: batched(): return jnp.einsum(form, left, right, preferred_element_type=jnp.float32)]
    unnamed x232 -> x62, local copies, waits for them, and re-layouts: 45.3 us -> 10.5 us
  transfers between devices with their start and end apart: 26 -> 27, of which waited for: 13 -> 9; matrix products, arithmetic and copies ran while one was open for 31% -> 2% of each run, Pallas kernels for 0% -> 2%
where the time goes in v1:
time: 540 us; the launch traced here: 533 us
  waiting for transfers between devices  387 us (72%)
  Pallas kernels  75.1 us (14%)
  starting transfers between devices  37.3 us (7%)
  local copies, waits for them, and re-layouts  16.4 us (3%)
  between operations  14.8 us (3%)
    psum x2, waiting for transfers between devices, total(): return lax.psum(x, axes)  372 us
    pallas_call x8, Pallas kernels, run(): pl.pallas_call(kernel, out_shape=[jax.ShapeDtypeStruct(s, d) for s, d in...  75.1 us
    ppermute x25, starting transfers between devices, shifted(): return lax.ppermute(x, tuple(names), pairs)  37.2 us
    ppermute x25, waiting for transfers between devices, shifted(): return lax.ppermute(x, tuple(names), pairs)  14 us
  transfers between devices with their start and end apart: 27, of which 9 were waited for; matrix products, arithmetic and copies ran while one was open for 2% of the time, Pallas kernels for 2%

profile of v1, /device:TPU:1, one launch (start us, length us, event | category | flops | bytes accessed | tf_op | source)
XLA Modules:
  0.0 533.5 jit_solution(3474609864987649165)
XLA Ops:
  8.8 1.9 shard_map.211
  10.7 3.2 collective-permute-start
  13.9 8.6 %collective-permute-start.2 = (bf16[288,192]{1,0:T(8,128)(2,1)}, bf16[288,192]{1,0:T(8,128)(2,1)S(1)}, u32[]{:S(2)}, u32[]{:S(2)}) collective-permute-start(bf16[288,192]{1,0:T(8,128)(2,1)} %get-tuple-element.41), channel_id=1, source_target_pairs={{0,254},{2,240},{4,242},{6,244},{8,246},{10,248},{12,250},{14,252}... | collective-permute-start | bytes 331784 | tf_op jit(solution)/shard_map/ppermute | solution.py:575
  26.4 1.6 copy.45
  35.3 6.3 %shard_map.212 = (f32[2,2,864,128]{3,2,1,0:T(8,128)}, f32[1,2,1728,128]{3,2,1,0:T(8,128)}) custom-call(s32[2]{0:T(128)} %add_convert_fusion.flags_ref, f32[2,6,3312]{2,1,0:T(8,128)} %bitcast.33, f32[1,12,3312]{2,1,0:T(8,128)} %copy.34.coarse_ref), custom_call_target="tpu_custom_call" | custom-call | tf_op jit(solution)/shard_map/pallas_call | solution.py:555
  41.6 3.0 shard_map.213.next_bias_ref
  45.4 34.4 %shard_map.214 = (bf16[4,144,192]{2,1,0:T(8,128)(2,1)}, bf16[144,384]{1,0:T(8,128)(2,1)}, bf16[4,144,192]{2,1,0:T(8,128)(2,1)}, bf16[192,192]{1,0:T(8,128)(2,1)}...) custom-call(bf16[288,192]{1,0:T(8,128)(2,1)} %get-tuple-element.40.b000, ...), custom_call_target="tpu_custom_call" | custom-call | tf_op jit(solution)/shard_map/pallas_call | solution.py:555
  81.4 2.9 collective-permute-start.10
  84.3 2.4 collective-permute-done.10.corner_ref
  87.4 21.4 %shard_map.215 = (bf16[2,288,192]{2,1,0:T(8,128)(2,1)}, bf16[512,384]{1,0:T(8,128)(2,1)}, bf16[2,6,3312]{2,1,0:T(8,128)(2,1)}) custom-call(bf16[4,144,192]{2,1,0:T(8,128)(2,1)} %get-tuple-element.46.x_in, bf16[576,192]{1,0:T(8,128)(2,1)} %bitcast.36, bf16[192,192]{1,0:T(8,128)(2,1)} %copy-done.12, bf16[160,192]{1,0:T(8,128)(2,1)} %copy-done.14, ...), custom_call_target="tpu_custom_call" | custom-call | tf_op jit(solution)/shard_map/pallas_call | solution.py:555
  109.7 3.6 collective-permute-start.24
  123.4 2.5 collective-permute-start.12
  126.6 2.9 collective-permute-done.13.refs_3_
  129.5 1.8 collective-permute-start.11
  131.6 2.3 collective-permute-done.11.refs_1_
  134.0 3.7 collective-permute-done.15.refs_5_
  138.4 2.7 shard_map.216
  141.1 1.6 copy.38
  142.7 102.8 %all-reduce.7.cloned.1.call-done = (bf16[2,6,3312]{2,1,0:T(8,128)(2,1)}, bf16[12,3312]{1,0:T(8,128)(2,1)}) async-done(((bf16[2,6,3312]{2,1,0:T(8,128)(2,1)}, bf16[12,3312]{1,0:T(8,128)(2,1)}), (bf16[2,6,3312]{2,1,0:T(8,128)(2,1)}, bf16[12,3312]{1,0:T(8,128)(2,1)})) %all-reduce.7.cloned.1.call-update) | async-done | bytes 158992 | tf_op jit(solution)/shard_map/psum | solution.py:582
  245.5 269.1 %all-reduce.5.cloned.1.call-done = (bf16[512,384]{1,0:T(8,128)(2,1)}, bf16[2560,384]{1,0:T(8,128)(2,1)}) async-done(((bf16[512,384]{1,0:T(8,128)(2,1)}, bf16[2560,384]{1,0:T(8,128)(2,1)}), (bf16[512,384]{1,0:T(8,128)(2,1)}, bf16[2560,384]{1,0:T(8,128)(2,1)})) %all-reduce.5.cloned.1.call-update) | async-done | bytes 2359312 | tf_op jit(solution)/shard_map/psum | solution.py:582
  514.6 2.0 shard_map.217
  516.6 1.7 copy.39
  518.3 3.5 shard_map.218
  524.4 1.8 copy.40
  (116 shorter events, 30.9 us)
Async XLA Ops:
  7.2 238.3 %all-reduce.7.cloned.1.call-start = ((), (), s32[]{:S(2)}) async-start(), calls=%async_computation.1 | async-start | bytes 425984 | tf_op jit(solution)/shard_map/psum | solution.py:582
  10.7 22.7 %collective-permute-start = (bf16[288,192]{1,0:T(8,128)(2,1)}, bf16[288,192]{1,0:T(8,128)(2,1)S(1)}, u32[]{:S(2)}, u32[]{:S(2)}) collective-permute-start(bf16[288,192]{1,0:T(8,128)(2,1)} %get-tuple-element.40.b000), channel_id=1, source_target_pairs={{0,240},{16,0},{32,16},{48,32},{64,48},{80,64},{96,80},{112,96},{1... | collective-permute-start | bytes 331784 | tf_op jit(solution)/shard_map/ppermute | solution.py:575
  13.9 20.6 %collective-permute-start.2 = (bf16[288,192]{1,0:T(8,128)(2,1)}, bf16[288,192]{1,0:T(8,128)(2,1)S(1)}, u32[]{:S(2)}, u32[]{:S(2)}) collective-permute-start(bf16[288,192]{1,0:T(8,128)(2,1)} %get-tuple-element.41), channel_id=1, source_target_pairs={{0,254},{2,240},{4,242},{6,244},{8,246},{10,248},{12,250},{14,252}... | collective-permute-start | bytes 331784 | tf_op jit(solution)/shard_map/ppermute | solution.py:575
  23.6 8.6 %collective-permute-start.7 = (f32[1,1,6,3312]{3,2,1,0:T(8,128)S(1)}, f32[1,1,6,3312]{3,2,1,0:T(8,128)S(1)}, u32[]{:S(2)}, u32[]{:S(2)}) collective-permute-start(f32[1,1,6,3312]{3,2,1,0:T(8,128)S(1)} %copy.44), channel_id=1, source_target_pairs={{0,14},{2,0},{4,2},{6,4},{8,6},{10,8},{12,10},{14,12},{1,15},{3,1}... | collective-permute-start | bytes 238472 | tf_op jit(solution)/shard_map/ppermute | solution.py:575
  24.4 20.2 %collective-permute-start.1 = (bf16[288,192]{1,0:T(8,128)(2,1)}, bf16[288,192]{1,0:T(8,128)(2,1)S(1)}, u32[]{:S(2)}, u32[]{:S(2)}) collective-permute-start(bf16[288,192]{1,0:T(8,128)(2,1)} %get-tuple-element.41), channel_id=1, source_target_pairs={{0,14},{2,0},{4,2},{6,4},{8,6},{10,8},{12,10},{14,12},{1,15},{3,1}... | collective-permute-start | bytes 331784 | tf_op jit(solution)/shard_map/ppermute | solution.py:575
  25.1 19.4 %collective-permute-start.4 = (bf16[288,192]{1,0:T(8,128)(2,1)}, bf16[288,192]{1,0:T(8,128)(2,1)S(1)}, u32[]{:S(2)}, u32[]{:S(2)}) collective-permute-start(bf16[288,192]{1,0:T(8,128)(2,1)} %get-tuple-element.42), channel_id=1, source_target_pairs={{0,241},{1,240},{16,1},{17,0},{32,17},{33,16},{48,33},{49,32},{64,... | collective-permute-start | bytes 331784 | tf_op jit(solution)/shard_map/ppermute | solution.py:575
  32.2 12.4 %collective-permute-start.3 = (bf16[288,192]{1,0:T(8,128)(2,1)}, bf16[288,192]{1,0:T(8,128)(2,1)S(1)}, u32[]{:S(2)}, u32[]{:S(2)}) collective-permute-start(bf16[288,192]{1,0:T(8,128)(2,1)} %get-tuple-element.42), channel_id=1, source_target_pairs={{0,1},{1,0},{2,3},{3,2},{4,5},{5,4},{6,7},{7,6},{8,9},{9,8},{10,11... | collective-permute-start | bytes 331784 | tf_op jit(solution)/shard_map/ppermute | solution.py:575
  33.4 11.2 %collective-permute-start.6 = (bf16[288,192]{1,0:T(8,128)(2,1)}, bf16[288,192]{1,0:T(8,128)(2,1)S(1)}, u32[]{:S(2)}, u32[]{:S(2)}) collective-permute-start(bf16[288,192]{1,0:T(8,128)(2,1)} %get-tuple-element.43), channel_id=1, source_target_pairs={{0,255},{1,254},{2,241},{3,240},{4,243},{5,242},{6,245},{7,244},{8... | collective-permute-start | bytes 331784 | tf_op jit(solution)/shard_map/ppermute | solution.py:575
  34.5 10.1 %collective-permute-start.5 = (bf16[288,192]{1,0:T(8,128)(2,1)}, bf16[288,192]{1,0:T(8,128)(2,1)S(1)}, u32[]{:S(2)}, u32[]{:S(2)}) collective-permute-start(bf16[288,192]{1,0:T(8,128)(2,1)} %get-tuple-element.43), channel_id=1, source_target_pairs={{0,15},{1,14},{2,1},{3,0},{4,3},{5,2},{6,5},{7,4},{8,7},{9,6},{10,... | collective-permute-start | bytes 331784 | tf_op jit(solution)/shard_map/ppermute | solution.py:575
  79.9 6.9 %collective-permute-start.8 = (bf16[192,192]{1,0:T(8,128)(2,1)}, bf16[192,192]{1,0:T(8,128)(2,1)S(1)}, u32[]{:S(2)}, u32[]{:S(2)}) collective-permute-start(bf16[192,192]{1,0:T(8,128)(2,1)} %get-tuple-element.48), channel_id=1, source_target_pairs={{0,2},{2,4},{4,6},{6,8},{8,10},{10,12},{12,14},{14,0},{1,3},{3,5},... | collective-permute-start | bytes 221192 | tf_op jit(solution)/shard_map/ppermute | solution.py:575
  81.4 5.3 %collective-permute-start.10 = (bf16[160,192]{1,0:T(8,128)(2,1)}, bf16[160,192]{1,0:T(8,128)(2,1)S(1)}, u32[]{:S(2)}, u32[]{:S(2)}) collective-permute-start(bf16[160,192]{1,0:T(8,128)(2,1)} %get-tuple-element.49), channel_id=1, source_target_pairs={{0,18},{2,20},{4,22},{6,24},{8,26},{10,28},{12,30},{14,16},{16,34}... | collective-permute-start | bytes 184328 | tf_op jit(solution)/shard_map/ppermute | solution.py:575
  108.8 405.8 %all-reduce.5.cloned.1.call-start = ((), (), s32[]{:S(2)}) async-start(), calls=%async_computation | async-start | bytes 4718592 | tf_op jit(solution)/shard_map/psum | solution.py:582
  109.7 8.9 %collective-permute-start.24 = (bf16[72,384]{1,0:T(8,128)(2,1)S(1)}, bf16[72,384]{1,0:T(8,128)(2,1)S(1)}, u32[]{:S(2)}, u32[]{:S(2)}) collective-permute-start(bf16[72,384]{1,0:T(8,128)(2,1)S(1)} %get-tuple-element.104), channel_id=1, source_target_pairs={{0,19},{1,18},{2,21},{3,20},{4,23},{5,22},{6,25},{7,24},{8,27},{9,... | collective-permute-start | bytes 165896 | tf_op jit(solution)/shard_map/ppermute | solution.py:575
  113.3 6.8 %collective-permute-start.23 = (bf16[72,384]{1,0:T(8,128)(2,1)S(1)}, bf16[72,384]{1,0:T(8,128)(2,1)S(1)}, u32[]{:S(2)}, u32[]{:S(2)}) collective-permute-start(bf16[72,384]{1,0:T(8,128)(2,1)S(1)} %get-tuple-element.104), channel_id=1, source_target_pairs={{0,3},{1,2},{2,5},{3,4},{4,7},{5,6},{6,9},{7,8},{8,11},{9,10},{10,... | collective-permute-start | bytes 165896 | tf_op jit(solution)/shard_map/ppermute | solution.py:575
  114.9 6.5 %collective-permute-start.22 = (bf16[72,384]{1,0:T(8,128)(2,1)S(1)}, bf16[72,384]{1,0:T(8,128)(2,1)S(1)}, u32[]{:S(2)}, u32[]{:S(2)}) collective-permute-start(bf16[72,384]{1,0:T(8,128)(2,1)S(1)} %get-tuple-element.104), channel_id=1, source_target_pairs={{0,17},{1,16},{16,33},{17,32},{32,49},{33,48},{48,65},{49,64},{64,... | collective-permute-start | bytes 165896 | tf_op jit(solution)/shard_map/ppermute | solution.py:575
  114.9 6.9 %collective-permute-start.21 = (bf16[72,384]{1,0:T(8,128)(2,1)S(1)}, bf16[72,384]{1,0:T(8,128)(2,1)S(1)}, u32[]{:S(2)}, u32[]{:S(2)}) collective-permute-start(bf16[72,384]{1,0:T(8,128)(2,1)S(1)} %get-tuple-element.104), channel_id=1, source_target_pairs={{0,1},{1,0},{2,3},{3,2},{4,5},{5,4},{6,7},{7,6},{8,9},{9,8},{10,11... | collective-permute-start | bytes 165896 | tf_op jit(solution)/shard_map/ppermute | solution.py:575
  115.9 6.3 %collective-permute-start.20 = (bf16[72,384]{1,0:T(8,128)(2,1)S(1)}, bf16[72,384]{1,0:T(8,128)(2,1)S(1)}, u32[]{:S(2)}, u32[]{:S(2)}) collective-permute-start(bf16[72,384]{1,0:T(8,128)(2,1)S(1)} %get-tuple-element.105.refs_8_), channel_id=1, source_target_pairs={{0,18},{2,20},{4,22},{6,24},{8,26},{10,28},{12,30},{14,16},{16,34}... | collective-permute-start | bytes 165896 | tf_op jit(solution)/shard_map/ppermute | solution.py:575
  120.2 5.8 %collective-permute-start.18 = (bf16[72,384]{1,0:T(8,128)(2,1)S(1)}, bf16[72,384]{1,0:T(8,128)(2,1)S(1)}, u32[]{:S(2)}, u32[]{:S(2)}) collective-permute-start(bf16[72,384]{1,0:T(8,128)(2,1)S(1)} %get-tuple-element.105.refs_8_), channel_id=1, source_target_pairs={{0,16},{16,32},{32,48},{48,64},{64,80},{80,96},{96,112},{112,128},... | collective-permute-start | bytes 165896 | tf_op jit(solution)/shard_map/ppermute | solution.py:575
  121.3 8.2 %collective-permute-start.13 = (bf16[72,192]{1,0:T(8,128)(2,1)S(1)}, bf16[72,192]{1,0:T(8,128)(2,1)S(1)}, u32[]{:S(2)}, u32[]{:S(2)}) collective-permute-start(bf16[72,192]{1,0:T(8,128)(2,1)S(1)} %slice_bitcast_fusion.1), channel_id=1, source_target_pairs={{0,18},{2,20},{4,22},{6,24},{8,26},{10,28},{12,30},{14,16},{16,34}... | collective-permute-start | bytes 82952 | tf_op jit(solution)/shard_map/ppermute | solution.py:575
  121.8 16.0 %collective-permute-start.14 = (bf16[288,192]{1,0:T(8,128)(2,1)S(1)}, bf16[288,192]{1,0:T(8,128)(2,1)S(1)}, u32[]{:S(2)}, u32[]{:S(2)}) collective-permute-start(bf16[288,192]{1,0:T(8,128)(2,1)S(1)} %get-tuple-element.102), channel_id=1, source_target_pairs={{0,1},{1,0},{2,3},{3,2},{4,5},{5,4},{6,7},{7,6},{8,9},{9,8},{10,11... | collective-permute-start | bytes 331784 | tf_op jit(solution)/shard_map/ppermute | solution.py:575
  122.2 9.1 %collective-permute-start.17 = (bf16[72,192]{1,0:T(8,128)(2,1)S(1)}, bf16[72,192]{1,0:T(8,128)(2,1)S(1)}, u32[]{:S(2)}, u32[]{:S(2)}) collective-permute-start(bf16[72,192]{1,0:T(8,128)(2,1)S(1)} %slice_bitcast_fusion), channel_id=1, source_target_pairs={{0,19},{1,18},{2,21},{3,20},{4,23},{5,22},{6,25},{7,24},{8,27},{9,... | collective-permute-start | bytes 82952 | tf_op jit(solution)/shard_map/ppermute | solution.py:575
  123.4 7.9 %collective-permute-start.12 = (bf16[144,192]{1,0:T(8,128)(2,1)S(1)}, bf16[144,192]{1,0:T(8,128)(2,1)S(1)}, u32[]{:S(2)}, u32[]{:S(2)}) collective-permute-start(bf16[144,192]{1,0:T(8,128)(2,1)S(1)} %get-tuple-element.97), channel_id=1, source_target_pairs={{0,2},{2,4},{4,6},{6,8},{8,10},{10,12},{12,14},{14,0},{1,3},{3,5},... | collective-permute-start | bytes 165896 | tf_op jit(solution)/shard_map/ppermute | solution.py:575
  125.9 5.7 %collective-permute-start.16 = (bf16[144,192]{1,0:T(8,128)(2,1)S(1)}, bf16[144,192]{1,0:T(8,128)(2,1)S(1)}, u32[]{:S(2)}, u32[]{:S(2)}) collective-permute-start(bf16[144,192]{1,0:T(8,128)(2,1)S(1)} %get-tuple-element.98), channel_id=1, source_target_pairs={{0,3},{1,2},{2,5},{3,4},{4,7},{5,6},{6,9},{7,8},{8,11},{9,10},{10,... | collective-permute-start | bytes 165896 | tf_op jit(solution)/shard_map/ppermute | solution.py:575
  131.3 6.4 %collective-permute-start.15 = (bf16[144,192]{1,0:T(8,128)(2,1)S(1)}, bf16[144,192]{1,0:T(8,128)(2,1)S(1)}, u32[]{:S(2)}, u32[]{:S(2)}) collective-permute-start(bf16[144,192]{1,0:T(8,128)(2,1)S(1)} %bitcast.42), channel_id=1, source_target_pairs={{0,17},{1,16},{16,33},{17,32},{32,49},{33,48},{48,65},{49,64},{64,... | collective-permute-start | bytes 165896 | tf_op jit(solution)/shard_map/ppermute | solution.py:575
  (31 other events, 228.0 us)
Sparse Core Ops, SparseCore 0:
  109.0 136.4 all-reduce.6
  252.7 261.8 all-reduce.4

commit v2 on v1

v2 whole, which is shorter than its diff:
```python
import numpy as np
import jax
import jax.numpy as jnp
from jax import lax
from jax.experimental import pallas as pl
from jax.experimental.pallas import tpu as pltpu
from jax.sharding import PartitionSpec as P

F32, BF = jnp.float32, jnp.bfloat16
EPS = 1e-05
TOK, HALF, LANES = 144, 72, 256
POS, DIAG = 3312, 23
RUN = 6 * DIAG
HEAD = 32
NEG = -1e30
COARSE, FINE, TAB = 432, 80, 64
GRAIN = COARSE + FINE
WIDE = 3328
VMEM_LIMIT = 56 * 1024 * 1024


def dot(a, b, ca, cb):
    return lax.dot_general(a, b, (((ca,), (cb,)), ((), ())), preferred_element_type=F32)


def mm(a, b):
    return dot(a, b, 1, 0)


def mm_t(a, b):
    return dot(a, b, 1, 1)


def t_mm(a, b):
    return dot(a, b, 0, 0)


def low(x):
    return x.astype(BF)


def split3(x):
    hi = low(x)
    rest = x - hi.astype(F32)
    mid = low(rest)
    return hi, mid, low(rest - mid.astype(F32))


def iota(shape, dim):
    return lax.broadcasted_iota(jnp.int32, shape, dim)


def div_const(x, n):
    return lax.shift_right_logical(x * (65536 // n + 1), 16)


def one_hot(target, count):
    return jnp.where(iota((target.shape[0], count), 1) == target, 1.0, 0.0).astype(BF)


def window_index(rows):
    r = iota((rows, 1), 0)
    z = div_const(r, 72)
    r = r - z * 72
    w = div_const(r, 6)
    return z, r - w * 6, w


def pad_keys(x):
    gap = jnp.zeros((128 - HALF, x.shape[1]), F32)
    return low(jnp.concatenate([x[:HALF], gap, x[HALF:], gap], axis=0))


def unpad_keys(x):
    return jnp.concatenate([x[:HALF], x[128 : 128 + HALF]], axis=0)


def norm(x):
    width = sum(p.shape[1] for p in x)
    mean = sum(jnp.sum(p, axis=1, keepdims=True) for p in x) * (1.0 / width)
    shifted = [p - mean for p in x]
    var = sum(jnp.sum(p * p, axis=1, keepdims=True) for p in shifted) * (1.0 / width)
    inv = lax.rsqrt(var + EPS)
    return [p * inv for p in shifted], inv


def norm_back(grad, gain, hat, inv):
    width = sum(p.shape[1] for p in grad)
    scaled = [g * a for g, a in zip(grad, gain)]
    first = sum(jnp.sum(s, axis=1, keepdims=True) for s in scaled) * (1.0 / width)
    second = sum(jnp.sum(s * n, axis=1, keepdims=True) for s, n in zip(scaled, hat)) * (1.0 / width)
    gains = [jnp.sum(g * n, axis=0, keepdims=True) for g, n in zip(grad, hat)]
    return [inv * (s - first - n * second) for s, n in zip(scaled, hat)], gains


def load_bias(ref, kind, rows):
    return jnp.concatenate([ref[kind, 0, rows], ref[kind, 1, rows]], axis=1)


def head_mask(width, slot):
    lane = iota((1, width), 1)
    return (lane >= slot * HEAD) & (lane < (slot + 1) * HEAD)


def only_head(x, slot):
    return x * jnp.where(head_mask(x.shape[1], slot), 1.0, 0.0).astype(BF)


def by_head(x, slots):
    return jnp.concatenate([only_head(x, slot) for slot in range(slots)], axis=0)


def own_columns(x, slots):
    out = x[:TOK]
    for slot in range(1, slots):
        out = jnp.where(head_mask(x.shape[1], slot), x[slot * TOK : (slot + 1) * TOK], out)
    return out


def probabilities(q_stack, keys, bias):
    e = jnp.exp(mm_t(q_stack, keys) + bias)
    return e * (1.0 / jnp.sum(e, axis=1, keepdims=True))


def tile_forward(q, keys, values, bias, slots):
    p = probabilities(by_head(q, slots), keys, bias)
    return own_columns(mm(low(p), values), slots)


def tile_both(q, keys, values, gmix, bias, bias_grad_to, slots):
    q_stack, g_stack = by_head(q, slots), by_head(gmix, slots)
    p = probabilities(q_stack, keys, bias)
    p_low = low(p)
    mixed = own_columns(mm(p_low, values), slots)
    gp = mm_t(g_stack, values)
    gs = p * (gp - jnp.sum(p * gp, axis=1, keepdims=True))
    bias_grad_to(gs)
    gs_low = low(gs)
    gq = own_columns(mm(gs_low, keys), slots)
    return mixed, gq, t_mm(gs_low, q_stack), t_mm(p_low, g_stack)


def put(ref, grain, start, value, place=lambda chunk: chunk):
    at = 0
    while at < value.shape[0]:
        chunk, row = divmod(start + at, grain)
        n = min(grain - row, value.shape[0] - at)
        ref[place(chunk), row : row + n] = value[at : at + n]
        at += n


def place_of(chunk):
    return chunk % 8 * 2 + chunk // 8


def get_chunk(sums, chunk, rows):
    mine, other, core = sums
    return jnp.where(core == chunk // 8, mine[chunk % 8, rows].astype(F32), other[chunk % 8, rows].astype(F32))


def get(sums, grain, base, start, count):
    parts, at = [], 0
    while at < count:
        chunk, row = divmod(start + at, grain)
        n = min(grain - row, count - at)
        parts.append(get_chunk(sums, chunk, slice(base + row, base + row + n)))
        at += n
    return parts[0] if len(parts) == 1 else jnp.concatenate(parts, axis=0)


def gain_rows(pieces):
    line = pieces[0] if len(pieces) == 1 else jnp.concatenate(pieces, axis=1)
    width = line.shape[1]
    if width % 128:
        line = jnp.concatenate([line, jnp.zeros((1, 128 - width % 128), F32)], axis=1)
    rows = [line[:, 128 * i : 128 * i + 128] for i in range(line.shape[1] // 128)]
    rows.append(jnp.zeros((16 - len(rows), 128), F32))
    return low(jnp.concatenate(rows, axis=0))


def diagonal_select(first):
    lane = iota((1, 256), 1)
    wq = first + lax.shift_right_logical(lane, 7)
    lane = lane & 127
    wk = div_const(lane, 6)
    hk = lane - wk * 6
    diagonal = wq - wk + 11
    low_half = jnp.where((lane < HALF) & (hk < 3), hk * DIAG + diagonal, -1)
    high_half = jnp.where((lane < HALF) & (hk >= 3), (hk - 3) * DIAG + diagonal + 128, -1)
    target = jnp.maximum(low_half, high_half)
    return jnp.where(iota((256, 256), 0) == target, 1.0, 0.0).astype(BF)


HALF_RUN = 3 * DIAG


def table_groups():
    return [(g, (g // 12) * 16 + ((g // 6) % 2) * 8 + g % 6) for g in range(24)]


def table_slice(table, start):
    n = min(128, POS - start)
    part = table[:, start : start + n]
    if n < 128:
        part = jnp.concatenate([part, jnp.zeros((part.shape[0], 128 - n), F32)], axis=1)
    return part


def expand_tables(at_end, kinds, u_ref):
    lane, sub = iota((8, 128), 1), iota((8, 128), 0)
    column = div_const(lane, 6)
    crossing = (sub >= 3) != (lane - column * 6 >= 3)
    outside = jnp.where(lane >= HALF, NEG, 0.0)
    lev_term = jnp.where(at_end[0], NEG, 0.0)
    lat_term = jnp.where(crossing, jnp.where(at_end[1], NEG, 0.0), 0.0)
    u_ref[...] = jnp.zeros(u_ref.shape, F32)
    base = 0
    for table, _, _ in kinds:
        heads = table.shape[0]
        for g, row in table_groups():
            for half in range(2):
                u_ref[half, pl.ds(base + row, heads, stride=32)] = table_slice(table, g * RUN + half * HALF_RUN)
        base += heads * 32
    u = jnp.concatenate([u_ref[0], u_ref[1]], axis=1)
    hi = low(u)
    mid = low(u - hi.astype(F32))
    for first in range(0, 12, 2):
        sel = diagonal_select(first)
        x = mm(hi, sel) + mm(mid, sel)
        base = 0
        for table, may_end, out_ref in kinds:
            same = outside + lat_term if may_end else outside
            terms = same, same + lev_term
            for n in range(table.shape[0]):
                for zq in range(2):
                    for zk in range(2):
                        at = base + zq * 16 + zk * 8
                        for k in range(2):
                            to = n * TOK + zq * HALF + (first + k) * 6
                            part = x[at : at + 8, 128 * k : 128 * k + 128]
                            out_ref[zk, to : to + 6] = (part + terms[zq != zk])[:6]
                base += 32


def fold_tables(types, heads, grad_ref, y_ref, acc_ref, out_to):
    y_ref[...] = jnp.zeros(y_ref.shape, F32)
    for t in range(types):
        acc = None
        for first in range(0, 12, 2):
            sel = diagonal_select(first)
            for n in range(heads):
                for zq in range(2):
                    for zk in range(2):
                        at = n * 32 + zq * 16 + zk * 8
                        for k in range(2):
                            to = n * TOK + zq * HALF + (first + k) * 6
                            y_ref[at : at + 6, 128 * k : 128 * k + 128] = grad_ref[t, zk, to : to + 6]
            y = y_ref[...]
            hi = low(y)
            part = mm_t(hi, sel) + mm_t(low(y - hi.astype(F32)), sel)
            acc = part if acc is None else acc + part
        for half in range(2):
            acc_ref[half] = acc[:, 128 * half : 128 * half + 128]
        for g, row in table_groups():
            for half in range(2):
                out_to(t, g * RUN + half * HALF_RUN, acc_ref[half, pl.ds(row, heads, stride=32)][:, :HALF_RUN])


def bias_kernel(fine_ref, next_ref, coarse_ref, fine_out, coarse_out, u_ref):
    at_end = [lax.axis_index(name) == lax.axis_size(name) - 1 for name in ("rep", "lat")]
    kinds = [
        (fine_ref[:, 0, :], False, fine_out.at[0]),
        (fine_ref[:, 1, :], True, fine_out.at[1]),
        (next_ref[:, 0, :], False, fine_out.at[2]),
        (coarse_ref[:, 0, :], True, coarse_out.at[0]),
    ]
    expand_tables(at_end, kinds, u_ref)


def pack_kernel(field_ref, cot_ref, *outs):
    for s in range(2):
        for t in range(2):
            out = outs[2 * s + t]
            lev = 1 - s
            row, crow = (3, 3) if t == 0 else (0, 0)
            for h in range(9):
                out[h * 24 : h * 24 + 24] = field_ref[lev, row + h]
            for h in range(3):
                part = cot_ref[crow + h, :, lev, :].astype(F32)
                both = jnp.concatenate([part[:, :192], part[:, 192:]], axis=0)
                out[216 + h * 24 : 240 + h * 24] = low(both)


def fine_weights(qkv_ref):
    w = qkv_ref[...]
    return w[:, :192], w[:, 192:384], w[:, 384:]


FINE_TILES = ((0, 128, 4), (128, 64, 2))


def tile_rows(start, slots):
    return slice(start // HEAD * TOK, (start // HEAD + slots) * TOK)


def store_keys(ref, x):
    gap = jnp.zeros((128 - HALF, x.shape[1]), F32)
    for n in range(ref.shape[0]):
        part = x[n * TOK : (n + 1) * TOK]
        for z in range(2):
            ref[n, 128 * z : 128 * z + 128] = low(jnp.concatenate([part[HALF * z : HALF * z + HALF], gap], axis=0))


def main_kernel(
    b000, b001, b010, b011, b100, b101, b110, b111,
    bias_ref, cbias_ref,
    fgain_ref, fqkv_ref, fproj_ref, mgain_ref, mw_ref, cgain_ref, cqkv_ref, cproj_ref,
    x_out, gfo_out, latp_out, lonp_out, cin_out, gy_out, xc_out, mnorm_out, gci_out, mix_ref, g_ref, gb_ref, gains_out,
    x_ref, fo_ref, fq_ref, fk_ref, fv_ref, fm_ref,
    q_ref, k_ref, v_ref, gm_ref,
):
    bufs = ((b000, b001), (b010, b011)), ((b100, b101), (b110, b111))
    _, hh, ww = window_index(HALF)
    seen = set()
    for t in range(2):
        for u in range(2):
            hots = []
            for wr in (t, t + 1):
                for wc in (u, u + 1):
                    lat = 6 * wr + hh - 9 * t
                    lon = 12 * wc + ww - 18 * u
                    good = (lat >= 0) & (lat < 9) & (lon >= 0) & (lon < 18)
                    hots.append(one_hot(jnp.where(good, lat * 24 + lon + (6 if u == 0 else 0), -1), 216))
            hot = jnp.concatenate(hots, axis=0)
            for z in range(2):
                part = mm(hot, bufs[z][t][u][:216])
                for n in range(4):
                    place = 3 * (t + n // 2) + u + n % 2, slice(z * HALF, (z + 1) * HALF)
                    value = part[n * HALF : (n + 1) * HALF]
                    if (place[0], z) in seen:
                        value = value + x_ref[place]
                    seen.add((place[0], z))
                    x_ref[place] = value
    for wr in range(2):
        for wc in range(2):
            x_out[2 * wr + wc] = low(x_ref[3 * wr + wc])
    wq, wk, wv = fine_weights(fqkv_ref)
    x = x_ref[...].reshape(9 * TOK, 192)
    (hat,), _ = norm([x])
    xn = low(hat * fgain_ref[...].reshape(1, 192))
    fq_ref[...] = low(mm(xn, wq) * HEAD**-0.5).reshape(9, TOK, 192)
    store_keys(fk_ref, mm(xn, wk))
    store_keys(fv_ref, mm(xn, wv))

    def fine_window(w, table_ref, wr):
        for start, width, slots in FINE_TILES:
            lanes = slice(start, start + width)

            bias = load_bias(table_ref, wr, tile_rows(start, slots))
            fm_ref[w, :, lanes] = low(
                tile_forward(fq_ref[w, :, lanes], fk_ref[w, :, lanes], fv_ref[w, :, lanes], bias, slots)
            )

    @pl.loop(0, 9)
    def _(w):
        fine_window(w, bias_ref, div_const(w, 3))

    out = low(mm(fm_ref[...].reshape(9 * TOK, 192), fproj_ref[...])).astype(F32)
    fo_ref[...] = low(x_ref[...].reshape(9 * TOK, 192) + out)

    z, i, j = window_index(TOK)
    hots = []
    for p in range(4):
        lat = 3 + 2 * i + p // 2
        lon = 6 + 2 * j + p % 2
        wr, wc = div_const(lat, 6), div_const(lon, 12)
        target = (3 * wr + wc) * TOK + z * HALF + (lon - 12 * wc) * 6 + lat - 6 * wr
        hots.append(one_hot(target, 9 * TOK))
    merged = mm(jnp.concatenate(hots, axis=0), fo_ref[...])
    merged = [merged[p * TOK : (p + 1) * TOK] for p in range(4)]
    mhat, minv = norm(merged)
    mgain = mgain_ref[...].reshape(1, 768)
    mgain = [mgain[:, 192 * p : 192 * p + 192] for p in range(4)]
    mnorm = [low(h * g) for h, g in zip(mhat, mgain)]
    mweight = [mw_ref[192 * p : 192 * p + 192] for p in range(4)]
    cin = low(sum(mm(n, w) for n, w in zip(mnorm, mweight))).astype(F32)
    (chat,), cinv = norm([cin])
    cgain = cgain_ref[...].reshape(1, 384)
    xc = low(chat * cgain)
    _, ci, cj = window_index(HALF)
    cot_rows = [None, None]
    for t in range(2):
        for u in range(2):
            lat, lon = ci - 3 * t, cj - 6 * u
            good = (lat >= 0) & (lat < 3) & (lon >= 0) & (lon < 6)
            col = lat * 24 + lon + (6 if u == 0 else 0)
            hot = jnp.concatenate([one_hot(jnp.where(good, col + 12 * half, -1), HALF) for half in range(2)], axis=0)
            for s in range(2):
                part = mm(hot, bufs[s][t][u][216:])
                cot_rows[s] = part if cot_rows[s] is None else cot_rows[s] + part
    cot_rows = [jnp.concatenate([c[:HALF], c[HALF:]], axis=1) for c in cot_rows]
    cot = jnp.concatenate(cot_rows, axis=0)
    gy = low(cot)
    gmix = low(mm_t(gy, cproj_ref[...]))
    for tile in range(3):
        lanes = slice(128 * tile, 128 * tile + 128)
        q_ref[tile] = low(mm(xc, cqkv_ref[:, lanes]) * HEAD**-0.5)
        k_ref[tile] = pad_keys(mm(xc, cqkv_ref[:, 384 + 128 * tile : 512 + 128 * tile]))
        v_ref[tile] = pad_keys(mm(xc, cqkv_ref[:, 768 + 128 * tile : 896 + 128 * tile]))
        gm_ref[tile] = gmix[:, lanes]

    def coarse_tile(tile, carry):
        rows = pl.ds(pl.multiple_of(tile * 4 * TOK, 64), 4 * TOK)

        def bias_grad_to(gs):
            gb_ref[0, 0, rows] = gs[:, :128]
            gb_ref[0, 1, rows] = gs[:, 128:]

        mixed, gq, gk, gv = tile_both(
            q_ref[tile], k_ref[tile], v_ref[tile], gm_ref[tile], load_bias(cbias_ref, 0, rows), bias_grad_to, 4
        )
        mix_ref[tile] = low(mixed)
        g_ref[0, tile] = low(gq * HEAD**-0.5)
        g_ref[1, tile] = low(unpad_keys(gk))
        g_ref[2, tile] = low(unpad_keys(gv))
        return carry

    lax.fori_loop(0, 3, coarse_tile, 0)
    grolled = None
    for tile in range(3):
        for m in range(3):
            wcols = slice(384 * m + 128 * tile, 384 * m + 128 * tile + 128)
            part = mm_t(g_ref[m, tile], cqkv_ref[:, wcols])
            grolled = part if grolled is None else grolled + part
    cin_out[...] = low(cin)
    gy_out[...] = gy
    xc_out[...] = xc
    (gci,), (cgain_grad,) = norm_back([low(grolled).astype(F32)], [cgain], [chat], cinv)
    gci = low(cot + gci)
    gml = []
    gci_out[...] = gci
    for p in range(4):
        mnorm_out[p] = mnorm[p]
        gml.append(low(mm_t(gci, mweight[p])).astype(F32))
    gmerged, mgain_grad = norm_back(gml, mgain, mhat, minv)
    gains_out[...] = gain_rows(list(mgain_grad) + [cgain_grad])
    r48 = iota((48, 1), 0)
    zi = div_const(r48, 24)
    rest = r48 - 24 * zi
    lat_hot = one_hot(zi * HALF + lax.shift_right_logical(rest, 1) * 6 + 4 + (rest & 1), TOK)
    r40 = iota((40, 1), 0)
    zi = jnp.where(r40 >= 18, 1, 0)
    lon_hot = one_hot(jnp.where(r40 < 36, zi * HALF + 54 + r40 - 18 * zi, -1), TOK)
    hot = jnp.concatenate([lat_hot, lon_hot], axis=0)
    for p in range(4):
        g = low(gmerged[p])
        gfo_out[p] = g
        part = low(mm(hot, g))
        latp_out[48 * p : 48 * p + 48] = part[:48]
        lonp_out[40 * p : 40 * p + 40] = part[48:]


def side_kernel(
    cin_ref, gy_ref, xc_ref, mnorm_ref, gci_ref, mix_ref, g_ref, gb_ref, cproj_ref,
    cout_out, pack_out, ctab_out, y_ref, acc_ref,
):
    gy, xc, gci = gy_ref[...], xc_ref[...], gci_ref[...]
    out = None
    for tile in range(3):
        lanes = slice(128 * tile, 128 * tile + 128)
        part = mm(mix_ref[tile], cproj_ref[lanes])
        out = part if out is None else out + part
        dproj = low(t_mm(mix_ref[tile], gy))
        for c in range(3):
            start = 5760 + 384 * c + 128 * tile
            put(pack_out, COARSE, start, dproj[:, 128 * c : 128 * c + 128])
    cout_out[...] = low(cin_ref[...].astype(F32) + low(out).astype(F32))
    for m in range(3):
        dqkv = low(t_mm(xc, jnp.concatenate([g_ref[m, tile] for tile in range(3)], axis=1)))
        for tile in range(3):
            start = 2304 + 384 * (3 * m + tile)
            put(pack_out, COARSE, start, dqkv[:, 128 * tile : 128 * tile + 128])
    for p in range(4):
        dmw = low(t_mm(mnorm_ref[p], gci))
        for c in range(3):
            start = 768 * c + 192 * p
            put(pack_out, COARSE, start, dmw[:, 128 * c : 128 * c + 128])
    ctab_out[...] = jnp.zeros(ctab_out.shape, F32)

    def ctab(t, start, rows):
        ctab_out[:12, start : start + HALF_RUN] = rows

    fold_tables(1, 12, gb_ref, y_ref, acc_ref, ctab)


QUARTERS = ((0, 0), (1, 0), (0, 1), (1, 1))
FINE_PAD = (176, 64, 64, 32)
PIECE = tuple(n + 48 for n in FINE_PAD)


def fine_rows_of(s, t, u):
    r = iota((FINE_PAD[QUARTERS.index((t, u))], 1), 0)
    width, height = 6 if u else 18, 3 if t else 9
    row = div_const(r, width)
    lat, lon = row + 9 * t, r - row * width + 18 * u
    wr, wc = div_const(lat, 6), div_const(lon, 12)
    target = (2 * wr + wc) * TOK + s * HALF + (lon - 12 * wc) * 6 + lat - 6 * wr
    return jnp.where(row < height, target, -1)


def coarse_rows_of(s, t, u):
    r = iota((24, 1), 0)
    row = div_const(r, 6)
    return jnp.where(row < 3, s * HALF + (r - row * 6 + 6 * u) * 6 + row + 3 * t, -1)


def back_kernel(
    x_in, gfo_ref, latp_ref, lonp_ref, corner_ref, bias_ref, fgain_ref, fqkv_ref, fproj_ref, ctab_ref, gains_ref, cout_ref,
    p000, p010, p001, p011, p100, p110, p101, p111, pack_out,
    src_ref, fq_ref, fk_ref, fv_ref, fm_ref, gm_ref, g_ref, gb_ref, y_ref, acc_ref, tab_ref,
):
    src_ref[:576] = gfo_ref[...]
    src_ref[576:768] = latp_ref[...]
    src_ref[768:928] = lonp_ref[...]
    src_ref[928:] = corner_ref[...]
    z, h, w = window_index(TOK)
    hots = []
    for wr in range(2):
        for wc in range(2):
            lat, lon = 6 * wr + h, 12 * wc + w
            behind, before = lat < 3, lon < 6
            lat = jnp.where(behind, lat + 9, lat - 3)
            lon = jnp.where(before, lon + 18, lon - 6)
            p = 2 * (lat & 1) + (lon & 1)
            i, j = lax.shift_right_logical(lat, 1), lax.shift_right_logical(lon, 1)
            own = p * TOK + z * HALF + j * 6 + i
            from_lat = 576 + p * 48 + z * 24 + j * 2 + i - 4
            from_lon = 768 + p * 40 + z * 18 + (j - 9) * 6 + i
            target = jnp.where(before, from_lon + jnp.where(behind, 160, 0), jnp.where(behind, from_lat, own))
            hots.append(one_hot(target, 1088))
    gy = low(mm(jnp.concatenate(hots, axis=0), src_ref[...]))
    gy32 = gy.astype(F32)
    gb_ref[...] = jnp.zeros(gb_ref.shape, F32)
    weights = fine_weights(fqkv_ref)
    gain = fgain_ref[...].reshape(1, 192)
    x = x_in[...].reshape(4 * TOK, 192).astype(F32)
    (hat,), inv = norm([x])
    xn = low(hat * gain)
    fq_ref[...] = low(mm(xn, weights[0]) * HEAD**-0.5).reshape(4, TOK, 192)
    store_keys(fk_ref, mm(xn, weights[1]))
    store_keys(fv_ref, mm(xn, weights[2]))
    gm_ref[...] = low(mm_t(gy, fproj_ref[...])).reshape(4, TOK, 192)

    @pl.loop(0, 4)
    def _(n):
        wr = lax.shift_right_logical(n, 1)
        for start, width, slots in FINE_TILES:
            lanes = slice(start, start + width)

            rows = tile_rows(start, slots)

            def bias_grad_to(gs):
                gb_ref[wr, 0, rows] += gs[:, :128]
                gb_ref[wr, 1, rows] += gs[:, 128:]

            mixed, gq, gk, gv = tile_both(
                fq_ref[n, :, lanes], fk_ref[n, :, lanes], fv_ref[n, :, lanes], gm_ref[n, :, lanes],
                load_bias(bias_ref, wr, rows), bias_grad_to, slots,
            )
            fm_ref[n, :, lanes] = low(mixed)
            g_ref[0, n, :, lanes] = low(gq * HEAD**-0.5)
            g_ref[1, n, :, lanes] = low(unpad_keys(gk))
            g_ref[2, n, :, lanes] = low(unpad_keys(gv))

    dproj = t_mm(fm_ref[...].reshape(4 * TOK, 192), gy)
    grads = [g_ref[m].reshape(4 * TOK, 192) for m in range(3)]
    dqkv = [t_mm(xn, g) for g in grads]
    grolled = sum(mm_t(g, w) for g, w in zip(grads, weights))
    (gx,), (ggain,) = norm_back([low(grolled).astype(F32)], [gain], [hat], inv)
    fg = low(gy32 + gx)
    cout = cout_ref[...]
    for s, outs in enumerate(((p000, p010, p001, p011), (p100, p110, p101, p111))):
        hots, coarse_hots = [], []
        for t, u in QUARTERS:
            hots.append(one_hot(fine_rows_of(s, t, u), 4 * TOK))
            coarse_hots.append(one_hot(coarse_rows_of(s, t, u), TOK))
        fine = low(mm(jnp.concatenate(hots, axis=0), fg))
        coarse = low(mm(jnp.concatenate(coarse_hots, axis=0), cout))
        at = 0
        for n, ((t, u), out) in enumerate(zip(QUARTERS, outs)):
            rows = FINE_PAD[n]
            out[:rows] = fine[at : at + rows]
            out[rows : rows + 24] = coarse[24 * n : 24 * n + 24, :192]
            out[rows + 24 :] = coarse[24 * n : 24 * n + 24, 192:]
            at += rows
    first = low(jnp.concatenate([dqkv[0], dqkv[1]], axis=1))
    second = low(jnp.concatenate([dqkv[2], dproj], axis=1))
    for c in range(3):
        put(pack_out, FINE, 192 * c, first[:, 128 * c : 128 * c + 128], place_of)
        put(pack_out, FINE, 576 + 192 * c, second[:, 128 * c : 128 * c + 128], place_of)
    put(pack_out, FINE, 1152, gain_rows([ggain]), place_of)
    put(pack_out, FINE, 1168, gains_ref[...], place_of)
    put(pack_out, FINE, 1184, jnp.zeros((96, 128), BF), place_of)
    tab_ref[...] = jnp.zeros(tab_ref.shape, F32)
    tab_ref[16:32] = ctab_ref[...]

    def ftab(t, start, rows):
        tab_ref[8 * t : 8 * t + 6, start : start + HALF_RUN] = rows

    fold_tables(2, 6, gb_ref, y_ref, acc_ref, ftab)
    for c in range(13):
        for half in range(2):
            lanes = slice(256 * c + 128 * half, 256 * c + 128 * half + 128)
            pack_out[place_of(c), FINE + 32 * half : FINE + 32 * half + 32] = low(tab_ref[:, lanes])
    for c in range(13, 16):
        pack_out[place_of(c), FINE:] = jnp.zeros((TAB, 128), BF)


def place_kernel(*refs):
    field_out, coarse_out, src_ref = refs[8:]
    base = [sum(PIECE[:n]) for n in range(4)]

    def chosen(later_row, later_col, values):
        near = jnp.where(later_row, values[1], values[0])
        return jnp.where(later_col, jnp.where(later_row, values[3], values[2]), near)

    r = iota((288, 1), 0)
    lat = div_const(r, 24)
    col = r - lat * 24
    later_row, later_col = lat < 3, col < 6
    row = jnp.where(later_row, lat, lat - 3)
    inside = jnp.where(later_col, row * 6 + col, row * 18 + col - 6)
    hots = [one_hot(chosen(later_row, later_col, base) + inside, sum(PIECE))]
    r = iota((HALF, 1), 0)
    lat = div_const(r, 12)
    col = r - lat * 12
    later_row, later_col = lat < 3, col < 6
    inside = jnp.where(later_row, lat, lat - 3) * 6 + jnp.where(later_col, col, col - 6)
    inside = inside + chosen(later_row, later_col, [b + n for b, n in zip(base, FINE_PAD)])
    hots += [one_hot(inside, sum(PIECE)), one_hot(inside + 24, sum(PIECE))]
    hot = jnp.concatenate(hots, axis=0)
    for s in range(2):
        for n in range(4):
            src_ref[base[n] : base[n] + PIECE[n]] = refs[4 * s + n][...]
        out = low(mm(hot, src_ref[...]))
        for h in range(12):
            field_out[1 - s, h] = out[24 * h : 24 * h + 24]
        coarse = jnp.concatenate([out[288:360], out[360:]], axis=1)
        for h in range(6):
            coarse_out[h, :, 1 - s, :] = coarse[12 * h : 12 * h + 12]


def unpack_kernel(fine_scale, coarse_scale, fine_table_scale, coarse_table_scale, mine_ref, other_ref, *outs):
    sums = mine_ref, other_ref, lax.axis_index("lon") % 2
    fgain_out, qkv_out, proj_out, ftab_out, mgain_out, mw_out, cgain_out, cqkv_out, cproj_out, ctab_out = outs
    def coarse_get(start, count):
        return get(sums, COARSE, 0, start, count) * coarse_scale

    def fine_get(start, count, scale):
        return get(sums, FINE, COARSE, start, count) * scale

    for c in range(3):
        lanes = slice(128 * c, 128 * c + 128)
        mw_out[:, lanes] = coarse_get(768 * c, 768)
        cproj_out[:, lanes] = coarse_get(5760 + 384 * c, 384)
        qkv_out[:, lanes] = fine_get(192 * c, 192, fine_scale)
    for c in range(9):
        cqkv_out[:, 128 * c : 128 * c + 128] = coarse_get(2304 + 384 * c, 384)
    second = [fine_get(576 + 192 * c, 192, fine_scale) for c in range(3)]
    qkv_out[:, 384:512] = second[0]
    qkv_out[:, 512:] = second[1][:, :64]
    proj_out[...] = jnp.concatenate([second[1][:, 64:], second[2]], axis=1)
    gains = fine_get(1168, 16, coarse_scale)
    for c in range(6):
        mgain_out[pl.ds(128 * c, 128)] = gains[c]
    for c in range(3):
        cgain_out[pl.ds(128 * c, 128)] = gains[6 + c]
    gains = fine_get(1152, 16, fine_scale)
    fgain_out[pl.ds(0, 128)] = gains[0]
    fgain_out[pl.ds(128, 64)] = gains[1, :64]
    for c in range(13):
        for half in range(2):
            start = 256 * c + 128 * half
            n = min(128, POS - start)
            block = get_chunk(sums, c, slice(GRAIN + 32 * half, GRAIN + 32 * half + 32))[:, :n]
            for t in range(2):
                ftab_out[:, t, start : start + n] = block[8 * t : 8 * t + 6] * fine_table_scale
            ctab_out[:, 0, start : start + n] = block[16:28] * coarse_table_scale


def call(kernel, out_shapes, scratch=(), smem=0, flops=0, moved=0):
    def run(*args):
        specs = [pl.BlockSpec(memory_space=pltpu.SMEM)] * smem
        specs += [pl.BlockSpec(memory_space=pltpu.VMEM)] * (len(args) - smem)
        return pl.pallas_call(
            kernel,
            out_shape=[jax.ShapeDtypeStruct(s, d) for s, d in out_shapes],
            in_specs=specs,
            out_specs=[pl.BlockSpec(memory_space=pltpu.VMEM)] * len(out_shapes),
            scratch_shapes=[pltpu.VMEM(s, d) for s, d in scratch],
            compiler_params=pltpu.CompilerParams(vmem_limit_bytes=VMEM_LIMIT),
            cost_estimate=pl.CostEstimate(flops=flops, bytes_accessed=moved, transcendentals=0),
        )(*args)

    return run


def shifted(x, offset, sign):
    names = [n for n, o in zip(("lon", "lat", "rep"), offset[::-1]) if o]
    sizes = [lax.axis_size(n) for n in names]
    pairs = []
    for place in np.ndindex(*sizes):
        target = [(p - sign) % s for p, s in zip(place, sizes)]
        pairs.append((int(np.ravel_multi_index(place, sizes)), int(np.ravel_multi_index(target, sizes))))
    return lax.ppermute(x, tuple(names), pairs)


CORNERS = [(s, t, u) for s in range(2) for t in range(2) for u in range(2)]


def exchange(x, axes):
    return lax.all_to_all(lax.optimization_barrier(x), axes, 0, 0, tiled=True)


def summed(x):
    return jnp.sum(x.astype(F32), axis=0, keepdims=True).astype(BF)


def spread(x, count):
    return jnp.broadcast_to(x, (count,) + x.shape[1:])


def sibling(x):
    return lax.ppermute(x, "lon", [(i, i ^ 1) for i in range(lax.axis_size("lon"))])


def exchange_columns(x):
    size = lax.axis_size("lon")
    groups = [list(range(core, size, 2)) for core in range(2)]
    return lax.all_to_all(lax.optimization_barrier(x), "lon", 0, 0, axis_index_groups=groups, tiled=True)


def reduce_coarse(coarse):
    core = lax.axis_index("lon") % 2
    keep, send = (lax.dynamic_slice_in_dim(coarse, 8 * c, 8) for c in (core, 1 - core))
    both = (keep.astype(F32) + sibling(send).astype(F32)).astype(BF)
    return exchange_columns(both)


def reduce_everywhere(got, pack, beside):
    rest = lax.axis_size("lat") * lax.axis_size("rep")
    got, pack = lax.optimization_barrier((got, pack))
    pack, beside = lax.optimization_barrier((exchange(pack, "lon"), beside))
    got, pack = summed(got), summed(pack)
    part = jnp.concatenate([got, pack[:, :FINE]], axis=1).reshape(rest, -1, 128)
    part = summed(exchange(part, ("lat", "rep")))
    part = exchange(spread(part, rest), ("lat", "rep")).reshape(1, GRAIN, 128)
    mine = jnp.concatenate([part, pack[:, FINE:]], axis=1)
    mine = exchange_columns(spread(mine, lax.axis_size("lon") // 2))
    return (mine, sibling(mine)), beside


def body(
    fine_field, fine_gain, fine_qkv, fine_proj, fine_table, merge_gain, merge_weight,
    coarse_gain, coarse_qkv, coarse_proj, coarse_table, cotangent,
):
    rep, lat, lon = (lax.axis_size(n) for n in ("rep", "lat", "lon"))
    packs = call(pack_kernel, [((288, 192), BF)] * 4)(fine_field, cotangent.transpose(1, 2, 0, 3))
    bufs = []
    for s, t, u in CORNERS:
        b = packs[2 * s + t]
        bufs.append(shifted(b, (s, t, u), 1) if s + t + u else b)
    table = fine_table[0].transpose(1, 0, 2)
    bias, cbias = call(
        bias_kernel,
        [((3, 2, 6 * TOK, 128), F32), ((1, 2, 12 * TOK, 128), F32)],
        [((2, 30 * 32, 128), F32)],
        flops=1 << 32,
    )(table, shifted(fine_table, (0, 1, 0), 1)[0].transpose(1, 0, 2), coarse_table[0].transpose(1, 0, 2))
    x, gfo, latp, lonp, *coarse, cgains = call(
        main_kernel,
        [
            ((4, TOK, 192), BF), ((4, TOK, 192), BF), ((192, 192), BF), ((160, 192), BF),
            ((TOK, 384), BF), ((TOK, 384), BF), ((TOK, 384), BF), ((4, TOK, 192), BF), ((TOK, 384), BF),
            ((3, TOK, 128), BF), ((3, 3, TOK, 128), BF), ((1, 2, 12 * TOK, 128), F32), ((16, 128), BF),
        ],
        [
            ((9, TOK, 192), F32), ((9 * TOK, 192), BF),
            ((9, TOK, 192), BF), ((9, LANES, 192), BF), ((9, LANES, 192), BF), ((9, TOK, 192), BF),
            ((3, TOK, 128), BF), ((3, LANES, 128), BF), ((3, LANES, 128), BF), ((3, TOK, 128), BF),
        ],
        flops=1 << 34,
    )(
        *bufs, bias, cbias, fine_gain, fine_qkv, fine_proj, merge_gain,
        merge_weight, coarse_gain, coarse_qkv, coarse_proj,
    )
    lat_recv = shifted(latp, (0, 1, 0), -1)
    lon_recv = shifted(lonp, (0, 0, 1), -1)
    corner_recv = shifted(lonp, (0, 1, 1), -1)
    cout, cpack, ctab = call(
        side_kernel,
        [((TOK, 384), BF), ((16, COARSE, 128), BF), ((16, WIDE), F32)],
        [((384, 256), F32), ((2, 384, 128), F32)],
        flops=1 << 32,
    )(*coarse, coarse_proj)
    got = reduce_coarse(cpack)
    *pieces, pack = call(
        back_kernel,
        [((n, 192), BF) for n in PIECE + PIECE] + [((16, FINE + TAB, 128), BF)],
        [
            ((1088, 192), BF), ((4, TOK, 192), BF), ((4, LANES, 192), BF), ((4, LANES, 192), BF),
            ((4, TOK, 192), BF), ((4, TOK, 192), BF), ((3, 4, TOK, 192), BF),
            ((2, 2, 6 * TOK, 128), F32), ((192, 256), F32), ((2, 192, 128), F32), ((32, WIDE), F32),
        ],
        flops=1 << 33,
    )(x, gfo.reshape(4 * TOK, 192), lat_recv, lon_recv, corner_recv, bias, fine_gain, fine_qkv, fine_proj, ctab, cgains, cout)
    places = [(s, t, u) for s in range(2) for t, u in QUARTERS]
    pieces = [shifted(b, place, -1) if any(place) else b for b, place in zip(pieces, places)]
    sums, pieces = reduce_everywhere(got, pack, pieces)
    field_grad, coarse_out = call(
        place_kernel, [((2, 12, 24, 192), BF), ((6, 12, 2, 384), BF)], [((sum(PIECE), 192), BF)]
    )(*pieces)
    levels, rows, cols = 2 * rep, 12 * lat, 24 * lon
    fine_scale = (levels * rows * cols) ** -0.5
    coarse_scale = (levels * rows * cols // 4) ** -0.5
    fine_table_scale = (cols // 12) ** -0.5
    coarse_table_scale = (cols // 24) ** -0.5
    fgain_g, fqkv_g, fproj_g, ftab_g, mgain_g, mw_g, cgain_g, cqkv_g, cproj_g, ctab_g = call(
        lambda *refs: unpack_kernel(fine_scale, coarse_scale, fine_table_scale, coarse_table_scale, *refs),
        [
            ((192,), F32), ((192, 576), F32), ((192, 192), F32), ((6, 2, POS), F32), ((768,), F32),
            ((768, 384), F32), ((384,), F32), ((384, 1152), F32), ((384, 384), F32), ((12, 1, POS), F32),
        ],
    )(*sums)
    return (
        coarse_out.transpose(2, 0, 1, 3), field_grad, fgain_g, fqkv_g, fproj_g, ftab_g.transpose(1, 0, 2)[None],
        mgain_g, mw_g, cgain_g, cqkv_g, cproj_g, ctab_g.transpose(1, 0, 2)[None],
    )


def solution(mesh):
    tokens, tables = P("rep", "lat", "lon", None), P("rep", "lat", None, None)
    return jax.shard_map(
        body,
        mesh=mesh,
        in_specs=(tokens, P(), P(), P(), tables, P(), P(), P(), P(), P(), tables, tokens),
        out_specs=(tokens, tokens, P(), P(), P(), tables, P(), P(), P(), P(), P(), tables),
        check_vma=False,
    )
```

time: 540 us -> 162 us (0.30); the launches traced: 533 us -> 162 us
  waiting for transfers between devices: 387 us -> 13.8 us
  blocking collectives: 0 us -> 31.6 us
  Pallas kernels: 75.1 us -> 51 us
  starting transfers between devices: 37.3 us -> 58.6 us
  between operations: 14.8 us -> 0.95 us
  local copies, waits for them, and re-layouts: 16.4 us -> 4.03 us
    psum x2 -> x0, waiting for transfers between devices: 372 us -> none  [total(): return lax.psum(x, axes)]
    all_to_all x0 -> x2, blocking collectives: none -> 31.6 us  [the longest x1 17.8 us: exchange_columns(): lax.all_to_all(lax.optimization_barrier(x), 'lon', 0, 0, axis_index_group...]
    pallas_call x8 -> x7, Pallas kernels: 75.1 us -> 51 us  [run(): pl.pallas_call(kernel, out_shape=[jax.ShapeDtypeStruct(s, d) for s, d in...]
    all_to_all x0 -> x3, starting transfers between devices: none -> 17.5 us  [the longest x2 11.7 us: exchange(): return lax.all_to_all(lax.optimization_barrier(x), axes, 0, 0, tiled=True)]
    ppermute x25 -> x18, waiting for transfers between devices: 14 us -> 4.1 us  [shifted(): return lax.ppermute(x, tuple(names), pairs)]
    unnamed x62 -> x36, local copies, waits for them, and re-layouts: 10.5 us -> 1.84 us
    all_to_all x0 -> x3, waiting for transfers between devices: none -> 8.5 us  [the longest x2 8.5 us: exchange(): return lax.all_to_all(lax.optimization_barrier(x), axes, 0, 0, tiled=True)]
    ppermute x0 -> x2, starting transfers between devices: none -> 7.17 us  [sibling(): lax.ppermute(x, 'lon', [(i, i ^ 1) for i in range(lax.axis_size('lon'))])]
  transfers between devices with their start and end apart: 27 -> 23, of which waited for: 9 -> 6; matrix products, arithmetic and copies ran while one was open for 2% -> 1% of each run, Pallas kernels for 2% -> 15%
where the time goes in v2:
time: 162 us
  starting transfers between devices  58.6 us (36%)
  Pallas kernels  51 us (31%)
  blocking collectives  31.6 us (20%)
  waiting for transfers between devices  13.8 us (9%)
  local copies, waits for them, and re-layouts  4.03 us (2%)
    pallas_call x7, Pallas kernels, run(): pl.pallas_call(kernel, out_shape=[jax.ShapeDtypeStruct(s, d) for s, d in...  51 us
    ppermute x18, starting transfers between devices, shifted(): return lax.ppermute(x, tuple(names), pairs)  34 us
    all_to_all x1, blocking collectives, exchange_columns(): lax.all_to_all(lax.optimization_barrier(x), 'lon', 0, 0, axis_index_group...  17.8 us
    all_to_all x1, blocking collectives, exchange(): return lax.all_to_all(lax.optimization_barrier(x), axes, 0, 0, tiled=True)  13.9 us
    all_to_all x2, starting transfers between devices, exchange(): return lax.all_to_all(lax.optimization_barrier(x), axes, 0, 0, tiled=True)  11.7 us
    all_to_all x2, waiting for transfers between devices, exchange(): return lax.all_to_all(lax.optimization_barrier(x), axes, 0, 0, tiled=True)  8.5 us
    ppermute x2, starting transfers between devices, sibling(): lax.ppermute(x, 'lon', [(i, i ^ 1) for i in range(lax.axis_size('lon'))])  7.17 us
    all_to_all x1, starting transfers between devices, exchange_columns(): lax.all_to_all(lax.optimization_barrier(x), 'lon', 0, 0, axis_index_group...  5.85 us
  transfers between devices with their start and end apart: 23, of which 6 were waited for; matrix products, arithmetic and copies ran while one was open for 1% of the time, Pallas kernels for 15%

profile of v2, /device:TPU:1, one launch (start us, length us, event | category | flops | bytes accessed | tf_op | source)
XLA Modules:
  0.0 161.5 jit_solution(12232999231837489718)
XLA Ops:
  0.6 6.5 %collective-permute-start.7 = (f32[1,2,6,3312]{3,1,2,0:T(2,128)}, f32[1,2,6,3312]{3,1,2,0:T(2,128)S(1)}, u32[]{:S(2)}, u32[]{:S(2)}) collective-permute-start(f32[1,2,6,3312]{3,1,2,0:T(2,128)} %param.16), channel_id=1, source_target_pairs={{0,14},{2,0},{4,2},{6,4},{8,6},{10,8},{12,10},{14,12},{1,15},{3,1}... | collective-permute-start | bytes 476936 | tf_op jit(solution)/shard_map/ppermute | solution.py:715
  7.1 1.9 %shard_map.211 = (bf16[288,192]{1,0:T(8,128)(2,1)}, bf16[288,192]{1,0:T(8,128)(2,1)}, bf16[288,192]{1,0:T(8,128)(2,1)}, bf16[288,192]{1,0:T(8,128)(2,1)}) custom-call(bf16[2,12,24,192]{3,2,1,0:T(8,128)(2,1)} %field_ref.1, bf16[6,12,2,384]{3,2,1,0:T(2,128)(2,1)} %bitcast.27), custom_call_target="tpu_custom_call" | custom-call | tf_op jit(solution)/shard_map/pallas_call | solution.py:695
  10.7 5.5 %collective-permute-start.2 = (bf16[288,192]{1,0:T(8,128)(2,1)}, bf16[288,192]{1,0:T(8,128)(2,1)S(1)}, u32[]{:S(2)}, u32[]{:S(2)}) collective-permute-start(bf16[288,192]{1,0:T(8,128)(2,1)} %get-tuple-element.67), channel_id=1, source_target_pairs={{0,254},{2,240},{4,242},{6,244},{8,246},{10,248},{12,250},{14,252}... | collective-permute-start | bytes 331784 | tf_op jit(solution)/shard_map/ppermute | solution.py:715
  16.6 1.8 %collective-permute-start.4 = (bf16[288,192]{1,0:T(8,128)(2,1)}, bf16[288,192]{1,0:T(8,128)(2,1)S(1)}, u32[]{:S(2)}, u32[]{:S(2)}) collective-permute-start(bf16[288,192]{1,0:T(8,128)(2,1)} %get-tuple-element.68), channel_id=1, source_target_pairs={{0,241},{1,240},{16,1},{17,0},{32,17},{33,16},{48,33},{49,32},{64,... | collective-permute-start | bytes 331784 | tf_op jit(solution)/shard_map/ppermute | solution.py:715
  19.4 5.9 %collective-permute-start.6 = (bf16[288,192]{1,0:T(8,128)(2,1)}, bf16[288,192]{1,0:T(8,128)(2,1)S(1)}, u32[]{:S(2)}, u32[]{:S(2)}) collective-permute-start(bf16[288,192]{1,0:T(8,128)(2,1)} %get-tuple-element.69), channel_id=1, source_target_pairs={{0,255},{1,254},{2,241},{3,240},{4,243},{5,242},{6,245},{7,244},{8... | collective-permute-start | bytes 331784 | tf_op jit(solution)/shard_map/ppermute | solution.py:715
  25.3 6.3 %shard_map.212 = (f32[3,2,864,128]{3,2,1,0:T(8,128)}, f32[1,2,1728,128]{3,2,1,0:T(8,128)}) custom-call(f32[6,2,3312]{2,1,0:T(2,128)} %bitcast.28, f32[6,2,3312]{2,1,0:T(2,128)} %bitcast.30, f32[12,1,3312]{2,1,0:T(1,128)} %bitcast.29), custom_call_target="tpu_custom_call" | custom-call | flops 4294967296 | tf_op jit(solution)/shard_map/pallas_call | solution.py:695
  32.4 18.0 %shard_map.213 = (bf16[4,144,192]{2,1,0:T(8,128)(2,1)}, bf16[4,144,192]{2,1,0:T(8,128)(2,1)}, bf16[192,192]{1,0:T(8,128)(2,1)}, bf16[160,192]{1,0:T(8,128)(2,1)}...) custom-call(bf16[288,192]{1,0:T(8,128)(2,1)} %get-tuple-element.66.b, ...), custom_call_target="tpu_custom_call" | custom-call | flops 17179869184 | tf_op jit(solution)/shard_map/pallas_call | solution.py:695
  50.5 5.1 %shard_map.214 = (bf16[144,384]{1,0:T(8,128)(2,1)}, bf16[16,432,128]{2,1,0:T(8,128)(2,1)}, f32[16,3328]{1,0:T(8,128)}) custom-call(bf16[144,384]{1,0:T(8,128)(2,1)} %get-tuple-element.72.cin_ref, bf16[144,384]{1,0:T(8,128)(2,1)} %get-tuple-element.73.gy_ref, bf16[144,384]{1,0:T(8,128)(2,1)} %get-tuple-element.74.xc_ref, ...), custom_call_target="tpu_custom_call" | custom-call | flops 4294967296 | tf_op jit(solution)/shard_map/pallas_call | solution.py:695
  60.5 5.8 %all-to-all-start = ((bf16[8,432,128]{2,1,0:T(8,128)(2,1)}), bf16[8,432,128]{2,1,0:T(8,128)(2,1)S(1)}, u32[]{:S(2)}, u32[]{:S(2)}) async-start(bf16[8,432,128]{2,1,0:T(8,128)(2,1)} %add_convert_fusion), calls=%async_computation | async-start | bytes 1769472 | tf_op jit(solution)/shard_map/all_to_all | solution.py:740
  66.4 13.4 %shard_map.215 = (bf16[224,192]{1,0:T(8,128)(2,1)}, bf16[112,192]{1,0:T(8,128)(2,1)}, bf16[112,192]{1,0:T(8,128)(2,1)}, bf16[80,192]{1,0:T(8,128)(2,1)}, bf16[22...) custom-call(bf16[4,144,192]{2,1,0:T(8,128)(2,1)} %get-tuple-element., ...), custom_call_target="tpu_custom_call" | custom-call | flops 8589934592 | tf_op jit(solution)/shard_map/pallas_call | solution.py:695
  79.8 8.1 %all-to-all-start.1 = ((bf16[16,144,128]{2,1,0:T(8,128)(2,1)}), bf16[16,144,128]{2,1,0:T(8,128)(2,1)S(1)}, u32[]{:S(2)}, u32[]{:S(2)}) async-start(bf16[16,144,128]{2,1,0:T(8,128)(2,1)} %get-tuple-element.89), calls=%async_computation.1 | async-start | bytes 1179648 | tf_op jit(solution)/shard_map/all_to_all | solution.py:722
  87.9 1.6 collective-permute-start.14
  89.6 2.1 %collective-permute-start.18 = (bf16[80,192]{1,0:T(8,128)(2,1)}, bf16[80,192]{1,0:T(8,128)(2,1)S(1)}, u32[]{:S(2)}, u32[]{:S(2)}) collective-permute-start(bf16[80,192]{1,0:T(8,128)(2,1)} %get-tuple-element.97), channel_id=1, source_target_pairs={{0,19},{1,18},{2,21},{3,20},{4,23},{5,22},{6,25},{7,24},{8,27},{9,... | collective-permute-start | bytes 92168 | tf_op jit(solution)/shard_map/ppermute | solution.py:715
  93.0 2.0 %collective-permute-start.13 = (bf16[112,192]{1,0:T(8,128)(2,1)}, bf16[112,192]{1,0:T(8,128)(2,1)S(1)}, u32[]{:S(2)}, u32[]{:S(2)}) collective-permute-start(bf16[112,192]{1,0:T(8,128)(2,1)} %get-tuple-element.92), channel_id=1, source_target_pairs={{0,16},{16,32},{32,48},{48,64},{64,80},{80,96},{96,112},{112,128},... | collective-permute-start | bytes 129032 | tf_op jit(solution)/shard_map/ppermute | solution.py:715
  96.0 2.0 %collective-permute-start.17 = (bf16[112,192]{1,0:T(8,128)(2,1)}, bf16[112,192]{1,0:T(8,128)(2,1)S(1)}, u32[]{:S(2)}, u32[]{:S(2)}) collective-permute-start(bf16[112,192]{1,0:T(8,128)(2,1)} %get-tuple-element.96), channel_id=1, source_target_pairs={{0,17},{1,16},{16,33},{17,32},{32,49},{33,48},{48,65},{49,64},{64,... | collective-permute-start | bytes 129032 | tf_op jit(solution)/shard_map/ppermute | solution.py:715
  98.2 2.1 %collective-permute-done.16.refs_5_ = bf16[112,192]{1,0:T(8,128)(2,1)S(1)} collective-permute-done((bf16[112,192]{1,0:T(8,128)(2,1)}, bf16[112,192]{1,0:T(8,128)(2,1)S(1)}, u32[]{:S(2)}, u32[]{:S(2)}) %collective-permute-start.16) | collective-permute-done | bytes 43040 | tf_op jit(solution)/shard_map/ppermute | solution.py:715
  100.3 1.9 %collective-permute-done.17.refs_6_ = bf16[112,192]{1,0:T(8,128)(2,1)S(1)} collective-permute-done((bf16[112,192]{1,0:T(8,128)(2,1)}, bf16[112,192]{1,0:T(8,128)(2,1)S(1)}, u32[]{:S(2)}, u32[]{:S(2)}) %collective-permute-start.17) | collective-permute-done | bytes 43040 | tf_op jit(solution)/shard_map/ppermute | solution.py:715
  102.4 13.9 %all_to_all.25 = bf16[16,32,128]{2,1,0:T(8,128)(2,1)S(1)} all-to-all(bf16[16,32,128]{2,1,0:T(8,128)(2,1)S(1)} %bitcast.23), channel_id=1, replica_groups=mesh['lon'=16,'lat'=8,'rep'=2] {'lat','rep'}, dimensions={0} | all-to-all | bytes 262144 | tf_op jit(solution)/shard_map/all_to_all | solution.py:722
  116.9 3.5 %all-to-all-start.3 = ((bf16[16,32,128]{2,1,0:T(8,128)(2,1)}), bf16[16,32,128]{2,1,0:T(8,128)(2,1)S(1)}, u32[]{:S(2)}, u32[]{:S(2)}) async-start(bf16[16,32,128]{2,1,0:T(8,128)(2,1)} %broadcast_in_dim.8), calls=%async_computation.3 | async-start | bytes 262144 | tf_op jit(solution)/shard_map/all_to_all | solution.py:722
  120.5 8.5 %all-to-all-done.3 = bf16[16,32,128]{2,1,0:T(8,128)(2,1)S(1)} async-done(((bf16[16,32,128]{2,1,0:T(8,128)(2,1)}), bf16[16,32,128]{2,1,0:T(8,128)(2,1)S(1)}, u32[]{:S(2)}, u32[]{:S(2)}) %all-to-all-start.3) | async-done | bytes 131104 | tf_op jit(solution)/shard_map/all_to_all | solution.py:722
  129.1 17.8 %all_to_all.26.refs_0_ = bf16[8,576,128]{2,1,0:T(8,128)(2,1)S(1)} all-to-all(bf16[8,576,128]{2,1,0:T(8,128)(2,1)S(1)} %broadcast_in_dim.20), channel_id=1, replica_groups={{0,32,64,96,128,160,192,224},{16,48,80,112,144,176,208,240},{1,33,65,97..., dimensions={0} | all-to-all | bytes 2359296 | tf_op jit(solution)/shard_map/all_to_all | solution.py:740
  147.0 7.1 %collective-permute-start.19 = (bf16[8,576,128]{2,1,0:T(8,128)(2,1)S(1)}, bf16[8,576,128]{2,1,0:T(8,128)(2,1)S(1)}, u32[]{:S(2)}, u32[]{:S(2)}) collective-permute-start(bf16[8,576,128]{2,1,0:T(8,128)(2,1)S(1)} %all_to_all.26.refs_0_), channel_id=1, source_target_pairs={{0,16},{16,0},{32,48},{48,32},{64,80},{80,64},{96,112},{112,96},{1... | collective-permute-start | bytes 3538952 | tf_op jit(solution)/shard_map/ppermute | solution.py:734
  154.0 2.4 %shard_map.216 = (bf16[2,12,24,192]{3,2,1,0:T(8,128)(2,1)}, bf16[6,12,2,384]{3,2,1,0:T(2,128)(2,1)}) custom-call(bf16[224,192]{1,0:T(8,128)(2,1)} %get-tuple-element.98.refs_0_, bf16[112,192]{1,0:T(8,128)(2,1)} %copy-done.4, bf16[112,192]{1,0:T(8,128)(2,1)} %copy-done.5, bf16[80,192]{1,0:T(8,128)(2,1)} %copy-done.8, bf16[224,192]{1,0:T(8,128)(2,1)} %copy-done.3, ...), custom_call_target="tpu_custom_call" | custom-call | tf_op jit(solution)/shard_map/pallas_call | solution.py:695
  157.5 4.0 %shard_map.217 = (f32[192]{0:T(256)}, f32[192,576]{1,0:T(8,128)}, f32[192,192]{1,0:T(8,128)}, f32[6,2,3312]{2,1,0:T(2,128)}, f32[768]{0:T(1024)}, /*index=5*/f32...) custom-call(bf16[8,576,128]{2,1,0:T(8,128)(2,1)} %copy-done, ...), custom_call_target="tpu_custom_call" | custom-call | tf_op jit(solution)/shard_map/pallas_call | solution.py:695
  (78 shorter events, 13.4 us)
Async XLA Ops:
  0.6 18.8 %collective-permute-start.7 = (f32[1,2,6,3312]{3,1,2,0:T(2,128)}, f32[1,2,6,3312]{3,1,2,0:T(2,128)S(1)}, u32[]{:S(2)}, u32[]{:S(2)}) collective-permute-start(f32[1,2,6,3312]{3,1,2,0:T(2,128)} %param.16), channel_id=1, source_target_pairs={{0,14},{2,0},{4,2},{6,4},{8,6},{10,8},{12,10},{14,12},{1,15},{3,1}... | collective-permute-start | bytes 476936 | tf_op jit(solution)/shard_map/ppermute | solution.py:715
  9.0 7.5 %collective-permute-start = (bf16[288,192]{1,0:T(8,128)(2,1)}, bf16[288,192]{1,0:T(8,128)(2,1)S(1)}, u32[]{:S(2)}, u32[]{:S(2)}) collective-permute-start(bf16[288,192]{1,0:T(8,128)(2,1)} %get-tuple-element.66.b000), channel_id=1, source_target_pairs={{0,240},{16,0},{32,16},{48,32},{64,48},{80,64},{96,80},{112,96},{1... | collective-permute-start | bytes 331784 | tf_op jit(solution)/shard_map/ppermute | solution.py:715
  10.0 8.4 %collective-permute-start.1 = (bf16[288,192]{1,0:T(8,128)(2,1)}, bf16[288,192]{1,0:T(8,128)(2,1)S(1)}, u32[]{:S(2)}, u32[]{:S(2)}) collective-permute-start(bf16[288,192]{1,0:T(8,128)(2,1)} %get-tuple-element.67), channel_id=1, source_target_pairs={{0,14},{2,0},{4,2},{6,4},{8,6},{10,8},{12,10},{14,12},{1,15},{3,1}... | collective-permute-start | bytes 331784 | tf_op jit(solution)/shard_map/ppermute | solution.py:715
  10.7 20.8 %collective-permute-start.2 = (bf16[288,192]{1,0:T(8,128)(2,1)}, bf16[288,192]{1,0:T(8,128)(2,1)S(1)}, u32[]{:S(2)}, u32[]{:S(2)}) collective-permute-start(bf16[288,192]{1,0:T(8,128)(2,1)} %get-tuple-element.67), channel_id=1, source_target_pairs={{0,254},{2,240},{4,242},{6,244},{8,246},{10,248},{12,250},{14,252}... | collective-permute-start | bytes 331784 | tf_op jit(solution)/shard_map/ppermute | solution.py:715
  16.2 15.3 %collective-permute-start.3 = (bf16[288,192]{1,0:T(8,128)(2,1)}, bf16[288,192]{1,0:T(8,128)(2,1)S(1)}, u32[]{:S(2)}, u32[]{:S(2)}) collective-permute-start(bf16[288,192]{1,0:T(8,128)(2,1)} %get-tuple-element.68), channel_id=1, source_target_pairs={{0,1},{1,0},{2,3},{3,2},{4,5},{5,4},{6,7},{7,6},{8,9},{9,8},{10,11... | collective-permute-start | bytes 331784 | tf_op jit(solution)/shard_map/ppermute | solution.py:715
  16.6 15.0 %collective-permute-start.4 = (bf16[288,192]{1,0:T(8,128)(2,1)}, bf16[288,192]{1,0:T(8,128)(2,1)S(1)}, u32[]{:S(2)}, u32[]{:S(2)}) collective-permute-start(bf16[288,192]{1,0:T(8,128)(2,1)} %get-tuple-element.68), channel_id=1, source_target_pairs={{0,241},{1,240},{16,1},{17,0},{32,17},{33,16},{48,33},{49,32},{64,... | collective-permute-start | bytes 331784 | tf_op jit(solution)/shard_map/ppermute | solution.py:715
  18.4 13.2 %collective-permute-start.5 = (bf16[288,192]{1,0:T(8,128)(2,1)}, bf16[288,192]{1,0:T(8,128)(2,1)S(1)}, u32[]{:S(2)}, u32[]{:S(2)}) collective-permute-start(bf16[288,192]{1,0:T(8,128)(2,1)} %get-tuple-element.69), channel_id=1, source_target_pairs={{0,15},{1,14},{2,1},{3,0},{4,3},{5,2},{6,5},{7,4},{8,7},{9,6},{10,... | collective-permute-start | bytes 331784 | tf_op jit(solution)/shard_map/ppermute | solution.py:715
  19.4 12.2 %collective-permute-start.6 = (bf16[288,192]{1,0:T(8,128)(2,1)}, bf16[288,192]{1,0:T(8,128)(2,1)S(1)}, u32[]{:S(2)}, u32[]{:S(2)}) collective-permute-start(bf16[288,192]{1,0:T(8,128)(2,1)} %get-tuple-element.69), channel_id=1, source_target_pairs={{0,255},{1,254},{2,241},{3,240},{4,243},{5,242},{6,245},{7,244},{8... | collective-permute-start | bytes 331784 | tf_op jit(solution)/shard_map/ppermute | solution.py:715
  56.9 2.5 %collective-permute-start.8 = (bf16[8,432,128]{2,1,0:T(8,128)(2,1)S(1)}, bf16[8,432,128]{2,1,0:T(8,128)(2,1)S(1)}, u32[]{:S(2)}, u32[]{:S(2)}) collective-permute-start(bf16[8,432,128]{2,1,0:T(8,128)(2,1)S(1)} %constant_dynamic-slice_fusion), channel_id=1, source_target_pairs={{0,16},{16,0},{32,48},{48,32},{64,80},{80,64},{96,112},{112,96},{1... | collective-permute-start | bytes 2654216 | tf_op jit(solution)/shard_map/ppermute | solution.py:734
  57.0 9.4 %collective-permute-start.10 = (bf16[160,192]{1,0:T(8,128)(2,1)}, bf16[160,192]{1,0:T(8,128)(2,1)}, u32[]{:S(2)}, u32[]{:S(2)}) collective-permute-start(bf16[160,192]{1,0:T(8,128)(2,1)} %get-tuple-element.84), channel_id=1, source_target_pairs={{0,16},{16,32},{32,48},{48,64},{64,80},{80,96},{96,112},{112,128},... | collective-permute-start | bytes 184328 | tf_op jit(solution)/shard_map/ppermute | solution.py:715
  57.3 9.1 %collective-permute-start.11 = (bf16[160,192]{1,0:T(8,128)(2,1)}, bf16[160,192]{1,0:T(8,128)(2,1)}, u32[]{:S(2)}, u32[]{:S(2)}) collective-permute-start(bf16[160,192]{1,0:T(8,128)(2,1)} %get-tuple-element.84), channel_id=1, source_target_pairs={{0,18},{2,20},{4,22},{6,24},{8,26},{10,28},{12,30},{14,16},{16,34}... | collective-permute-start | bytes 184328 | tf_op jit(solution)/shard_map/ppermute | solution.py:715
  57.4 9.0 %collective-permute-start.9 = (bf16[192,192]{1,0:T(8,128)(2,1)}, bf16[192,192]{1,0:T(8,128)(2,1)}, u32[]{:S(2)}, u32[]{:S(2)}) collective-permute-start(bf16[192,192]{1,0:T(8,128)(2,1)} %get-tuple-element.83), channel_id=1, source_target_pairs={{0,2},{2,4},{4,6},{6,8},{8,10},{10,12},{12,14},{14,0},{1,3},{3,5},... | collective-permute-start | bytes 221192 | tf_op jit(solution)/shard_map/ppermute | solution.py:715
  60.5 19.2 %all-to-all-start = ((bf16[8,432,128]{2,1,0:T(8,128)(2,1)}), bf16[8,432,128]{2,1,0:T(8,128)(2,1)S(1)}, u32[]{:S(2)}, u32[]{:S(2)}) async-start(bf16[8,432,128]{2,1,0:T(8,128)(2,1)} %add_convert_fusion), calls=%async_computation | async-start | bytes 1769472 | tf_op jit(solution)/shard_map/all_to_all | solution.py:740
  79.8 22.4 %all-to-all-start.1 = ((bf16[16,144,128]{2,1,0:T(8,128)(2,1)}), bf16[16,144,128]{2,1,0:T(8,128)(2,1)S(1)}, u32[]{:S(2)}, u32[]{:S(2)}) async-start(bf16[16,144,128]{2,1,0:T(8,128)(2,1)} %get-tuple-element.89), calls=%async_computation.1 | async-start | bytes 1179648 | tf_op jit(solution)/shard_map/all_to_all | solution.py:722
  87.9 14.3 %collective-permute-start.15 = (bf16[224,192]{1,0:T(8,128)(2,1)}, bf16[224,192]{1,0:T(8,128)(2,1)S(1)}, u32[]{:S(2)}, u32[]{:S(2)}) collective-permute-start(bf16[224,192]{1,0:T(8,128)(2,1)} %get-tuple-element.94), channel_id=1, source_target_pairs={{0,1},{1,0},{2,3},{3,2},{4,5},{5,4},{6,7},{7,6},{8,9},{9,8},{10,11... | collective-permute-start | bytes 258056 | tf_op jit(solution)/shard_map/ppermute | solution.py:715
  87.9 7.0 %collective-permute-start.14 = (bf16[80,192]{1,0:T(8,128)(2,1)}, bf16[80,192]{1,0:T(8,128)(2,1)S(1)}, u32[]{:S(2)}, u32[]{:S(2)}) collective-permute-start(bf16[80,192]{1,0:T(8,128)(2,1)} %get-tuple-element.93), channel_id=1, source_target_pairs={{0,18},{2,20},{4,22},{6,24},{8,26},{10,28},{12,30},{14,16},{16,34}... | collective-permute-start | bytes 92168 | tf_op jit(solution)/shard_map/ppermute | solution.py:715
  89.6 6.5 %collective-permute-start.18 = (bf16[80,192]{1,0:T(8,128)(2,1)}, bf16[80,192]{1,0:T(8,128)(2,1)S(1)}, u32[]{:S(2)}, u32[]{:S(2)}) collective-permute-start(bf16[80,192]{1,0:T(8,128)(2,1)} %get-tuple-element.97), channel_id=1, source_target_pairs={{0,19},{1,18},{2,21},{3,20},{4,23},{5,22},{6,25},{7,24},{8,27},{9,... | collective-permute-start | bytes 92168 | tf_op jit(solution)/shard_map/ppermute | solution.py:715
  91.7 6.5 %collective-permute-start.12 = (bf16[112,192]{1,0:T(8,128)(2,1)}, bf16[112,192]{1,0:T(8,128)(2,1)S(1)}, u32[]{:S(2)}, u32[]{:S(2)}) collective-permute-start(bf16[112,192]{1,0:T(8,128)(2,1)} %get-tuple-element.91), channel_id=1, source_target_pairs={{0,2},{2,4},{4,6},{6,8},{8,10},{10,12},{12,14},{14,0},{1,3},{3,5},... | collective-permute-start | bytes 129032 | tf_op jit(solution)/shard_map/ppermute | solution.py:715
  93.0 5.2 %collective-permute-start.13 = (bf16[112,192]{1,0:T(8,128)(2,1)}, bf16[112,192]{1,0:T(8,128)(2,1)S(1)}, u32[]{:S(2)}, u32[]{:S(2)}) collective-permute-start(bf16[112,192]{1,0:T(8,128)(2,1)} %get-tuple-element.92), channel_id=1, source_target_pairs={{0,16},{16,32},{32,48},{48,64},{64,80},{80,96},{96,112},{112,128},... | collective-permute-start | bytes 129032 | tf_op jit(solution)/shard_map/ppermute | solution.py:715
  95.0 5.4 %collective-permute-start.16 = (bf16[112,192]{1,0:T(8,128)(2,1)}, bf16[112,192]{1,0:T(8,128)(2,1)S(1)}, u32[]{:S(2)}, u32[]{:S(2)}) collective-permute-start(bf16[112,192]{1,0:T(8,128)(2,1)} %get-tuple-element.95), channel_id=1, source_target_pairs={{0,3},{1,2},{2,5},{3,4},{4,7},{5,6},{6,9},{7,8},{8,11},{9,10},{10,... | collective-permute-start | bytes 129032 | tf_op jit(solution)/shard_map/ppermute | solution.py:715
  96.0 6.2 %collective-permute-start.17 = (bf16[112,192]{1,0:T(8,128)(2,1)}, bf16[112,192]{1,0:T(8,128)(2,1)S(1)}, u32[]{:S(2)}, u32[]{:S(2)}) collective-permute-start(bf16[112,192]{1,0:T(8,128)(2,1)} %get-tuple-element.96), channel_id=1, source_target_pairs={{0,17},{1,16},{16,33},{17,32},{32,49},{33,48},{48,65},{49,64},{64,... | collective-permute-start | bytes 129032 | tf_op jit(solution)/shard_map/ppermute | solution.py:715
  98.2 48.7 %copy-start.4 = (bf16[112,192]{1,0:T(8,128)(2,1)}, bf16[112,192]{1,0:T(8,128)(2,1)S(1)}, u32[]{:S(2)}) copy-start(bf16[112,192]{1,0:T(8,128)(2,1)S(1)} %collective-permute-done.12.refs_1_) | copy-start | bytes 129028
  116.9 12.0 %all-to-all-start.3 = ((bf16[16,32,128]{2,1,0:T(8,128)(2,1)}), bf16[16,32,128]{2,1,0:T(8,128)(2,1)S(1)}, u32[]{:S(2)}, u32[]{:S(2)}) async-start(bf16[16,32,128]{2,1,0:T(8,128)(2,1)} %broadcast_in_dim.8), calls=%async_computation.3 | async-start | bytes 262144 | tf_op jit(solution)/shard_map/all_to_all | solution.py:722
  147.0 9.6 %collective-permute-start.19 = (bf16[8,576,128]{2,1,0:T(8,128)(2,1)S(1)}, bf16[8,576,128]{2,1,0:T(8,128)(2,1)S(1)}, u32[]{:S(2)}, u32[]{:S(2)}) collective-permute-start(bf16[8,576,128]{2,1,0:T(8,128)(2,1)S(1)} %all_to_all.26.refs_0_), channel_id=1, source_target_pairs={{0,16},{16,0},{32,48},{48,32},{64,80},{80,64},{96,112},{112,96},{1... | collective-permute-start | bytes 3538952 | tf_op jit(solution)/shard_map/ppermute | solution.py:734
  (17 other events, 304.0 us)

commit v3 on v2

--- a/solution.py
+++ b/solution.py
@@ -15,8 +15,9 @@
 NEG = -1e30
 COARSE, FINE, TAB = 432, 80, 64
 GRAIN = COARSE + FINE
-WIDE = 3328
-VMEM_LIMIT = 56 * 1024 * 1024
+WIDE = 3456
+FINE_ROWS, COARSE_ROWS = 6 * TOK + 8, 12 * TOK + 8
+VMEM_LIMIT = 24 * 1024 * 1024
 
 
 def dot(a, b, ca, cb):
@@ -221,7 +222,7 @@
             for half in range(2):
                 u_ref[half, pl.ds(base + row, heads, stride=32)] = table_slice(table, g * RUN + half * HALF_RUN)
         base += heads * 32
-    u = jnp.concatenate([u_ref[0], u_ref[1]], axis=1)
+    u = jnp.concatenate([u_ref[0, :base], u_ref[1, :base]], axis=1)
     hi = low(u)
     mid = low(u - hi.astype(F32))
     for first in range(0, 12, 2):
@@ -260,7 +261,7 @@
             part = mm_t(hi, sel) + mm_t(low(y - hi.astype(F32)), sel)
             acc = part if acc is None else acc + part
         for half in range(2):
-            acc_ref[half] = acc[:, 128 * half : 128 * half + 128]
+            acc_ref[half, : heads * 32] = acc[:, 128 * half : 128 * half + 128]
         for g, row in table_groups():
             for half in range(2):
                 out_to(t, g * RUN + half * HALF_RUN, acc_ref[half, pl.ds(row, heads, stride=32)][:, :HALF_RUN])
@@ -268,27 +269,60 @@
 
 def bias_kernel(fine_ref, next_ref, coarse_ref, fine_out, coarse_out, u_ref):
     at_end = [lax.axis_index(name) == lax.axis_size(name) - 1 for name in ("rep", "lat")]
+    own, later, coarse = fine_ref[...], next_ref[...], coarse_ref[...]
     kinds = [
-        (fine_ref[:, 0, :], False, fine_out.at[0]),
-        (fine_ref[:, 1, :], True, fine_out.at[1]),
-        (next_ref[:, 0, :], False, fine_out.at[2]),
-        (coarse_ref[:, 0, :], True, coarse_out.at[0]),
+        (own[:, 0, :], False, fine_out.at[0]),
+        (own[:, 1, :], True, fine_out.at[1]),
+        (later[:, 0, :], False, fine_out.at[2]),
+        (coarse[:, 0, :], True, coarse_out.at[0]),
     ]
     expand_tables(at_end, kinds, u_ref)
 
 
+FIELD_PAD, COT_PAD = 176, 24
+MESSAGE = FIELD_PAD + FIELD_PAD // 2 + 3 * COT_PAD
+
+
 def pack_kernel(field_ref, cot_ref, *outs):
+    r = iota((FIELD_PAD, 1), 0)
+    row = div_const(r, 18)
+    rc = iota((COT_PAD, 1), 0)
+    crow = div_const(rc, 6)
+    hots, cot_hots = [], []
+    for t in range(2):
+        for u in range(2):
+            target = (row + (0 if t else 3)) * 24 + r - row * 18 + (0 if u else 6)
+            hots.append(one_hot(jnp.where(r < 162, target, -1), 288))
+    hot = jnp.concatenate(hots, axis=0)
     for s in range(2):
         for t in range(2):
-            out = outs[2 * s + t]
-            lev = 1 - s
-            row, crow = (3, 3) if t == 0 else (0, 0)
-            for h in range(9):
-                out[h * 24 : h * 24 + 24] = field_ref[lev, row + h]
-            for h in range(3):
-                part = cot_ref[crow + h, :, lev, :].astype(F32)
-                both = jnp.concatenate([part[:, :192], part[:, 192:]], axis=0)
-                out[216 + h * 24 : 240 + h * 24] = low(both)
+            for u in range(2):
+                target = (crow + (0 if t else 3)) * 12 + rc - crow * 6 + (0 if u else 6)
+                cot_hots.append(one_hot(jnp.where(rc < 18, target * 2 + 1 - s, -1), TOK))
+    cot = mm(jnp.concatenate(cot_hots, axis=0), low(cot_ref[...].astype(F32).reshape(TOK, 384)))
+    half = FIELD_PAD // 2
+    for s in range(2):
+        rows = mm(hot, low(field_ref[1 - s].astype(F32).reshape(288, 192)))
+        for n in range(4):
+            out = outs[4 * s + n]
+            part = rows[n * FIELD_PAD : (n + 1) * FIELD_PAD]
+            out[:FIELD_PAD] = low(part[:, :128])
+            rest = [low(jnp.concatenate([part[:half, 128:], part[half:, 128:]], axis=1))]
+            first = (4 * s + n) * COT_PAD
+            rest += [low(cot[first : first + COT_PAD, 128 * c : 128 * c + 128]) for c in range(3)]
+            out[FIELD_PAD:] = jnp.concatenate([x.astype(F32) for x in rest], axis=0).astype(BF)
+
+
+def field_of(ref):
+    half = FIELD_PAD // 2
+    rest = ref[FIELD_PAD : FIELD_PAD + half].astype(F32)
+    rest = jnp.concatenate([rest[:, :64], rest[:, 64:]], axis=0)
+    return low(jnp.concatenate([ref[:FIELD_PAD].astype(F32), rest], axis=1))
+
+
+def cot_of(ref):
+    rows = ref[FIELD_PAD:].astype(F32)[FIELD_PAD // 2 :]
+    return low(jnp.concatenate([rows[COT_PAD * c : COT_PAD * c + COT_PAD] for c in range(3)], axis=1))
 
 
 def fine_weights(qkv_ref):
@@ -330,10 +364,10 @@
                     lat = 6 * wr + hh - 9 * t
                     lon = 12 * wc + ww - 18 * u
                     good = (lat >= 0) & (lat < 9) & (lon >= 0) & (lon < 18)
-                    hots.append(one_hot(jnp.where(good, lat * 24 + lon + (6 if u == 0 else 0), -1), 216))
+                    hots.append(one_hot(jnp.where(good, lat * 18 + lon, -1), FIELD_PAD))
             hot = jnp.concatenate(hots, axis=0)
             for z in range(2):
-                part = mm(hot, bufs[z][t][u][:216])
+                part = mm(hot, field_of(bufs[z][t][u]))
                 for n in range(4):
                     place = 3 * (t + n // 2) + u + n % 2, slice(z * HALF, (z + 1) * HALF)
                     value = part[n * HALF : (n + 1) * HALF]
@@ -393,12 +427,10 @@
         for u in range(2):
             lat, lon = ci - 3 * t, cj - 6 * u
             good = (lat >= 0) & (lat < 3) & (lon >= 0) & (lon < 6)
-            col = lat * 24 + lon + (6 if u == 0 else 0)
-            hot = jnp.concatenate([one_hot(jnp.where(good, col + 12 * half, -1), HALF) for half in range(2)], axis=0)
+            hot = one_hot(jnp.where(good, lat * 6 + lon, -1), COT_PAD)
             for s in range(2):
-                part = mm(hot, bufs[s][t][u][216:])
+                part = mm(hot, cot_of(bufs[s][t][u]))
                 cot_rows[s] = part if cot_rows[s] is None else cot_rows[s] + part
-    cot_rows = [jnp.concatenate([c[:HALF], c[HALF:]], axis=1) for c in cot_rows]
     cot = jnp.concatenate(cot_rows, axis=0)
     gy = low(cot)
     gmix = low(mm_t(gy, cproj_ref[...]))
@@ -493,9 +525,10 @@
     fold_tables(1, 12, gb_ref, y_ref, acc_ref, ctab)
 
 
-QUARTERS = ((0, 0), (1, 0), (0, 1), (1, 1))
-FINE_PAD = (176, 64, 64, 32)
+QUARTERS = ((0, 0), (0, 1), (1, 1), (1, 0))
+FINE_PAD = (176, 64, 32, 64)
 PIECE = tuple(n + 48 for n in FINE_PAD)
+BASE = tuple(sum(PIECE[:n]) for n in range(5))
 
 
 def fine_rows_of(s, t, u):
@@ -516,7 +549,7 @@
 
 def back_kernel(
     x_in, gfo_ref, latp_ref, lonp_ref, corner_ref, bias_ref, fgain_ref, fqkv_ref, fproj_ref, ctab_ref, gains_ref, cout_ref,
-    p000, p010, p001, p011, p100, p110, p101, p111, pack_out,
+    level0_out, level1_out, pack_out,
     src_ref, fq_ref, fk_ref, fv_ref, fm_ref, gm_ref, g_ref, gb_ref, y_ref, acc_ref, tab_ref,
 ):
     src_ref[:576] = gfo_ref[...]
@@ -579,7 +612,7 @@
     (gx,), (ggain,) = norm_back([low(grolled).astype(F32)], [gain], [hat], inv)
     fg = low(gy32 + gx)
     cout = cout_ref[...]
-    for s, outs in enumerate(((p000, p010, p001, p011), (p100, p110, p101, p111))):
+    for s, out in enumerate((level0_out, level1_out)):
         hots, coarse_hots = [], []
         for t, u in QUARTERS:
             hots.append(one_hot(fine_rows_of(s, t, u), 4 * TOK))
@@ -587,11 +620,11 @@
         fine = low(mm(jnp.concatenate(hots, axis=0), fg))
         coarse = low(mm(jnp.concatenate(coarse_hots, axis=0), cout))
         at = 0
-        for n, ((t, u), out) in enumerate(zip(QUARTERS, outs)):
-            rows = FINE_PAD[n]
-            out[:rows] = fine[at : at + rows]
-            out[rows : rows + 24] = coarse[24 * n : 24 * n + 24, :192]
-            out[rows + 24 :] = coarse[24 * n : 24 * n + 24, 192:]
+        for n, rows in enumerate(FINE_PAD):
+            to = BASE[n]
+            out[to : to + rows] = fine[at : at + rows]
+            out[to + rows : to + rows + 24] = coarse[24 * n : 24 * n + 24, :192]
+            out[to + rows + 24 : to + rows + 48] = coarse[24 * n : 24 * n + 24, 192:]
             at += rows
     first = low(jnp.concatenate([dqkv[0], dqkv[1]], axis=1))
     second = low(jnp.concatenate([dqkv[2], dproj], axis=1))
@@ -616,14 +649,13 @@
         pack_out[place_of(c), FINE:] = jnp.zeros((TAB, 128), BF)
 
 
-def place_kernel(*refs):
-    field_out, coarse_out, src_ref = refs[8:]
-    base = [sum(PIECE[:n]) for n in range(4)]
-
+def place_kernel(level0_ref, level1_ref, lat_ref, lon_ref, field_out, coarse_out, src_ref):
     def chosen(later_row, later_col, values):
-        near = jnp.where(later_row, values[1], values[0])
-        return jnp.where(later_col, jnp.where(later_row, values[3], values[2]), near)
-
+        value = dict(zip(QUARTERS, values))
+        near = jnp.where(later_row, value[1, 0], value[0, 0])
+        return jnp.where(later_col, jnp.where(later_row, value[1, 1], value[0, 1]), near)
+
+    base = BASE[:4]
     r = iota((288, 1), 0)
     lat = div_const(r, 24)
     col = r - lat * 24
@@ -639,15 +671,19 @@
     inside = inside + chosen(later_row, later_col, [b + n for b, n in zip(base, FINE_PAD)])
     hots += [one_hot(inside, sum(PIECE)), one_hot(inside + 24, sum(PIECE))]
     hot = jnp.concatenate(hots, axis=0)
+    placed = []
     for s in range(2):
-        for n in range(4):
-            src_ref[base[n] : base[n] + PIECE[n]] = refs[4 * s + n][...]
+        src_ref[: BASE[1]] = (level0_ref, level1_ref)[s][: BASE[1]]
+        src_ref[BASE[1] : BASE[3]] = lon_ref[s]
+        src_ref[BASE[3] :] = lat_ref[s, PIECE[2] :]
         out = low(mm(hot, src_ref[...]))
         for h in range(12):
             field_out[1 - s, h] = out[24 * h : 24 * h + 24]
-        coarse = jnp.concatenate([out[288:360], out[360:]], axis=1)
-        for h in range(6):
-            coarse_out[h, :, 1 - s, :] = coarse[12 * h : 12 * h + 12]
+        coarse = jnp.concatenate([out[288:360], out[360:]], axis=1).astype(F32)
+        placed.append(coarse)
+    for h in range(6):
+        rows = slice(12 * h, 12 * h + 12)
+        coarse_out[h] = low(jnp.stack([placed[1][rows], placed[0][rows]], axis=1))
 
 
 def unpack_kernel(fine_scale, coarse_scale, fine_table_scale, coarse_table_scale, mine_ref, other_ref, *outs):
@@ -676,19 +712,18 @@
     for c in range(3):
         cgain_out[pl.ds(128 * c, 128)] = gains[6 + c]
     gains = fine_get(1152, 16, fine_scale)
-    fgain_out[pl.ds(0, 128)] = gains[0]
-    fgain_out[pl.ds(128, 64)] = gains[1, :64]
+    fgain_out[...] = jnp.concatenate([gains[:1], gains[1:2, :64]], axis=1).reshape(192)
     for c in range(13):
         for half in range(2):
             start = 256 * c + 128 * half
             n = min(128, POS - start)
             block = get_chunk(sums, c, slice(GRAIN + 32 * half, GRAIN + 32 * half + 32))[:, :n]
-            for t in range(2):
-                ftab_out[:, t, start : start + n] = block[8 * t : 8 * t + 6] * fine_table_scale
+            both = jnp.stack([block[:6], block[8:14]], axis=1)
+            ftab_out[:, :, start : start + n] = both * fine_table_scale
             ctab_out[:, 0, start : start + n] = block[16:28] * coarse_table_scale
 
 
-def call(kernel, out_shapes, scratch=(), smem=0, flops=0, moved=0):
+def call(kernel, out_shapes, scratch=(), smem=0, flops=0, moved=0, vmem=VMEM_LIMIT):
     def run(*args):
         specs = [pl.BlockSpec(memory_space=pltpu.SMEM)] * smem
         specs += [pl.BlockSpec(memory_space=pltpu.VMEM)] * (len(args) - smem)
@@ -698,7 +733,7 @@
             in_specs=specs,
             out_specs=[pl.BlockSpec(memory_space=pltpu.VMEM)] * len(out_shapes),
             scratch_shapes=[pltpu.VMEM(s, d) for s, d in scratch],
-            compiler_params=pltpu.CompilerParams(vmem_limit_bytes=VMEM_LIMIT),
+            compiler_params=pltpu.CompilerParams(vmem_limit_bytes=vmem),
             cost_estimate=pl.CostEstimate(flops=flops, bytes_accessed=moved, transcendentals=0),
         )(*args)
 
@@ -747,17 +782,22 @@
     return exchange_columns(both)
 
 
-def reduce_everywhere(got, pack, beside):
+def reduce_everywhere(got, pack, level0, level1):
     rest = lax.axis_size("lat") * lax.axis_size("rep")
     got, pack = lax.optimization_barrier((got, pack))
-    pack, beside = lax.optimization_barrier((exchange(pack, "lon"), beside))
+    pack, level1 = lax.optimization_barrier((exchange(pack, "lon"), shifted(level1, (1, 0, 0), -1)))
     got, pack = summed(got), summed(pack)
     part = jnp.concatenate([got, pack[:, :FINE]], axis=1).reshape(rest, -1, 128)
-    part = summed(exchange(part, ("lat", "rep")))
-    part = exchange(spread(part, rest), ("lat", "rep")).reshape(1, GRAIN, 128)
-    mine = jnp.concatenate([part, pack[:, FINE:]], axis=1)
+    later = shifted(jnp.stack([level0[BASE[2] :], level1[BASE[2] :]]), (0, 1, 0), -1)
+    part, later = lax.optimization_barrier((exchange(part, ("lat", "rep")), later))
+    part = spread(summed(part), rest)
+    corner = later[:, : PIECE[2]]
+    column = [jnp.concatenate([x[BASE[1] : BASE[2]], c]) for x, c in zip((level0, level1), corner)]
+    column = shifted(jnp.stack(column), (0, 0, 1), -1)
+    part, column = lax.optimization_barrier((exchange(part, ("lat", "rep")), column))
+    mine = jnp.concatenate([part.reshape(1, GRAIN, 128), pack[:, FINE:]], axis=1)
     mine = exchange_columns(spread(mine, lax.axis_size("lon") // 2))
-    return (mine, sibling(mine)), beside
+    return (mine, sibling(mine)), (level0, level1, later, column)
 
 
 def body(
@@ -765,16 +805,13 @@
     coarse_gain, coarse_qkv, coarse_proj, coarse_table, cotangent,
 ):
     rep, lat, lon = (lax.axis_size(n) for n in ("rep", "lat", "lon"))
-    packs = call(pack_kernel, [((288, 192), BF)] * 4)(fine_field, cotangent.transpose(1, 2, 0, 3))
-    bufs = []
-    for s, t, u in CORNERS:
-        b = packs[2 * s + t]
-        bufs.append(shifted(b, (s, t, u), 1) if s + t + u else b)
+    packs = call(pack_kernel, [((MESSAGE, 128), BF)] * 8)(fine_field, cotangent.transpose(1, 2, 0, 3))
+    bufs = [shifted(b, place, 1) if any(place) else b for b, place in zip(packs, CORNERS)]
     table = fine_table[0].transpose(1, 0, 2)
     bias, cbias = call(
         bias_kernel,
-        [((3, 2, 6 * TOK, 128), F32), ((1, 2, 12 * TOK, 128), F32)],
-        [((2, 30 * 32, 128), F32)],
+        [((3, 2, FINE_ROWS, 128), F32), ((1, 2, COARSE_ROWS, 128), F32)],
+        [((2, 34 * 32, 128), F32)],
         flops=1 << 32,
     )(table, shifted(fine_table, (0, 1, 0), 1)[0].transpose(1, 0, 2), coarse_table[0].transpose(1, 0, 2))
     x, gfo, latp, lonp, *coarse, cgains = call(
@@ -782,7 +819,7 @@
         [
             ((4, TOK, 192), BF), ((4, TOK, 192), BF), ((192, 192), BF), ((160, 192), BF),
             ((TOK, 384), BF), ((TOK, 384), BF), ((TOK, 384), BF), ((4, TOK, 192), BF), ((TOK, 384), BF),
-            ((3, TOK, 128), BF), ((3, 3, TOK, 128), BF), ((1, 2, 12 * TOK, 128), F32), ((16, 128), BF),
+            ((3, TOK, 128), BF), ((3, 3, TOK, 128), BF), ((1, 2, COARSE_ROWS, 128), F32), ((16, 128), BF),
         ],
         [
             ((9, TOK, 192), F32), ((9 * TOK, 192), BF),
@@ -800,26 +837,24 @@
     cout, cpack, ctab = call(
         side_kernel,
         [((TOK, 384), BF), ((16, COARSE, 128), BF), ((16, WIDE), F32)],
-        [((384, 256), F32), ((2, 384, 128), F32)],
+        [((384, 256), F32), ((2, 512, 128), F32)],
         flops=1 << 32,
     )(*coarse, coarse_proj)
     got = reduce_coarse(cpack)
-    *pieces, pack = call(
+    level0, level1, pack = call(
         back_kernel,
-        [((n, 192), BF) for n in PIECE + PIECE] + [((16, FINE + TAB, 128), BF)],
+        [((BASE[4], 192), BF), ((BASE[4], 192), BF), ((16, FINE + TAB, 128), BF)],
         [
             ((1088, 192), BF), ((4, TOK, 192), BF), ((4, LANES, 192), BF), ((4, LANES, 192), BF),
             ((4, TOK, 192), BF), ((4, TOK, 192), BF), ((3, 4, TOK, 192), BF),
-            ((2, 2, 6 * TOK, 128), F32), ((192, 256), F32), ((2, 192, 128), F32), ((32, WIDE), F32),
+            ((2, 2, FINE_ROWS, 128), F32), ((192, 256), F32), ((2, 256, 128), F32), ((32, WIDE), F32),
         ],
         flops=1 << 33,
     )(x, gfo.reshape(4 * TOK, 192), lat_recv, lon_recv, corner_recv, bias, fine_gain, fine_qkv, fine_proj, ctab, cgains, cout)
-    places = [(s, t, u) for s in range(2) for t, u in QUARTERS]
-    pieces = [shifted(b, place, -1) if any(place) else b for b, place in zip(pieces, places)]
-    sums, pieces = reduce_everywhere(got, pack, pieces)
+    sums, back = reduce_everywhere(got, pack, level0, level1)
     field_grad, coarse_out = call(
         place_kernel, [((2, 12, 24, 192), BF), ((6, 12, 2, 384), BF)], [((sum(PIECE), 192), BF)]
-    )(*pieces)
+    )(*back)
     levels, rows, cols = 2 * rep, 12 * lat, 24 * lon
     fine_scale = (levels * rows * cols) ** -0.5
     coarse_scale = (levels * rows * cols // 4) ** -0.5

time: 162 us -> 154 us (0.951)
  waiting for transfers between devices: 13.8 us -> 30.4 us
  Pallas kernels: 51 us -> 34.8 us
  blocking collectives: 31.6 us -> 20.9 us
  local copies, waits for them, and re-layouts: 4.03 us -> 7.32 us
  starting transfers between devices: 58.6 us -> 55.5 us
  other arithmetic: 1.4 us -> 3.33 us
    ppermute x18 -> x14, waiting for transfers between devices: 4.1 us -> 24.2 us  [shifted(): return lax.ppermute(x, tuple(names), pairs)]
    pallas_call x7, Pallas kernels: 51 us -> 34.8 us  [run(): pl.pallas_call(kernel, out_shape=[jax.ShapeDtypeStruct(s, d) for s, d in...]
    all_to_all x1 -> x0, blocking collectives: 13.9 us -> none  [exchange(): return lax.all_to_all(lax.optimization_barrier(x), axes, 0, 0, tiled=True)]
    ppermute x18 -> x14, starting transfers between devices: 34 us -> 26.8 us  [shifted(): return lax.ppermute(x, tuple(names), pairs)]
    all_to_all x2 -> x3, starting transfers between devices: 11.7 us -> 18.8 us  [exchange(): return lax.all_to_all(lax.optimization_barrier(x), axes, 0, 0, tiled=True)]
    all_to_all x2 -> x3, waiting for transfers between devices: 8.5 us -> 3.2 us  [exchange(): return lax.all_to_all(lax.optimization_barrier(x), axes, 0, 0, tiled=True)]
    unnamed x36 -> x28, local copies, waits for them, and re-layouts: 1.84 us -> 5.48 us
    all_to_all x1, blocking collectives: 17.8 us -> 20.9 us  [exchange_columns(): lax.all_to_all(lax.optimization_barrier(x), 'lon', 0, 0, axis_index_group...]
  transfers between devices with their start and end apart: 23 -> 20, of which waited for: 6 -> 6; matrix products, arithmetic and copies ran while one was open for 1% -> 2% of each run, Pallas kernels for 15% -> 11%
where the time goes in v3:
time: 154 us; the launch traced here: 153 us
  starting transfers between devices  55.5 us (36%)
  Pallas kernels  34.8 us (23%)
  waiting for transfers between devices  30.4 us (20%)
  blocking collectives  20.9 us (14%)
  local copies, waits for them, and re-layouts  7.32 us (5%)
  other arithmetic  3.33 us (2%)
    pallas_call x7, Pallas kernels, run(): pl.pallas_call(kernel, out_shape=[jax.ShapeDtypeStruct(s, d) for s, d in...  34.8 us
    ppermute x14, starting transfers between devices, shifted(): return lax.ppermute(x, tuple(names), pairs)  26.8 us
    ppermute x14, waiting for transfers between devices, shifted(): return lax.ppermute(x, tuple(names), pairs)  24.2 us
    all_to_all x1, blocking collectives, exchange_columns(): lax.all_to_all(lax.optimization_barrier(x), 'lon', 0, 0, axis_index_group...  20.9 us
    all_to_all x3, starting transfers between devices, exchange(): return lax.all_to_all(lax.optimization_barrier(x), axes, 0, 0, tiled=True)  18.8 us
    unnamed x28, local copies, waits for them, and re-layouts  5.48 us
    all_to_all x1, starting transfers between devices, exchange_columns(): lax.all_to_all(lax.optimization_barrier(x), 'lon', 0, 0, axis_index_group...  5.36 us
    ppermute x2, starting transfers between devices, sibling(): lax.ppermute(x, 'lon', [(i, i ^ 1) for i in range(lax.axis_size('lon'))])  4.5 us
  transfers between devices with their start and end apart: 20, of which 6 were waited for; matrix products, arithmetic and copies ran while one was open for 2% of the time, Pallas kernels for 11%

profile of v3, /device:TPU:1, one launch (start us, length us, event | category | flops | bytes accessed | tf_op | source)
XLA Modules:
  0.0 153.1 jit_solution(11194710702530472626)
XLA Ops:
  0.6 6.5 %collective-permute-start.7 = (f32[1,2,6,3312]{3,1,2,0:T(2,128)}, f32[1,2,6,3312]{3,1,2,0:T(2,128)S(1)}, u32[]{:S(2)}, u32[]{:S(2)}) collective-permute-start(f32[1,2,6,3312]{3,1,2,0:T(2,128)} %param.16), channel_id=1, source_target_pairs={{0,14},{2,0},{4,2},{6,4},{8,6},{10,8},{12,10},{14,12},{1,15},{3,1}... | collective-permute-start | bytes 476936 | tf_op jit(solution)/shard_map/ppermute | solution.py:750
  11.4 5.5 %collective-permute-start.2 = (bf16[336,128]{1,0:T(8,128)(2,1)S(1)}, bf16[336,128]{1,0:T(8,128)(2,1)S(1)}, u32[]{:S(2)}, u32[]{:S(2)}) collective-permute-start(bf16[336,128]{1,0:T(8,128)(2,1)S(1)} %get-tuple-element.64), channel_id=1, source_target_pairs={{0,254},{2,240},{4,242},{6,244},{8,246},{10,248},{12,250},{14,252}... | collective-permute-start | bytes 258056 | tf_op jit(solution)/shard_map/ppermute | solution.py:750
  17.3 1.8 %collective-permute-start.4 = (bf16[336,128]{1,0:T(8,128)(2,1)S(1)}, bf16[336,128]{1,0:T(8,128)(2,1)S(1)}, u32[]{:S(2)}, u32[]{:S(2)}) collective-permute-start(bf16[336,128]{1,0:T(8,128)(2,1)S(1)} %get-tuple-element.66), channel_id=1, source_target_pairs={{0,241},{1,240},{16,1},{17,0},{32,17},{33,16},{48,33},{49,32},{64,... | collective-permute-start | bytes 258056 | tf_op jit(solution)/shard_map/ppermute | solution.py:750
  19.9 5.2 %collective-permute-start.6 = (bf16[336,128]{1,0:T(8,128)(2,1)S(1)}, bf16[336,128]{1,0:T(8,128)(2,1)S(1)}, u32[]{:S(2)}, u32[]{:S(2)}) collective-permute-start(bf16[336,128]{1,0:T(8,128)(2,1)S(1)} %get-tuple-element.68), channel_id=1, source_target_pairs={{0,255},{1,254},{2,241},{3,240},{4,243},{5,242},{6,245},{7,244},{8... | collective-permute-start | bytes 258056 | tf_op jit(solution)/shard_map/ppermute | solution.py:750
  27.0 3.3 %shard_map.212 = (f32[3,2,872,128]{3,2,1,0:T(8,128)S(1)}, f32[1,2,1736,128]{3,2,1,0:T(8,128)S(1)}) custom-call(f32[6,2,3312]{2,1,0:T(2,128)S(1)} %bitcast.35, f32[6,2,3312]{2,1,0:T(2,128)S(1)} %bitcast.37, f32[12,1,3312]{2,1,0:T(1,128)S(1)} %bitcast.36), custom_call_target="tpu_custom_call" | custom-call | flops 4294967296 | tf_op jit(solution)/shard_map/pallas_call | solution.py:730
  30.4 13.9 %shard_map.213 = (bf16[4,144,192]{2,1,0:T(8,128)(2,1)S(1)}, bf16[4,144,192]{2,1,0:T(8,128)(2,1)S(1)}, bf16[192,192]{1,0:T(8,128)(2,1)S(1)}, bf16[160,192]{1,0:T(...) custom-call(bf16[336,128]{1,0:T(8,128)(2,1)S(1)} %get-tuple-element., ...), custom_call_target="tpu_custom_call" | custom-call | flops 17179869184 | tf_op jit(solution)/shard_map/pallas_call | solution.py:730
  44.3 2.0 %shard_map.214 = (bf16[144,384]{1,0:T(8,128)(2,1)S(1)}, bf16[16,432,128]{2,1,0:T(8,128)(2,1)S(1)}, f32[16,3456]{1,0:T(8,128)S(1)}) custom-call(bf16[144,384]{1,0:T(8,128)(2,1)S(1)} %get-tuple-element.75.cin_ref, bf16[144,384]{1,0:T(8,128)(2,1)S(1)} %get-tuple-element.76.gy_ref, bf16[144,384]{1,0:T(8,128)(2,1)S(1)} %get-tuple-element.77.xc_ref, ...), custom_call_target="tpu_custom_call" | custom-call | flops 4294967296 | tf_op jit(solution)/shard_map/pallas_call | solution.py:730
  48.1 1.9 %collective-permute-done.11 = bf16[8,432,128]{2,1,0:T(8,128)(2,1)} collective-permute-done((bf16[8,432,128]{2,1,0:T(8,128)(2,1)}, bf16[8,432,128]{2,1,0:T(8,128)(2,1)}, u32[]{:S(2)}, u32[]{:S(2)}) %collective-permute-start.11) | collective-permute-done | bytes 884768 | tf_op jit(solution)/shard_map/ppermute | solution.py:769
  50.0 2.3 %add_convert_fusion = bf16[8,432,128]{2,1,0:T(8,128)(2,1)} fusion(bf16[8,432,128]{2,1,0:T(8,128)(2,1)} %collective-permute-done.11, bf16[16,432,128]{2,1,0:T(8,128)(2,1)S(1)} %get-tuple-element.87, s32[]{:T(128)S(6)} %select_n.14), kind=kLoop, calls=%fused_computation | loop fusion | flops 1769472 | bytes 2654212 | tf_op jit(solution)/shard_map/convert_element_type | solution.py:781
  52.4 5.4 %all-to-all-start = ((bf16[8,432,128]{2,1,0:T(8,128)(2,1)}), bf16[8,432,128]{2,1,0:T(8,128)(2,1)S(1)}, u32[]{:S(2)}, u32[]{:S(2)}) async-start(bf16[8,432,128]{2,1,0:T(8,128)(2,1)} %add_convert_fusion), calls=%async_computation | async-start | bytes 1769472 | tf_op jit(solution)/shard_map/all_to_all | solution.py:775
  57.7 1.7 %copy-done.13 = f32[3,2,872,128]{3,2,1,0:T(8,128)S(1)} copy-done((f32[3,2,872,128]{3,2,1,0:T(8,128)S(1)}, f32[3,2,872,128]{3,2,1,0:T(8,128)}, u32[]{:S(2)}) %copy-start.13) | copy-done | bytes 2678808
  59.5 11.1 %shard_map.215 = (bf16[528,192]{1,0:T(8,128)(2,1)S(1)}, bf16[528,192]{1,0:T(8,128)(2,1)S(1)}, bf16[16,144,128]{2,1,0:T(8,128)(2,1)}) custom-call(bf16[4,144,192]{2,1,0:T(8,128)(2,1)S(1)} %get-tuple-element.71.x_in, bf16[576,192]{1,0:T(8,128)(2,1)S(1)} %bitcast.38, bf16[192,192]{1,0:T(8,128)(2,1)S(1)} %collective-permute-done.8.latp_ref, ...), custom_call_target="tpu_custom_call" | custom-call | flops 8589934592 | tf_op jit(solution)/shard_map/pallas_call | solution.py:730
  70.6 8.1 %all-to-all-start.1 = ((bf16[16,144,128]{2,1,0:T(8,128)(2,1)}), bf16[16,144,128]{2,1,0:T(8,128)(2,1)S(1)}, u32[]{:S(2)}, u32[]{:S(2)}) async-start(bf16[16,144,128]{2,1,0:T(8,128)(2,1)} %get-tuple-element.89), calls=%async_computation.1 | async-start | bytes 1179648 | tf_op jit(solution)/shard_map/all_to_all | solution.py:757
  78.9 13.1 %collective-permute-done.12.level1_ref = bf16[528,192]{1,0:T(8,128)(2,1)S(1)} collective-permute-done((bf16[528,192]{1,0:T(8,128)(2,1)S(1)}, bf16[528,192]{1,0:T(8,128)(2,1)S(1)}, u32[]{:S(2)}, u32[]{:S(2)}) %collective-permute-start.12) | collective-permute-done | bytes 202784 | tf_op jit(solution)/shard_map/ppermute | solution.py:750
  92.8 5.0 %all-to-all-start.2 = ((bf16[16,32,128]{2,1,0:T(8,128)(2,1)}), bf16[16,32,128]{2,1,0:T(8,128)(2,1)S(1)}, u32[]{:S(2)}, u32[]{:S(2)}) async-start(bf16[16,32,128]{2,1,0:T(8,128)(2,1)} %bitcast.9), calls=%async_computation.2 | async-start | bytes 262144 | tf_op jit(solution)/shard_map/all_to_all | solution.py:757
  99.4 8.4 %collective-permute-done.13.lat_ref = bf16[2,192,192]{2,1,0:T(8,128)(2,1)S(1)} collective-permute-done((bf16[2,192,192]{2,1,0:T(8,128)(2,1)S(1)}, bf16[2,192,192]{2,1,0:T(8,128)(2,1)S(1)}, u32[]{:S(2)}, u32[]{:S(2)}) %collective-permute-start.13) | collective-permute-done | bytes 147488 | tf_op jit(solution)/shard_map/ppermute | solution.py:750
  108.5 5.7 %all-to-all-start.3 = ((bf16[16,32,128]{2,1,0:T(8,128)(2,1)}), bf16[16,32,128]{2,1,0:T(8,128)(2,1)S(1)}, u32[]{:S(2)}, u32[]{:S(2)}) async-start(bf16[16,32,128]{2,1,0:T(8,128)(2,1)} %broadcast_in_dim.8), calls=%async_computation.3 | async-start | bytes 262144 | tf_op jit(solution)/shard_map/all_to_all | solution.py:757
  114.3 2.6 %collective-permute-start.14 = (bf16[2,192,192]{2,1,0:T(8,128)(2,1)S(1)}, bf16[2,192,192]{2,1,0:T(8,128)(2,1)S(1)}, u32[]{:S(2)}, u32[]{:S(2)}) collective-permute-start(bf16[2,192,192]{2,1,0:T(8,128)(2,1)S(1)} %pad_maximum_fusion.1), channel_id=1, source_target_pairs={{0,16},{16,32},{32,48},{48,64},{64,80},{80,96},{96,112},{112,128},... | collective-permute-start | bytes 442376 | tf_op jit(solution)/shard_map/ppermute | solution.py:750
  116.9 2.6 %collective-permute-done.14.lon_ref = bf16[2,192,192]{2,1,0:T(8,128)(2,1)S(1)} collective-permute-done((bf16[2,192,192]{2,1,0:T(8,128)(2,1)S(1)}, bf16[2,192,192]{2,1,0:T(8,128)(2,1)S(1)}, u32[]{:S(2)}, u32[]{:S(2)}) %collective-permute-start.14) | collective-permute-done | bytes 147488 | tf_op jit(solution)/shard_map/ppermute | solution.py:750
  119.5 3.2 %all-to-all-done.3 = bf16[16,32,128]{2,1,0:T(8,128)(2,1)S(1)} async-done(((bf16[16,32,128]{2,1,0:T(8,128)(2,1)}), bf16[16,32,128]{2,1,0:T(8,128)(2,1)S(1)}, u32[]{:S(2)}, u32[]{:S(2)}) %all-to-all-start.3) | async-done | bytes 131104 | tf_op jit(solution)/shard_map/all_to_all | solution.py:757
  122.9 20.9 %all_to_all.25.refs_0_ = bf16[8,576,128]{2,1,0:T(8,128)(2,1)S(1)} all-to-all(bf16[8,576,128]{2,1,0:T(8,128)(2,1)S(1)} %broadcast_in_dim.20), channel_id=1, replica_groups={{0,32,64,96,128,160,192,224},{16,48,80,112,144,176,208,240},{1,33,65,97..., dimensions={0} | all-to-all | bytes 2359296 | tf_op jit(solution)/shard_map/all_to_all | solution.py:775
  143.8 4.5 %collective-permute-start.15 = (bf16[8,576,128]{2,1,0:T(8,128)(2,1)S(1)}, bf16[8,576,128]{2,1,0:T(8,128)(2,1)S(1)}, u32[]{:S(2)}, u32[]{:S(2)}) collective-permute-start(bf16[8,576,128]{2,1,0:T(8,128)(2,1)S(1)} %all_to_all.25.refs_0_), channel_id=1, source_target_pairs={{0,16},{16,0},{32,48},{48,32},{64,80},{80,64},{96,112},{112,96},{1... | collective-permute-start | bytes 3538952 | tf_op jit(solution)/shard_map/ppermute | solution.py:769
  148.3 1.5 shard_map.216
  150.7 2.4 %shard_map.217 = (f32[192]{0:T(256)}, f32[192,576]{1,0:T(8,128)}, f32[192,192]{1,0:T(8,128)}, f32[6,2,3312]{2,1,0:T(2,128)}, f32[768]{0:T(1024)}, /*index=5*/f32...) custom-call(bf16[8,576,128]{2,1,0:T(8,128)(2,1)S(1)} %all_to_all.25.refs_0_, ...), custom_call_target="tpu_custom_call" | custom-call | tf_op jit(solution)/shard_map/pallas_call | solution.py:730
  (71 shorter events, 13.4 us)
Async XLA Ops:
  0.6 19.2 %collective-permute-start.7 = (f32[1,2,6,3312]{3,1,2,0:T(2,128)}, f32[1,2,6,3312]{3,1,2,0:T(2,128)S(1)}, u32[]{:S(2)}, u32[]{:S(2)}) collective-permute-start(f32[1,2,6,3312]{3,1,2,0:T(2,128)} %param.16), channel_id=1, source_target_pairs={{0,14},{2,0},{4,2},{6,4},{8,6},{10,8},{12,10},{14,12},{1,15},{3,1}... | collective-permute-start | bytes 476936 | tf_op jit(solution)/shard_map/ppermute | solution.py:750
  9.7 7.6 %collective-permute-start = (bf16[336,128]{1,0:T(8,128)(2,1)S(1)}, bf16[336,128]{1,0:T(8,128)(2,1)S(1)}, u32[]{:S(2)}, u32[]{:S(2)}) collective-permute-start(bf16[336,128]{1,0:T(8,128)(2,1)S(1)} %get-tuple-element.62), channel_id=1, source_target_pairs={{0,240},{16,0},{32,16},{48,32},{64,48},{80,64},{96,80},{112,96},{1... | collective-permute-start | bytes 258056 | tf_op jit(solution)/shard_map/ppermute | solution.py:750
  10.7 8.4 %collective-permute-start.1 = (bf16[336,128]{1,0:T(8,128)(2,1)S(1)}, bf16[336,128]{1,0:T(8,128)(2,1)S(1)}, u32[]{:S(2)}, u32[]{:S(2)}) collective-permute-start(bf16[336,128]{1,0:T(8,128)(2,1)S(1)} %get-tuple-element.63), channel_id=1, source_target_pairs={{0,14},{2,0},{4,2},{6,4},{8,6},{10,8},{12,10},{14,12},{1,15},{3,1}... | collective-permute-start | bytes 258056 | tf_op jit(solution)/shard_map/ppermute | solution.py:750
  11.4 18.9 %collective-permute-start.2 = (bf16[336,128]{1,0:T(8,128)(2,1)S(1)}, bf16[336,128]{1,0:T(8,128)(2,1)S(1)}, u32[]{:S(2)}, u32[]{:S(2)}) collective-permute-start(bf16[336,128]{1,0:T(8,128)(2,1)S(1)} %get-tuple-element.64), channel_id=1, source_target_pairs={{0,254},{2,240},{4,242},{6,244},{8,246},{10,248},{12,250},{14,252}... | collective-permute-start | bytes 258056 | tf_op jit(solution)/shard_map/ppermute | solution.py:750
  17.0 13.3 %collective-permute-start.3 = (bf16[336,128]{1,0:T(8,128)(2,1)S(1)}, bf16[336,128]{1,0:T(8,128)(2,1)S(1)}, u32[]{:S(2)}, u32[]{:S(2)}) collective-permute-start(bf16[336,128]{1,0:T(8,128)(2,1)S(1)} %get-tuple-element.65), channel_id=1, source_target_pairs={{0,1},{1,0},{2,3},{3,2},{4,5},{5,4},{6,7},{7,6},{8,9},{9,8},{10,11... | collective-permute-start | bytes 258056 | tf_op jit(solution)/shard_map/ppermute | solution.py:750
  17.3 13.0 %collective-permute-start.4 = (bf16[336,128]{1,0:T(8,128)(2,1)S(1)}, bf16[336,128]{1,0:T(8,128)(2,1)S(1)}, u32[]{:S(2)}, u32[]{:S(2)}) collective-permute-start(bf16[336,128]{1,0:T(8,128)(2,1)S(1)} %get-tuple-element.66), channel_id=1, source_target_pairs={{0,241},{1,240},{16,1},{17,0},{32,17},{33,16},{48,33},{49,32},{64,... | collective-permute-start | bytes 258056 | tf_op jit(solution)/shard_map/ppermute | solution.py:750
  19.1 11.2 %collective-permute-start.5 = (bf16[336,128]{1,0:T(8,128)(2,1)S(1)}, bf16[336,128]{1,0:T(8,128)(2,1)S(1)}, u32[]{:S(2)}, u32[]{:S(2)}) collective-permute-start(bf16[336,128]{1,0:T(8,128)(2,1)S(1)} %get-tuple-element.67), channel_id=1, source_target_pairs={{0,15},{1,14},{2,1},{3,0},{4,3},{5,2},{6,5},{7,4},{8,7},{9,6},{10,... | collective-permute-start | bytes 258056 | tf_op jit(solution)/shard_map/ppermute | solution.py:750
  19.9 10.5 %collective-permute-start.6 = (bf16[336,128]{1,0:T(8,128)(2,1)S(1)}, bf16[336,128]{1,0:T(8,128)(2,1)S(1)}, u32[]{:S(2)}, u32[]{:S(2)}) collective-permute-start(bf16[336,128]{1,0:T(8,128)(2,1)S(1)} %get-tuple-element.68), channel_id=1, source_target_pairs={{0,255},{1,254},{2,241},{3,240},{4,243},{5,242},{6,245},{7,244},{8... | collective-permute-start | bytes 258056 | tf_op jit(solution)/shard_map/ppermute | solution.py:750
  27.0 3.4 %copy-start.8 = (bf16[192,192]{1,0:T(8,128)(2,1)S(1)}, bf16[192,192]{1,0:T(8,128)(2,1)}, u32[]{:S(2)}) copy-start(bf16[192,192]{1,0:T(8,128)(2,1)} %fproj_ref.3) | copy-start | bytes 221188
  27.0 3.4 %copy-start.9 = (f32[768]{0:T(1024)S(1)}, f32[768]{0:T(1024)}, u32[]{:S(2)}) copy-start(f32[768]{0:T(1024)} %mgain_ref.1) | copy-start | bytes 9220
  27.0 3.4 %copy-start.10 = (f32[384]{0:T(512)S(1)}, f32[384]{0:T(512)}, u32[]{:S(2)}) copy-start(f32[384]{0:T(512)} %cgain_ref.1) | copy-start | bytes 4612
  30.3 14.0 %copy-start.12 = (f32[3,2,872,128]{3,2,1,0:T(8,128)}, f32[3,2,872,128]{3,2,1,0:T(8,128)S(1)}, u32[]{:S(2)}) copy-start(f32[3,2,872,128]{3,2,1,0:T(8,128)S(1)} %get-tuple-element.69.bias_ref) | copy-start | bytes 8036356
  47.3 2.8 %collective-permute-start.11 = (bf16[8,432,128]{2,1,0:T(8,128)(2,1)}, bf16[8,432,128]{2,1,0:T(8,128)(2,1)}, u32[]{:S(2)}, u32[]{:S(2)}) collective-permute-start(bf16[8,432,128]{2,1,0:T(8,128)(2,1)} %constant_dynamic-slice_fusion), channel_id=1, source_target_pairs={{0,16},{16,0},{32,48},{48,32},{64,80},{80,64},{96,112},{112,96},{1... | collective-permute-start | bytes 2654216 | tf_op jit(solution)/shard_map/ppermute | solution.py:769
  47.3 10.4 %collective-permute-start.10 = (bf16[160,192]{1,0:T(8,128)(2,1)S(1)}, bf16[160,192]{1,0:T(8,128)(2,1)S(1)}, u32[]{:S(2)}, u32[]{:S(2)}) collective-permute-start(bf16[160,192]{1,0:T(8,128)(2,1)S(1)} %get-tuple-element.74), channel_id=1, source_target_pairs={{0,18},{2,20},{4,22},{6,24},{8,26},{10,28},{12,30},{14,16},{16,34}... | collective-permute-start | bytes 184328 | tf_op jit(solution)/shard_map/ppermute | solution.py:750
  47.3 10.4 %collective-permute-start.9 = (bf16[160,192]{1,0:T(8,128)(2,1)S(1)}, bf16[160,192]{1,0:T(8,128)(2,1)S(1)}, u32[]{:S(2)}, u32[]{:S(2)}) collective-permute-start(bf16[160,192]{1,0:T(8,128)(2,1)S(1)} %get-tuple-element.74), channel_id=1, source_target_pairs={{0,16},{16,32},{32,48},{48,64},{64,80},{80,96},{96,112},{112,128},... | collective-permute-start | bytes 184328 | tf_op jit(solution)/shard_map/ppermute | solution.py:750
  47.3 10.4 %collective-permute-start.8 = (bf16[192,192]{1,0:T(8,128)(2,1)S(1)}, bf16[192,192]{1,0:T(8,128)(2,1)S(1)}, u32[]{:S(2)}, u32[]{:S(2)}) collective-permute-start(bf16[192,192]{1,0:T(8,128)(2,1)S(1)} %get-tuple-element.73), channel_id=1, source_target_pairs={{0,2},{2,4},{4,6},{6,8},{8,10},{10,12},{12,14},{14,0},{1,3},{3,5},... | collective-permute-start | bytes 221192 | tf_op jit(solution)/shard_map/ppermute | solution.py:750
  52.4 18.3 %all-to-all-start = ((bf16[8,432,128]{2,1,0:T(8,128)(2,1)}), bf16[8,432,128]{2,1,0:T(8,128)(2,1)S(1)}, u32[]{:S(2)}, u32[]{:S(2)}) async-start(bf16[8,432,128]{2,1,0:T(8,128)(2,1)} %add_convert_fusion), calls=%async_computation | async-start | bytes 1769472 | tf_op jit(solution)/shard_map/all_to_all | solution.py:775
  70.6 21.4 %all-to-all-start.1 = ((bf16[16,144,128]{2,1,0:T(8,128)(2,1)}), bf16[16,144,128]{2,1,0:T(8,128)(2,1)S(1)}, u32[]{:S(2)}, u32[]{:S(2)}) async-start(bf16[16,144,128]{2,1,0:T(8,128)(2,1)} %get-tuple-element.89), calls=%async_computation.1 | async-start | bytes 1179648 | tf_op jit(solution)/shard_map/all_to_all | solution.py:757
  78.7 13.3 %collective-permute-start.12 = (bf16[528,192]{1,0:T(8,128)(2,1)S(1)}, bf16[528,192]{1,0:T(8,128)(2,1)S(1)}, u32[]{:S(2)}, u32[]{:S(2)}) collective-permute-start(bf16[528,192]{1,0:T(8,128)(2,1)S(1)} %get-tuple-element.90), channel_id=1, source_target_pairs={{0,1},{1,0},{2,3},{3,2},{4,5},{5,4},{6,7},{7,6},{8,9},{9,8},{10,11... | collective-permute-start | bytes 608264 | tf_op jit(solution)/shard_map/ppermute | solution.py:750
  92.8 15.0 %all-to-all-start.2 = ((bf16[16,32,128]{2,1,0:T(8,128)(2,1)}), bf16[16,32,128]{2,1,0:T(8,128)(2,1)S(1)}, u32[]{:S(2)}, u32[]{:S(2)}) async-start(bf16[16,32,128]{2,1,0:T(8,128)(2,1)} %bitcast.9), calls=%async_computation.2 | async-start | bytes 262144 | tf_op jit(solution)/shard_map/all_to_all | solution.py:757
  97.9 9.9 %collective-permute-start.13 = (bf16[2,192,192]{2,1,0:T(8,128)(2,1)S(1)}, bf16[2,192,192]{2,1,0:T(8,128)(2,1)S(1)}, u32[]{:S(2)}, u32[]{:S(2)}) collective-permute-start(bf16[2,192,192]{2,1,0:T(8,128)(2,1)S(1)} %pad_maximum_fusion), channel_id=1, source_target_pairs={{0,2},{2,4},{4,6},{6,8},{8,10},{10,12},{12,14},{14,0},{1,3},{3,5},... | collective-permute-start | bytes 442376 | tf_op jit(solution)/shard_map/ppermute | solution.py:750
  108.5 14.2 %all-to-all-start.3 = ((bf16[16,32,128]{2,1,0:T(8,128)(2,1)}), bf16[16,32,128]{2,1,0:T(8,128)(2,1)S(1)}, u32[]{:S(2)}, u32[]{:S(2)}) async-start(bf16[16,32,128]{2,1,0:T(8,128)(2,1)} %broadcast_in_dim.8), calls=%async_computation.3 | async-start | bytes 262144 | tf_op jit(solution)/shard_map/all_to_all | solution.py:757
  114.3 5.2 %collective-permute-start.14 = (bf16[2,192,192]{2,1,0:T(8,128)(2,1)S(1)}, bf16[2,192,192]{2,1,0:T(8,128)(2,1)S(1)}, u32[]{:S(2)}, u32[]{:S(2)}) collective-permute-start(bf16[2,192,192]{2,1,0:T(8,128)(2,1)S(1)} %pad_maximum_fusion.1), channel_id=1, source_target_pairs={{0,16},{16,32},{32,48},{48,64},{64,80},{80,96},{96,112},{112,128},... | collective-permute-start | bytes 442376 | tf_op jit(solution)/shard_map/ppermute | solution.py:750
  143.8 7.0 %collective-permute-start.15 = (bf16[8,576,128]{2,1,0:T(8,128)(2,1)S(1)}, bf16[8,576,128]{2,1,0:T(8,128)(2,1)S(1)}, u32[]{:S(2)}, u32[]{:S(2)}) collective-permute-start(bf16[8,576,128]{2,1,0:T(8,128)(2,1)S(1)} %all_to_all.25.refs_0_), channel_id=1, source_target_pairs={{0,16},{16,0},{32,48},{48,32},{64,80},{80,64},{96,112},{112,96},{1... | collective-permute-start | bytes 3538952 | tf_op jit(solution)/shard_map/ppermute | solution.py:769
  (10 other events, 22.5 us)
